TPU v7x, 32 devices: a whole 2x2x4 slice. The times are simulated.
32 devices in a mesh: grp: 2 (over y), seq: 4 (over z), head: 4 (over x, core).
Axes of the slice: x: 2, y: 2, z: 4, core: 2. Of those that a mesh axis runs over, the one named last changes fastest.
Arguments:
- queries: bfloat16 [4096, 4096], P(('grp', 'seq'), 'head'), parts along dimension 0, may hold values from -6 to 6
- key_rows: bfloat16 [4096, 4096], P(('grp', 'seq'), 'head'), parts along dimension 0, may hold values from -6 to 6
- value_rows: bfloat16 [4096, 4096], P(('grp', 'seq'), 'head'), parts along dimension 0, may hold values from -6 to 6
- grad_out: bfloat16 [4096, 4096], P(('grp', 'seq'), 'head'), parts along dimension 0, may hold values from -6 to 6
- packing: int32 [6, 4], P('grp'), parts along dimension 0, may hold values from 0 to 16, as said below
Outputs:
- attended: bfloat16 [4096, 4096], P(('grp', 'seq'), 'head'), parts along dimension 0
- grad_queries: bfloat16 [4096, 4096], P(('grp', 'seq'), 'head'), parts along dimension 0
- grad_keys: bfloat16 [4096, 4096], P(('grp', 'seq'), 'head'), parts along dimension 0
- grad_values: bfloat16 [4096, 4096], P(('grp', 'seq'), 'head'), parts along dimension 0
There are 2 independent parts, one for each index of `grp`. A program takes and returns all parts, laid end to end along the dimension named above; each array names one. Nothing has to cross between parts.
Inputs may be any that keep to these rules, and one draw needn't show every extreme that they name: `packing`: row r is the r-th segment along the sequence, in blocks of 128 tokens: row 0 starts at 0, each row starts where the previous one ends, the last ends at 16, every segment has one block or more. Rows 3p, 3p+1, 3p+2 form one pair: all carry the same pair id, the ids of the 1 pairs are 0 to 0 in some order; row 3p has role 0 (prompt), rows 3p+1 and 3p+2 have roles 1 (chosen) and 2 (rejected) in either order.
All inputs are finite; a program needn't handle non-finite values.
Results may differ from a plain program's by a relative error of at most 0.0053.
Values sent between devices are 32-bit elements; how exact they have to be, the bound alone decides.
No kernel may reach another device: no remote copies, remote signals or barrier semaphores. Data moves between devices by JAX's collectives and lax.ppermute only.
A program may use at most 128 MiB of HBM per device.

v0:
```python
import jax
import jax.numpy as jnp
from jax import lax
from jax.sharding import PartitionSpec as P

DH = 128
BLK = 128
GROUP = 512


highest = lax.Precision.HIGHEST


def carried_in(value, axis, combine, identity, reverse):
    length, index = (lax.axis_size(axis), lax.axis_index(axis))
    everything = jax.tree.map(lambda part: lax.all_gather(part, axis), value)
    start = jax.tree.map(
        lambda part, zero: jnp.broadcast_to(jnp.asarray(zero, part.dtype), part.shape),
        value,
        identity,
    )

    def turn(k, before):
        at = length - 1 - k if reverse else k
        reached = at > index if reverse else at < index
        new = combine(before, jax.tree.map(lambda part: part[at], everything))
        return jax.tree.map(lambda a, b: jnp.where(reached, a, b), new, before)

    return lax.fori_loop(0, length, turn, start)


def block_info(packing, first_block, block_count):
    seg_starts = packing[:, 0]
    seg_ends = packing[:, 1]
    pair_col = packing[:, 2]
    role_col = packing[:, 3]
    blocks = first_block + jnp.arange(block_count, dtype=jnp.int32)
    segment = jnp.sum((seg_starts[None, :] <= blocks[:, None]).astype(jnp.int32), axis=1) - 1
    seg_ranks = jnp.arange(seg_starts.shape[0], dtype=jnp.int32)
    select = segment[:, None] == seg_ranks[None, :]
    block_role = jnp.sum(jnp.where(select, role_col[None, :], 0), axis=1)
    block_pair = jnp.sum(jnp.where(select, pair_col[None, :], 0), axis=1)
    opening = jnp.sum(jnp.where(select, seg_starts[None, :], 0), axis=1)
    prompt_sel = (segment // 3 * 3)[:, None] == seg_ranks[None, :]
    prompt_len = jnp.sum(jnp.where(prompt_sel, (seg_ends - seg_starts)[None, :], 0), axis=1)
    position = (blocks - opening)[:, None] * BLK + jnp.arange(BLK, dtype=jnp.int32)[None, :]
    visible = position + 1 + jnp.where(block_role != 0, prompt_len * BLK, 0)[:, None]
    tok_scale = lax.rsqrt((visible * DH).astype(jnp.float32))
    return (segment, block_role, block_pair, tok_scale)


def link_combine(before, behind):
    back_a, open_a, state_a = before
    back_b, open_b, state_b = behind
    empty_b = open_b < 0.0
    joins = (back_b == open_b) & (open_a == back_b) | empty_b
    state = state_b + jnp.where(joins, state_a, jnp.zeros_like(state_a))
    back_id = jnp.where(open_a < 0.0, back_b, back_a)
    open_id = jnp.where(empty_b, open_a, open_b)
    return (back_id, open_id, state)


def pick_state(carry_open, carry_state, block_ids, allowed):
    chosen = (carry_open == block_ids.astype(jnp.float32)) & allowed
    return jnp.where(chosen[:, None, None, None], carry_state[None], 0.0)


def masked_sum(flags, states):
    return jnp.einsum("j,jhde->hde", flags.astype(jnp.float32), states, precision=highest)


def split_state(state):
    upper = state.astype(jnp.bfloat16)
    upper_wide = lax.optimization_barrier(upper).astype(jnp.float32)
    lower = (state - upper_wide).astype(jnp.bfloat16)
    return (upper, lower)


def state_product(form, token_rows, parts):
    first = jnp.einsum(form, token_rows, parts[0], preferred_element_type=jnp.float32)
    return first + jnp.einsum(form, token_rows, parts[1], preferred_element_type=jnp.float32)


def body(queries, key_rows, value_rows, grad_out, packing):
    block_count = queries.shape[0] // BLK
    local_heads = queries.shape[1] // DH
    group_count = queries.shape[0] // GROUP
    final_index = block_count - 1
    first_block = lax.axis_index("seq") * block_count
    segment, block_role, block_pair, tok_scale = block_info(packing, first_block, block_count)
    dpo_sign = jnp.where(block_role == 2, -1.0, 1.0).astype(jnp.float32)
    q_blocks = queries.reshape(block_count, BLK, local_heads, DH)
    k_blocks = key_rows.reshape(block_count, BLK, local_heads, DH)
    v_blocks = value_rows.reshape(block_count, BLK, local_heads, DH)
    weight = (dpo_sign[:, None] * tok_scale)[:, :, None, None]
    g_blocks = (
        weight * grad_out.reshape(block_count, BLK, local_heads, DH).astype(jnp.float32)
    ).astype(jnp.bfloat16)
    block_kv = jnp.einsum("bshd,bshe->bhde", k_blocks, v_blocks, preferred_element_type=jnp.float32)
    block_qg = jnp.einsum("bshd,bshe->bhde", q_blocks, g_blocks, preferred_element_type=jnp.float32)
    group_of = jnp.arange(block_count, dtype=jnp.int32) // (GROUP // BLK)
    same_seg = segment[:, None] == segment[None, :]
    link = same_seg & (group_of[None, :] < group_of[:, None])
    seg_first = segment[0].astype(jnp.float32)
    seg_last = segment[final_index].astype(jnp.float32)
    neutral = jnp.full((), -1.0, jnp.float32)
    zero_state = jnp.zeros((local_heads, DH, DH), jnp.float32)
    is_prompt = block_role == 0
    is_reply = block_role != 0
    pair_count = packing.shape[0] // 3
    pair_hot = (block_pair[:, None] == jnp.arange(pair_count, dtype=jnp.int32)[None, :]).astype(
        jnp.float32
    )
    fwd_seg = masked_sum(segment == segment[final_index], block_kv)
    carried = carried_in(
        (seg_first, seg_last, fwd_seg), "seq", link_combine, (neutral, neutral, zero_state), False
    )
    prompt_part = jnp.einsum(
        "jp,jhde->phde",
        pair_hot * is_prompt[:, None].astype(jnp.float32),
        block_kv,
        precision=highest,
    )
    prompt_all = lax.psum(prompt_part, "seq")
    outside_in = pick_state(carried[1], carried[2], segment, is_reply | is_prompt)
    outside_in = outside_in + jnp.einsum(
        "bp,phde->bhde",
        pair_hot * is_reply[:, None].astype(jnp.float32),
        prompt_all,
        precision=highest,
    )
    rev_seg = masked_sum(segment == segment[0], block_qg)
    returned = carried_in(
        (seg_last, seg_first, rev_seg), "seq", link_combine, (neutral, neutral, zero_state), True
    )
    reply_part = jnp.einsum(
        "jp,jhde->phde",
        pair_hot * is_reply[:, None].astype(jnp.float32),
        block_qg,
        precision=highest,
    )
    reply_all = lax.psum(reply_part, "seq")
    outside_back = pick_state(returned[1], returned[2], segment, is_reply | is_prompt)
    outside_back = outside_back + jnp.einsum(
        "bp,phde->bhde",
        pair_hot * is_prompt[:, None].astype(jnp.float32),
        reply_all,
        precision=highest,
    )
    link_f = link.astype(jnp.float32)
    state = jnp.einsum("bj,jhde->bhde", link_f, block_kv, precision=highest) + outside_in
    back_state = jnp.einsum("bj,bhde->jhde", link_f, block_qg, precision=highest) + outside_back
    state_parts = split_state(state)
    back_parts = split_state(back_state)
    tok_seg = jnp.repeat(segment, BLK).reshape(group_count, GROUP)
    places = jnp.arange(GROUP, dtype=jnp.int32)
    causal = (tok_seg[:, :, None] == tok_seg[:, None, :]) & (
        places[None, :, None] >= places[None, None, :]
    )
    q_groups = queries.reshape(group_count, GROUP, local_heads, DH)
    k_groups = key_rows.reshape(group_count, GROUP, local_heads, DH)
    v_groups = value_rows.reshape(group_count, GROUP, local_heads, DH)
    g_groups = g_blocks.reshape(group_count, GROUP, local_heads, DH)
    scores = jnp.einsum("cshd,cthd->chst", q_groups, k_groups, preferred_element_type=jnp.float32)
    attn_weights = jnp.where(causal[:, None], scores, 0.0).astype(jnp.bfloat16)
    inside = jnp.einsum(
        "chst,cthd->cshd", attn_weights, v_groups, preferred_element_type=jnp.float32
    )
    inside = inside.reshape(block_count, BLK, local_heads, DH)
    outside = state_product("bshd,bhde->bshe", q_blocks, state_parts)
    attended = (tok_scale[:, :, None, None] * (inside + outside)).astype(jnp.bfloat16)
    back_raw = jnp.einsum("cshd,cthd->chst", g_groups, v_groups, preferred_element_type=jnp.float32)
    back_weights = jnp.where(causal[:, None], back_raw, 0.0).astype(jnp.bfloat16)
    grad_q = jnp.einsum(
        "chst,cthd->cshd", back_weights, k_groups, preferred_element_type=jnp.float32
    )
    grad_q = grad_q.reshape(block_count, BLK, local_heads, DH)
    grad_q = grad_q + state_product("bshe,bhde->bshd", g_blocks, state_parts)
    grad_k = jnp.einsum(
        "chst,cshd->cthd", back_weights, q_groups, preferred_element_type=jnp.float32
    )
    grad_k = grad_k.reshape(block_count, BLK, local_heads, DH)
    grad_k = grad_k + state_product("bshe,bhde->bshd", v_blocks, back_parts)
    grad_v = jnp.einsum(
        "chst,cshd->cthd", attn_weights, g_groups, preferred_element_type=jnp.float32
    )
    grad_v = grad_v.reshape(block_count, BLK, local_heads, DH)
    grad_v = grad_v + state_product("bshd,bhde->bshe", k_blocks, back_parts)
    rows = queries.shape[0]
    columns = queries.shape[1]
    return (
        attended.reshape(rows, columns),
        grad_q.astype(jnp.bfloat16).reshape(rows, columns),
        grad_k.astype(jnp.bfloat16).reshape(rows, columns),
        grad_v.astype(jnp.bfloat16).reshape(rows, columns),
    )


def solution(mesh):
    placed = (
        P(("grp", "seq"), "head"),
        P(("grp", "seq"), "head"),
        P(("grp", "seq"), "head"),
        P(("grp", "seq"), "head"),
        P("grp", None),
    )
    return jax.shard_map(
        body,
        mesh=mesh,
        in_specs=placed,
        out_specs=(
            P(("grp", "seq"), "head"),
            P(("grp", "seq"), "head"),
            P(("grp", "seq"), "head"),
            P(("grp", "seq"), "head"),
        ),
        check_vma=False,
    )
```

profile of v0, /device:TPU:0, one launch (start us, length us, event | category | flops | bytes accessed | tf_op | source)
XLA Modules:
  0.0 220.5 jit_solution(9191016044965389598)
XLA Ops:
  7.2 1.0 slice_reduce_fusion.1
  8.5 1.5 convert_bitcast_fusion
  10.0 1.8 copy.230
  11.8 2.0 copy.183
  15.5 1.0 copy-done.10
  16.5 1.8 convolution_bitcast_fusion.1
  18.3 2.0 copy.191
  20.4 3.6 %fusion.44 = f32[1,8,128,128]{3,0,2,1:T(1,128)} fusion(f32[4,8,128,128]{3,0,2,1:T(4,128)S(1)} %copy.191, s32[]{:T(128)} %bitcast.14, s32[4]{0:T(128)S(1)} %convert_reduce_fusion), kind=kOutput, calls=%fused_computation.78 | convolution fusion | flops 6291464 | bytes 2621460 | tf_op jit(solution)/shard_map/j,jhde->hde/dot_general | solution.py:69
  24.0 1.5 copy.226
  26.9 1.3 copy-done
  28.2 4.6 %fusion.9 = f32[1,8,128,128]{3,0,2,1:T(1,128)} fusion(f32[4,8,128,128]{3,2,1,0:T(8,128)S(1)} %fusion.31, s32[]{:T(128)} %bitcast.6, s32[4]{0:T(128)S(1)} %convert_reduce_fusion), kind=kOutput, calls=%fused_computation.25 | convolution fusion | flops 6291464 | bytes 2621460 | tf_op jit(solution)/shard_map/j,jhde->hde/dot_general | solution.py:69
  33.0 4.3 %fusion.52 = f32[1,8,128,128]{3,0,2,1:T(1,128)} fusion(f32[4,8,128,128]{3,0,2,1:T(4,128)S(1)} %copy.191, f32[4]{0:T(128)S(1)} %get-tuple-element.402), kind=kOutput, calls=%fused_computation.100 | convolution fusion | flops 6291456 | bytes 2621456 | tf_op jit(solution)/shard_map/jp,jhde->phde/dot_general | solution.py:136
  37.4 5.0 %fusion.7 = f32[1,8,128,128]{3,0,2,1:T(1,128)} fusion(f32[4,8,128,128]{3,2,1,0:T(8,128)S(1)} %copy-done.1, f32[4]{0:T(128)S(1)} %get-tuple-element.403), kind=kOutput, calls=%fused_computation.23 | convolution fusion | flops 6291456 | bytes 2621456 | tf_op jit(solution)/shard_map/jp,jhde->phde/dot_general | solution.py:118
  43.7 2.6 %copy.222 = f32[512,1024]{0,1:T(8,128)} copy(bf16[512,1024]{1,0:T(8,128)(2,1)} %param.12) | data formatting | bytes 3145728 | tf_op jit(solution)/shard_map/convert_element_type | solution.py:97
  46.3 3.5 %fusion.47 = f32[4,8,128,128]{3,0,2,1:T(4,128)} fusion(f32[4,8,128,128]{3,0,2,1:T(4,128)S(1)} %copy.191, s32[4]{0:T(128)S(1)} %and_select_fusion, s32[4]{0:T(128)S(1)} %get-tuple-element.408), kind=kOutput, calls=%fused_computation.81 | convolution fusion | flops 25165872 | bytes 4194336 | tf_op jit(solution)/shard_map/bj,bhde->jhde/dot_general | solution.py:152
  49.8 3.5 %fusion.11 = f32[4,8,128,128]{3,0,2,1:T(4,128)S(1)} fusion(f32[4,8,128,128]{3,2,1,0:T(8,128)S(1)} %copy-done.2, s32[4]{0:T(128)S(1)} %and_select_fusion, s32[4]{0:T(128)S(1)} %get-tuple-element.408), kind=kOutput, calls=%fused_computation.27 | convolution fusion | flops 25165872 | bytes 4194336 | tf_op jit(solution)/shard_map/bj,jhde->bhde/dot_general | solution.py:151
  53.6 1.3 select_convert_fusion.1
  55.4 1.5 select_convert_fusion
  56.9 2.8 %fusion.21 = f32[8,512,128]{2,1,0:T(8,128)} fusion(bf16[8,512,512]{2,1,0:T(8,128)(2,1)S(1)} %select_convert_fusion, bf16[512,1024]{1,0:T(8,128)(2,1)S(1)} %copy-done.29), kind=kOutput, calls=%fused_computation.41 | convolution fusion | flops 536870912 | bytes 7340032 | tf_op jit(solution)/shard_map/chst,cshd->cthd/dot_general | solution.py:179
  59.7 2.6 %fusion.18 = f32[8,512,128]{2,1,0:T(8,128)} fusion(bf16[8,512,512]{2,1,0:T(8,128)(2,1)S(1)} %select_convert_fusion, bf16[512,1024]{1,0:T(8,128)(2,1)S(1)} %copy-done.30), kind=kOutput, calls=%fused_computation.38 | convolution fusion | flops 536870912 | bytes 7340032 | tf_op jit(solution)/shard_map/chst,cthd->cshd/dot_general | solution.py:174
  62.3 2.1 convolution_bitcast_fusion
  64.5 2.6 %fusion.16 = f32[8,512,128]{2,1,0:T(8,128)} fusion(bf16[8,512,512]{2,1,0:T(8,128)(2,1)S(1)} %select_convert_fusion.1, bf16[512,1024]{1,0:T(8,128)(2,1)S(1)} %copy-done.21), kind=kOutput, calls=%fused_computation.36 | convolution fusion | flops 536870912 | bytes 7340032 | tf_op jit(solution)/shard_map/chst,cthd->cshd/dot_general | solution.py:166
  67.0 2.9 %reshape.384 = f32[4,128,8,128]{1,0,3,2:T(4,128)} reshape(f32[1,512,8,128]{1,3,2,0:T(8,128)} %convolution_bitcast_fusion) | data formatting | bytes 4194304 | tf_op jit(solution)/shard_map/reshape | solution.py:187
  69.9 3.0 %copy.195 = f32[4,128,8,128]{1,3,2,0:T(8,128)} copy(f32[4,128,8,128]{3,1,0,2:T(8,128)} %bitcast.222) | data formatting | bytes 4194304 | tf_op jit(solution)/shard_map/reshape | solution.py:182
  72.9 2.9 %copy.186 = f32[4,128,8,128]{1,3,2,0:T(8,128)} copy(f32[4,128,8,128]{3,1,0,2:T(8,128)} %bitcast.221) | data formatting | bytes 4194304 | tf_op jit(solution)/shard_map/reshape | solution.py:177
  75.8 0.6 dynamic-slice
  76.5 0.8 dynamic-update-slice
  77.2 0.8 dynamic-update-slice.1
  78.0 2.9 %copy.177 = f32[4,128,8,128]{1,3,2,0:T(8,128)} copy(f32[4,128,8,128]{3,1,0,2:T(8,128)} %bitcast.220) | data formatting | bytes 4194304 | tf_op jit(solution)/shard_map/reshape | solution.py:169
  80.9 13.8 %all-reduce.2 = (f32[4]{0:T(128)S(1)}, f32[4]{0:T(128)S(1)}) all-reduce(f32[4]{0:T(128)S(1)} %dynamic-update-slice, f32[4]{0:T(128)S(1)} %dynamic-update-slice.1), channel_id=1, replica_groups=mesh['grp'=2,'seq'=4,'head'=4] {'seq'}, use_global_device_ids=true, to_apply=%add | all-reduce | flops 8 | bytes 64
  94.7 21.5 %while.35 = (s32[]{:T(128)}, f32[]{:T(128)}, f32[8,128,128]{2,1,0:T(8,128)S(1)}, s32[]{:T(128)}, f32[4]{0:T(128)S(1)}, /*index=5*/f32[4,8,128,128]{3,2,1,0:T(8,1...) while((s32[]{:T(128)}, f32[]{:T(128)}, ...), condition=%wide.region_9.10_spmd.clone, body=%wide.region_8.9_spmd.clone.sunk | while | flops 524303 | bytes 1573135 | solution.py:29
  98.3 1.2 fusion.89
  103.7 1.2 fusion.89
  109.1 1.2 fusion.89
  114.5 1.2 fusion.89
  116.3 2.9 %all-gather.5.cloned.1.call-done = f32[32,128,128]{2,1,0:T(8,128)} async-done(((f32[8,128,128]{2,1,0:T(8,128)}), f32[32,128,128]{2,1,0:T(8,128)}) %all-gather.5.cloned.1.call-update) | async-done | bytes 2097168 | tf_op jit(solution)/shard_map/all_gather | solution.py:16
  119.2 22.5 %while.34 = (s32[]{:T(128)}, f32[]{:T(128)}, f32[8,128,128]{2,1,0:T(8,128)S(1)}, s32[]{:T(128)}, f32[4]{0:T(128)S(1)}, /*index=5*/f32[4,8,128,128]{3,2,1,0:T(8,1...) while((s32[]{:T(128)}, f32[]{:T(128)}, f32[8,128,128]{2,1,0:T(8,128)S(1)}, s32[]{:T(128)}, ...), condition=%wide.region_5.6_spmd.clone, body=%wide.region_4.5_spmd.clone.sunk | while | flops 524299 | bytes 1573073 | solution.py:29
  123.0 1.2 fusion.88
  124.9 0.6 dynamic_slice.66
  128.6 1.2 fusion.88
  134.3 1.2 fusion.88
  136.1 0.6 dynamic_slice.66
  139.9 1.2 fusion.88
  141.8 31.4 %all-reduce.6.cloned.1.call-done = (f32[8,128,128]{2,1,0:T(8,128)}, f32[8,128,128]{2,1,0:T(8,128)}) async-done(((f32[8,128,128]{2,1,0:T(8,128)}, f32[8,128,128]{2,1,0:T(8,128)}), (f32[8,128,128]{2,1,0:T(8,128)}, f32[8,128,128]{2,1,0:T(8,128)})) %all-reduce.6.cloned.1.call-update) | async-done | bytes 1048592 | tf_op jit(solution)/shard_map/psum | solution.py:124
  173.2 2.2 fusion.14
  175.4 0.9 fusion.34
  176.6 2.2 fusion.41
  179.2 0.8 copy-done.11
  180.0 1.7 fusion.61
  182.0 2.2 %fusion.38 = f32[4,8,128,128]{3,2,1,0:T(8,128)} fusion(bf16[4,8,128,128]{3,2,1,0:T(8,128)(2,1)S(1)} %fusion.13, bf16[4,128,8,128]{3,2,1,0:T(8,128)(2,1)S(1)} %bitcast.217), kind=kOutput, calls=%fused_computation.59 | convolution fusion | flops 134217728 | bytes 4194304 | tf_op jit(solution)/shard_map/bshd,bhde->bshe/dot_general | solution.py:80
  184.8 1.0 copy-done.18
  186.0 1.8 fusion.2
  187.8 2.4 %copy.202 = bf16[4,128,8,128]{3,2,1,0:T(8,128)(2,1)} copy(bf16[4,128,8,128]{1,3,2,0:T(8,128)(2,1)} %fusion.2) | data formatting | bytes 2097152 | tf_op jit(solution)/shard_map/convert_element_type | solution.py:195
  190.3 2.6 %copy.297 = bf16[64,8,8,128]{3,1,2,0:T(8,128)(2,1)} copy(bf16[64,8,8,128]{3,2,1,0:T(8,128)(2,1)} %bitcast.226) | data formatting | bytes 2097152
  192.9 4.1 %fusion.3 = bf16[4,128,8,128]{1,3,2,0:T(8,128)(2,1)} fusion(f32[4,128,8,128]{1,3,2,0:T(8,128)} %copy.195, f32[4,8,128,128]{3,2,1,0:T(8,128)} %fusion.41, bf16[4,8,128,128]{3,2,1,0:T(8,128)(2,1)S(1)} %copy-done.19, bf16[4,128,8,128]{3,2,1,0:T(8,128)(2,1)S(1)} %bitcast.212), kind=kOutput, calls=%fused_computation.9 | convolution fusion | flops 135790592 | bytes 7340032 | tf_op jit(solution)/shard_map/bshe,bhde->bshd/dot_general | solution.py:81
  197.0 2.5 %copy.196 = bf16[4,128,8,128]{3,2,1,0:T(8,128)(2,1)} copy(bf16[4,128,8,128]{1,3,2,0:T(8,128)(2,1)} %fusion.3) | data formatting | bytes 2097152 | tf_op jit(solution)/shard_map/convert_element_type | solution.py:194
  199.4 2.6 %copy.298 = bf16[64,8,8,128]{3,1,2,0:T(8,128)(2,1)} copy(bf16[64,8,8,128]{3,2,1,0:T(8,128)(2,1)} %bitcast.227) | data formatting | bytes 2097152
  202.6 1.0 copy-done.22
  203.6 0.7 copy-done.24
  205.5 1.5 copy.187
  207.0 2.6 %copy.299 = bf16[64,8,8,128]{3,1,2,0:T(8,128)(2,1)} copy(bf16[64,8,8,128]{3,2,1,0:T(8,128)(2,1)} %bitcast.228) | data formatting | bytes 2097152
  209.6 2.4 %fusion.6 = bf16[4,128,8,128]{1,3,2,0:T(8,128)(2,1)S(1)} fusion(f32[4,128,8,128]{1,3,2,0:T(8,128)S(1)} %copy-done.27, f32[4,8,128,128]{3,2,1,0:T(8,128)} %fusion.38, bf16[4,8,128,128]{3,2,1,0:T(8,128)(2,1)S(1)} %copy-done.23, f32[4,128]{1,0:T(4,128)S(1)} %get-tuple-element.401, bf16[4,128,8,128]{3,2,1,0:T(8,128)(2,1)S(1)} %bitcast.218), kind=kOutput, calls=%fused_computation.14 | convolution fusion | flops 136314880 | bytes 7342080 | tf_op jit(solution)/shard_map/bshd,bhde->bshe/dot_general | solution.py:81
  212.0 0.7 copy.178
  212.8 1.2 copy.300
  (111 shorter events, 16.4 us)
Async XLA Ops:
  7.2 87.6 %all-gather.7.cloned.1.call-start = ((), (), s32[]{:S(2)}) async-start(), calls=%async_computation.1 | async-start | bytes 2621440 | tf_op jit(solution)/shard_map/all_gather | solution.py:16
  11.8 2.0 copy-start.28
  14.1 1.4 copy-start.15
  15.5 1.0 copy-start.10
  20.3 5.2 %copy-start.20 = (bf16[512,1024]{1,0:T(8,128)(2,1)S(1)}, bf16[512,1024]{1,0:T(8,128)(2,1)}, u32[]{:S(2)}) copy-start(bf16[512,1024]{1,0:T(8,128)(2,1)} %param.11) | copy-start | bytes 3145732
  24.0 95.2 %all-gather.5.cloned.1.call-start = ((), (), s32[]{:S(2)}) async-start(), calls=%async_computation | async-start | bytes 2621440 | tf_op jit(solution)/shard_map/all_gather | solution.py:16
  25.5 1.0 copy-start.8
  25.8 1.0 copy-start.5
  26.9 1.3 copy-start
  32.8 140.4 %all-reduce.6.cloned.1.call-start = ((), (), s32[]{:S(2)}) async-start(), calls=%async_computation.2 | async-start | bytes 2097152 | tf_op jit(solution)/shard_map/psum | solution.py:124
  33.0 4.3 %copy-start.1 = (f32[4,8,128,128]{3,2,1,0:T(8,128)S(1)}, f32[4,8,128,128]{3,2,1,0:T(8,128)}, u32[]{:S(2)}) copy-start(f32[4,8,128,128]{3,2,1,0:T(8,128)} %copy-done) | copy-start | bytes 6291460
  46.3 3.5 %copy-start.2 = (f32[4,8,128,128]{3,2,1,0:T(8,128)S(1)}, f32[4,8,128,128]{3,2,1,0:T(8,128)}, u32[]{:S(2)}) copy-start(f32[4,8,128,128]{3,2,1,0:T(8,128)} %copy-done) | copy-start | bytes 6291460
  49.8 3.8 %copy-start.29 = (bf16[512,1024]{1,0:T(8,128)(2,1)S(1)}, bf16[512,1024]{1,0:T(8,128)(2,1)}, u32[]{:S(2)}) copy-start(bf16[512,1024]{1,0:T(8,128)(2,1)} %param.9) | copy-start | bytes 3145732
  49.8 3.8 %copy-start.30 = (bf16[512,1024]{1,0:T(8,128)(2,1)S(1)}, bf16[512,1024]{1,0:T(8,128)(2,1)}, u32[]{:S(2)}) copy-start(bf16[512,1024]{1,0:T(8,128)(2,1)} %param.10) | copy-start | bytes 3145732
  53.5 1.6 copy-start.4
  53.5 1.9 copy-start.21
  72.9 2.9 %copy-start.34 = (u32[32]{0:T(128)S(1)}, u32[32]{0:T(128)}, u32[]{:S(2)}) copy-start(u32[32]{0:T(128)} %constant.136) | copy-start | bytes 388
  173.2 2.2 copy-start.9
  175.4 1.2 copy-start.6
  176.6 2.2 copy-start.31
  178.8 1.2 copy-start.11
  180.0 1.8 copy-start.13
  180.0 2.0 copy-start.16
  182.0 2.2 %copy-start.3 = (f32[4,8,128,128]{3,0,2,1:T(4,128)S(1)}, f32[4,8,128,128]{3,0,2,1:T(4,128)}, u32[]{:S(2)}) copy-start(f32[4,8,128,128]{3,0,2,1:T(4,128)} %fusion.47) | copy-start | bytes 6291460
  182.0 2.2 %copy-start.33 = (f32[8,128,128]{2,1,0:T(8,128)S(1)}, f32[8,128,128]{2,1,0:T(8,128)}, u32[]{:S(2)}) copy-start(f32[8,128,128]{2,1,0:T(8,128)} %get-tuple-element.396) | copy-start | bytes 1572868
  184.3 1.7 copy-start.25
  184.8 1.0 copy-start.18
  190.3 2.6 %copy-start.7 = (bf16[64,8,8,128]{3,2,1,0:T(8,128)(2,1)S(1)}, bf16[64,8,8,128]{3,2,1,0:T(8,128)(2,1)}, u32[]{:S(2)}) copy-start(bf16[64,8,8,128]{3,2,1,0:T(8,128)(2,1)} %copy-done.5) | copy-start | bytes 3145732
  190.3 2.6 %copy-start.19 = (bf16[4,8,128,128]{3,2,1,0:T(8,128)(2,1)S(1)}, bf16[4,8,128,128]{3,2,1,0:T(8,128)(2,1)}, u32[]{:S(2)}) copy-start(bf16[4,8,128,128]{3,2,1,0:T(8,128)(2,1)} %copy-done.18) | copy-start | bytes 3145732
  197.0 5.0 %copy-start.32 = (f32[8,128,128]{2,1,0:T(8,128)S(1)}, f32[8,128,128]{2,1,0:T(8,128)}, u32[]{:S(2)}) copy-start(f32[8,128,128]{2,1,0:T(8,128)} %get-tuple-element.395) | copy-start | bytes 1572868
  199.4 2.6 %copy-start.14 = (bf16[4,8,128,128]{3,2,1,0:T(8,128)(2,1)S(1)}, bf16[4,8,128,128]{3,2,1,0:T(8,128)(2,1)}, u32[]{:S(2)}) copy-start(bf16[4,8,128,128]{3,2,1,0:T(8,128)(2,1)} %copy-done.13) | copy-start | bytes 3145732
  202.0 1.6 copy-start.12
  202.0 2.3 %copy-start.24 = (f32[4,128,8,128]{1,3,2,0:T(8,128)S(1)}, f32[4,128,8,128]{1,3,2,0:T(8,128)}, u32[]{:S(2)}) copy-start(f32[4,128,8,128]{1,3,2,0:T(8,128)} %copy.186) | copy-start | bytes 6291460
  202.0 2.9 %copy-start.26 = (f32[4,8,128,128]{3,2,1,0:T(8,128)S(1)}, f32[4,8,128,128]{3,2,1,0:T(8,128)}, u32[]{:S(2)}) copy-start(f32[4,8,128,128]{3,2,1,0:T(8,128)} %fusion.61) | copy-start | bytes 6291460
  202.6 1.0 copy-start.22
  205.5 4.1 %copy-start.17 = (bf16[64,8,8,128]{3,2,1,0:T(8,128)(2,1)S(1)}, bf16[64,8,8,128]{3,2,1,0:T(8,128)(2,1)}, u32[]{:S(2)}) copy-start(bf16[64,8,8,128]{3,2,1,0:T(8,128)(2,1)} %copy-done.15) | copy-start | bytes 3145732
  205.5 4.1 %copy-start.23 = (bf16[4,8,128,128]{3,2,1,0:T(8,128)(2,1)S(1)}, bf16[4,8,128,128]{3,2,1,0:T(8,128)(2,1)}, u32[]{:S(2)}) copy-start(bf16[4,8,128,128]{3,2,1,0:T(8,128)(2,1)} %copy-done.22) | copy-start | bytes 3145732
  207.0 2.6 %copy-start.27 = (f32[4,128,8,128]{1,3,2,0:T(8,128)S(1)}, f32[4,128,8,128]{1,3,2,0:T(8,128)}, u32[]{:S(2)}) copy-start(f32[4,128,8,128]{1,3,2,0:T(8,128)} %copy.177) | copy-start | bytes 6291460
Sparse Core Ops, SparseCore 0:
  24.1 48.5 all-gather.6
  74.3 44.8 all-gather.4
  122.2 50.9 all-reduce.5
where the time goes:
time: 222 us; the launch traced here: 221 us
  local copies, waits for them, and re-layouts  60.3 us (27%)
  matrix products  55.7 us (25%)
  waiting for transfers between devices  34.4 us (15%)
  loops' own time  24.5 us (11%)
  other arithmetic  16.1 us (7%)
  between operations  15.4 us (7%)
  blocking collectives  13.8 us (6%)
    psum x1, waiting for transfers between devices, body(): prompt_all = lax.psum(prompt_part, 'seq')  31.4 us
    another operation x2, loops' own time, carried_in(): return lax.fori_loop(0, length, turn, start)  24.5 us
    unnamed x83, local copies, waits for them, and re-layouts  23.4 us
    unnamed x1, blocking collectives  13.8 us
    select_n x8, other arithmetic, turn(): return jax.tree.map(lambda a, b: jnp.where(reached, a, b), new, before)  9.79 us
    dynamic_slice x16, local copies, waits for them, and re-layouts, turn(): new = combine(before, jax.tree.map(lambda part: part[at], everything))  9.74 us
    dot_general x4, matrix products, state_product(): jnp.einsum(form, token_rows, parts[1], preferred_element_type=jnp.float32)  8.89 us
    dot_general x2, matrix products, masked_sum(): jnp.einsum('j,jhde->hde', flags.astype(jnp.float32), states, precision=hi...  8.21 us
  transfers between devices with their start and end apart: 3, of which 2 were waited for; matrix products, arithmetic and copies ran while one was open for 33% of the time, Pallas kernels for 0%

commit v1 on v0

--- a/solution.py
+++ b/solution.py
@@ -1,11 +1,503 @@
+import functools
+
 import jax
 import jax.numpy as jnp
 from jax import lax
+from jax.experimental import pallas as pl
+from jax.experimental.pallas import tpu as pltpu
 from jax.sharding import PartitionSpec as P
 
 DH = 128
 BLK = 128
 GROUP = 512
+NB = GROUP // BLK
+CHUNKS = 2
+F32 = jnp.float32
+BF16 = jnp.bfloat16
+
+
+def flag(condition):
+    return jnp.where(condition, 1, 0).astype(jnp.int32)
+
+
+def either(*flags):
+    out = flags[0]
+    for f in flags[1:]:
+        out = jnp.maximum(out, f)
+    return out
+
+
+def pick(index, choices):
+    out = jnp.int32(0) + choices[-1]
+    for n in range(len(choices) - 2, -1, -1):
+        out = jnp.where(index == n, choices[n], out)
+    return out
+
+
+def pick_rows(index, rows):
+    return [pick(index, [row[c] for row in rows]) for c in range(len(rows[0]))]
+
+
+def edges(pack, blocks):
+    one, two = pack[1, 0], pack[2, 0]
+
+    def seg(b):
+        return flag(b >= one) + flag(b >= two)
+
+    first = [seg(blocks * i) for i in range(4)]
+    last = [seg(blocks * i + blocks - 1) for i in range(4)]
+    return seg, first, last
+
+
+def message_one(pack, d, blocks):
+    _, f, l = edges(pack, blocks)
+    every = either(flag(l[2] == 0), flag(l[2] == 1) * flag(l[1] == 0))
+    at_p, from_p = flag(l[0] == 0), flag(f[2] == 0)
+    return pick_rows(
+        d,
+        [
+            [1, 1, flag(f[2] == 1), flag(f[2] == 2)],
+            [at_p, at_p, 0, 1 - at_p],
+            [from_p, 0, from_p * flag(f[3] == 1), from_p * flag(f[3] == 2) + 1 - from_p],
+            [0, every, either(every, flag(l[2] == 1)), either(every, flag(l[2] == 2))],
+        ],
+    )
+
+
+def message_two(pack, d, blocks):
+    _, f, l = edges(pack, blocks)
+    return pick_rows(
+        d,
+        [
+            [flag(l[0] == 0), 1, 1, 0, 0],
+            [1, 1, 1, flag(f[2] == 1), flag(f[2] == 2)],
+            [
+                1 - flag(l[1] == 1) * flag(l[2] == 2),
+                0,
+                flag(l[1] == 0),
+                flag(l[1] <= 1),
+                flag(l[1] != 1),
+            ],
+            [flag(f[2] != 0), 0, 0, 0, 1],
+        ],
+    )
+
+
+def message_three(pack, d, blocks):
+    _, f, l = edges(pack, blocks)
+    from_p, at_p, first_p = flag(f[2] == 0), flag(l[1] == 0), flag(f[1] == 0)
+    return pick_rows(
+        d,
+        [
+            [first_p, 1, 0, 1 - first_p, 0],
+            [
+                1 - flag(l[0] == 1) * flag(l[1] == 2),
+                0,
+                flag(l[0] == 0),
+                flag(l[0] <= 1),
+                flag(l[0] != 1),
+            ],
+            [
+                either(from_p, flag(f[2] == f[3])),
+                1,
+                from_p,
+                (1 - from_p) * flag(f[3] == 1),
+                (1 - from_p) * flag(f[3] == 2),
+            ],
+            [1 - at_p, 0, 0, at_p, 0],
+        ],
+    )
+
+
+def state_table(pack, d, blocks):
+    _, f, l = edges(pack, blocks)
+    apart = flag(f[2] == 1) * flag(l[1] != 0)
+    from_p = flag(f[2] == 0)
+    crossing = (1 - from_p) * flag(f[3] == 1)
+    forward = [
+        pick_rows(d, [[0, 0, 0], [1, 0, 0], [0, 1, 0], [0, 0, 1]]),
+        pick_rows(
+            d,
+            [
+                [0, 0, 0],
+                [1, 0, flag(f[1] == 1) * flag(f[2] == 2)],
+                [0, 1, 0],
+                [from_p * flag(f[3] == 1), 0, 1],
+            ],
+        ),
+        pick_rows(
+            d,
+            [
+                [0, 0, 0],
+                [1, 0, 0],
+                [0, 1 - apart, apart],
+                [
+                    from_p * flag(f[3] == 2),
+                    either(crossing, (1 - from_p) * flag(f[2] != f[3])),
+                    1 - crossing,
+                ],
+            ],
+        ),
+    ]
+    backward = [
+        pick_rows(
+            d,
+            [
+                [
+                    flag(l[0] == 1),
+                    either(flag(l[0] == 1), flag(l[0] == 0) * flag(l[1] == 1)),
+                    1,
+                ],
+                [0, 1, flag(l[1] == 1)],
+                [1, 0, 0],
+                [0, 0, 0],
+            ],
+        ),
+        pick_rows(
+            d,
+            [
+                [0, 0, flag(l[0] == 1)],
+                [0, flag(l[1] == 1), 0],
+                [flag(l[2] == 1) * flag(l[1] != 0), 0, flag(l[2] == 1) * flag(l[1] == 0)],
+                [0, 0, 0],
+            ],
+        ),
+        pick_rows(
+            d,
+            [
+                [0, 0, flag(l[0] == 2)],
+                [0, flag(l[1] == 2), 0],
+                [flag(l[2] == 2), 0, 0],
+                [0, 0, 0],
+            ],
+        ),
+    ]
+    return forward, backward
+
+
+def block_rows(value_of, like):
+    return jnp.concatenate([jnp.full((BLK, like), value_of(b), F32) for b in range(NB)], axis=0)
+
+
+def fill_scale(pack, d, blocks, scale_ref, sign_ref):
+    seg, _, _ = edges(pack, blocks)
+    prompt = pack[0, 1] - pack[0, 0]
+    for b in range(NB):
+        block = d * blocks + b
+        s = seg(block)
+        start = pick(s, [pack[0, 0], pack[1, 0], pack[2, 0]])
+        role = pick(s, [pack[0, 3], pack[1, 3], pack[2, 3]])
+        base = (block - start) * BLK + 1 + jnp.where(role != 0, prompt * BLK, 0)
+        seen = base + lax.broadcasted_iota(jnp.int32, (BLK, DH), 0)
+        scale = lax.rsqrt((seen * DH).astype(F32))
+        rows = pl.ds(b * BLK, BLK)
+        if scale_ref is not None:
+            scale_ref[rows, :] = scale
+        if sign_ref is not None:
+            sign_ref[rows, :] = jnp.where(role == 2, -1.0, 1.0) * scale
+
+
+def weighted(grad, sign_ref):
+    return (grad.astype(F32) * sign_ref[...]).astype(BF16)
+
+
+def contract_rows(a, b):
+    return lax.dot_general(a, b, (((0,), (0,)), ((), ())), preferred_element_type=F32)
+
+
+def contract_cols(a, b):
+    return lax.dot_general(a, b, (((1,), (1,)), ((), ())), preferred_element_type=F32)
+
+
+def plain(a, b):
+    return lax.dot_general(a, b, (((1,), (0,)), ((), ())), preferred_element_type=F32)
+
+
+def row_mask(pack, d, blocks, coefs):
+    seg, _, _ = edges(pack, blocks)
+    return block_rows(lambda b: pick(seg(d * blocks + b), coefs).astype(F32), DH).astype(BF16)
+
+
+def sums_kernel(blocks, per_step, messages, pack, place, q_ref, k_ref, v_ref, g_ref, *refs):
+    outs, sign_ref = refs[:-1], refs[-1]
+    d = place[0]
+    step = pl.program_id(0)
+
+    @pl.when(step == 0)
+    def _():
+        fill_scale(pack, d, blocks, None, sign_ref)
+
+    tables = [m(pack, d, blocks)[-4:] for m in messages]
+    masks = [row_mask(pack, d, blocks, t[1:]) for t in tables]
+    per_chunk = pl.num_programs(0) // CHUNKS
+
+    def emit(index, head, value):
+        for c in range(CHUNKS):
+
+            @pl.when(step // per_chunk == c)
+            def _():
+                outs[index * CHUNKS + c][head] = value
+
+    for head in range(per_step):
+        cols = pl.ds(head * DH, DH)
+        for index, (table, mask) in enumerate(zip(tables, masks)):
+
+            @pl.when(table[0] == 1)
+            def _():
+                emit(index, head, contract_rows(k_ref[:, cols] * mask, v_ref[:, cols]))
+
+            @pl.when(table[0] == 0)
+            def _():
+                grads = weighted(g_ref[:, cols], sign_ref)
+                emit(index, head, contract_rows(q_ref[:, cols] * mask, grads))
+
+
+def local_sums(messages, blocks, pack, place, q, k, v, g):
+    heads = q.shape[1] // DH
+    per_step = 2 if heads % (2 * CHUNKS) == 0 else 1
+    steps = heads // per_step
+    per_chunk = steps // CHUNKS
+
+    def needed(kind):
+        def index(i, pack_ref, place_ref):
+            use = jnp.int32(0)
+            for m in messages:
+                use = either(use, flag(m(pack_ref, place_ref[0], blocks)[-4] == kind))
+            return (0, i * use)
+
+        return index
+
+    def chunk(c):
+        return lambda i, *_: (jnp.clip(i - c * per_chunk, 0, per_chunk - 1), 0, 0)
+
+    rows = q.shape[0]
+    tokens = (rows, per_step * DH)
+    out = jax.ShapeDtypeStruct((heads // CHUNKS, DH, DH), F32)
+    return pl.pallas_call(
+        functools.partial(sums_kernel, blocks, per_step, messages),
+        out_shape=[out] * (CHUNKS * len(messages)),
+        grid_spec=pltpu.PrefetchScalarGridSpec(
+            num_scalar_prefetch=2,
+            grid=(steps,),
+            in_specs=[
+                pl.BlockSpec(tokens, needed(0)),
+                pl.BlockSpec(tokens, needed(1)),
+                pl.BlockSpec(tokens, needed(1)),
+                pl.BlockSpec(tokens, needed(0)),
+            ],
+            out_specs=[
+                pl.BlockSpec((per_step, DH, DH), chunk(c)) for _ in messages for c in range(CHUNKS)
+            ],
+            scratch_shapes=[pltpu.VMEM((rows, DH), F32)],
+        ),
+        compiler_params=pltpu.CompilerParams(vmem_limit_bytes=16 * 2**20),
+        cost_estimate=pl.CostEstimate(
+            flops=2 * rows * DH * DH * heads * len(messages),
+            bytes_accessed=4 * rows * heads * DH,
+            transcendentals=0,
+        ),
+        name="local_sums",
+    )(pack, place, q, k, v, g)
+
+
+def join_kernel(blocks, message, pack, place, got_ref, own_ref, out_ref):
+    keep = message(pack, place[0], blocks)[0] == 1
+
+    @pl.when(keep)
+    def _():
+        out_ref[...] = got_ref[...] + own_ref[...]
+
+    @pl.when(jnp.logical_not(keep))
+    def _():
+        out_ref[...] = own_ref[...]
+
+
+def join(message, blocks, pack, place, got, own):
+    heads = got.shape[0]
+    return pl.pallas_call(
+        functools.partial(join_kernel, blocks, message),
+        out_shape=jax.ShapeDtypeStruct(got.shape, F32),
+        grid_spec=pltpu.PrefetchScalarGridSpec(
+            num_scalar_prefetch=2,
+            grid=(1,),
+            in_specs=[pl.BlockSpec((heads, DH, DH), lambda i, *_: (0, 0, 0))] * 2,
+            out_specs=pl.BlockSpec((heads, DH, DH), lambda i, *_: (0, 0, 0)),
+        ),
+        compiler_params=pltpu.CompilerParams(vmem_limit_bytes=8 * 2**20),
+        cost_estimate=pl.CostEstimate(
+            flops=got.size, bytes_accessed=12 * got.size, transcendentals=0
+        ),
+        name="join",
+    )(pack, place, got, own)
+
+
+def inside_kernel(blocks, pack, place, q_ref, k_ref, v_ref, g_ref, o1, o2, o3, o4, mask_ref, sign_ref):
+    d = place[0]
+    half = GROUP // 2
+
+    @pl.when(pl.program_id(0) == 0)
+    def _():
+        fill_scale(pack, d, blocks, None, sign_ref)
+        seg, _, _ = edges(pack, blocks)
+        tri = lax.broadcasted_iota(jnp.int32, (BLK, BLK), 0) >= lax.broadcasted_iota(
+            jnp.int32, (BLK, BLK), 1
+        )
+        for t in range(NB):
+            for s in range(NB):
+                seg_t, seg_s = seg(d * blocks + t), seg(d * blocks + s)
+                ok = either(flag(seg_t == seg_s), flag(seg_s == 0)).astype(F32)
+                if s > t:
+                    tile = jnp.zeros((BLK, BLK), F32)
+                elif s == t:
+                    tile = jnp.where(tri, 1.0, 0.0)
+                else:
+                    tile = jnp.full((BLK, BLK), ok, F32)
+                mask_ref[pl.ds(t * BLK, BLK), pl.ds(s * BLK, BLK)] = tile.astype(BF16)
+
+    q, k, v = q_ref[...], k_ref[...], v_ref[...]
+    g = weighted(g_ref[...], sign_ref)
+    lo, hi = slice(0, half), slice(half, GROUP)
+
+    def masked(a, b, rows, cols):
+        return contract_cols(a[rows], b[cols]).astype(BF16) * mask_ref[rows, cols]
+
+    s_lo = masked(q, k, lo, lo)
+    s_hi = masked(q, k, hi, slice(0, GROUP))
+    o1[lo, :] = plain(s_lo, v[lo])
+    o1[hi, :] = plain(s_hi, v)
+    gv = contract_rows(s_hi, g[hi])
+    o4[lo, :] = gv[lo] + contract_rows(s_lo, g[lo])
+    o4[hi, :] = gv[hi]
+    b_lo = masked(g, v, lo, lo)
+    b_hi = masked(g, v, hi, slice(0, GROUP))
+    o2[lo, :] = plain(b_lo, k[lo])
+    o2[hi, :] = plain(b_hi, k)
+    gk = contract_rows(b_hi, q[hi])
+    o3[lo, :] = gk[lo] + contract_rows(b_lo, q[lo])
+    o3[hi, :] = gk[hi]
+
+
+def inside_products(blocks, pack, place, q, k, v, g):
+    rows, cols = q.shape
+    heads = cols // DH
+    spec = pl.BlockSpec((rows, DH), lambda i, *_: (0, i))
+    return pl.pallas_call(
+        functools.partial(inside_kernel, blocks),
+        out_shape=[jax.ShapeDtypeStruct((rows, cols), F32)] * 4,
+        grid_spec=pltpu.PrefetchScalarGridSpec(
+            num_scalar_prefetch=2,
+            grid=(heads,),
+            in_specs=[spec] * 4,
+            out_specs=[spec] * 4,
+            scratch_shapes=[pltpu.VMEM((rows, rows), BF16), pltpu.VMEM((rows, DH), F32)],
+        ),
+        compiler_params=pltpu.CompilerParams(vmem_limit_bytes=24 * 2**20),
+        cost_estimate=pl.CostEstimate(
+            flops=9 * rows * rows * DH * heads,
+            bytes_accessed=24 * rows * cols,
+            transcendentals=0,
+        ),
+        name="inside_products",
+    )(pack, place, q, k, v, g)
+
+
+def final_kernel(blocks, first, pack, place, *refs):
+    q_ref, k_ref, v_ref, g_ref, i1, i2, i3, i4, r1, r2, r3 = refs[:11]
+    o1, o2, o3, o4, scale_ref, sign_ref, st_ref, bk_ref = refs[-8:]
+    d = place[0]
+
+    @pl.when(pl.program_id(0) == 0)
+    def _():
+        fill_scale(pack, d, blocks, scale_ref, sign_ref)
+
+    seg, _, _ = edges(pack, blocks)
+    forward, backward = state_table(pack, d, blocks)
+    got = [r1[0], r2[0], r3[0]]
+    for x in range(3):
+        for table, out in ((forward, st_ref), (backward, bk_ref)):
+            total = None
+            for weight, part in zip(table[x], got):
+                term = weight.astype(F32) * part
+                total = term if total is None else total + term
+            out[x] = total.astype(BF16)
+    for b in range(NB):
+        rows = pl.ds(b * BLK, BLK)
+        s = seg(d * blocks + b)
+        st, bk = st_ref[s], bk_ref[s]
+        q, k, v = q_ref[rows, :], k_ref[rows, :], v_ref[rows, :]
+        g = (g_ref[rows, :].astype(F32) * sign_ref[rows, :]).astype(BF16)
+        o1[rows, :] = (scale_ref[rows, :] * (i1[rows, :] + plain(q, st))).astype(BF16)
+        o2[rows, :] = (i2[rows, :] + contract_cols(g, st)).astype(BF16)
+        o3[rows, :] = (i3[rows, :] + contract_cols(v, bk)).astype(BF16)
+        o4[rows, :] = (i4[rows, :] + plain(k, bk)).astype(BF16)
+
+
+def final_products(blocks, chunk, pack, place, tokens, inside, got, before):
+    rows, cols = tokens[0].shape
+    heads = cols // DH // CHUNKS
+    first = chunk * heads
+    spec = pl.BlockSpec((rows, DH), lambda i, *_: (0, first + i))
+    state = pl.BlockSpec((1, DH, DH), lambda i, *_: (i, 0, 0))
+    operands = [*tokens, *inside, *got]
+    specs = [spec] * 8 + [state] * 3
+    aliases = {}
+    if before is not None:
+        aliases = {2 + len(operands) + n: n for n in range(4)}
+        operands += list(before)
+        specs += [pl.BlockSpec(memory_space=pl.ANY)] * 4
+    return pl.pallas_call(
+        functools.partial(final_kernel, blocks, first),
+        out_shape=[jax.ShapeDtypeStruct((rows, cols), BF16)] * 4,
+        grid_spec=pltpu.PrefetchScalarGridSpec(
+            num_scalar_prefetch=2,
+            grid=(heads,),
+            in_specs=specs,
+            out_specs=[spec] * 4,
+            scratch_shapes=[
+                pltpu.VMEM((rows, DH), F32),
+                pltpu.VMEM((rows, DH), F32),
+                pltpu.VMEM((3, DH, DH), BF16),
+                pltpu.VMEM((3, DH, DH), BF16),
+            ],
+        ),
+        input_output_aliases=aliases,
+        compiler_params=pltpu.CompilerParams(vmem_limit_bytes=16 * 2**20),
+        cost_estimate=pl.CostEstimate(
+            flops=8 * rows * DH * DH * heads,
+            bytes_accessed=32 * rows * DH * heads,
+            transcendentals=0,
+        ),
+        name="final_products",
+    )(pack, place, *operands)
+
+
+def exchange_body(queries, key_rows, value_rows, grad_out, packing):
+    blocks = queries.shape[0] // BLK
+    place = lax.axis_index("seq").astype(jnp.int32).reshape(1)
+    tokens = (queries, key_rows, value_rows, grad_out)
+    near = [(i, i ^ 1) for i in range(4)]
+    across = [(i, 3 - i) for i in range(4)]
+
+    def send(values, pairs):
+        return [lax.ppermute(value, "seq", pairs) for value in values]
+
+    sent = local_sums((message_one,), blocks, packing, place, *tokens)
+    one = send(sent, near)
+    own = local_sums((message_two, message_three), blocks, packing, place, *tokens)
+    own_two, own_three = own[:CHUNKS], own[CHUNKS:]
+    inside = inside_products(blocks, packing, place, *tokens)
+    two = send(
+        [join(message_two, blocks, packing, place, a, b) for a, b in zip(one, own_two)], across
+    )
+    three = send(
+        [join(message_three, blocks, packing, place, a, b) for a, b in zip(two, own_three)], near
+    )
+    out = None
+    for c in range(CHUNKS):
+        out = final_products(
+            blocks, c, packing, place, tokens, inside, (one[c], two[c], three[c]), out
+        )
+    return tuple(out)
 
 
 highest = lax.Precision.HIGHEST
@@ -204,8 +696,18 @@
         P(("grp", "seq"), "head"),
         P("grp", None),
     )
-    return jax.shard_map(
-        body,
+    pairs_of = lambda packing: packing.shape[0] // mesh.shape["grp"] // 3
+
+    def program(queries, key_rows, value_rows, grad_out, packing):
+        small = mesh.shape["seq"] == 4 and pairs_of(packing) == 1
+        rows = queries.shape[0] // mesh.shape["grp"] // mesh.shape["seq"]
+        fits = rows == GROUP and queries.shape[1] // mesh.shape["head"] % (CHUNKS * DH) == 0
+        return placed_call(exchange_body if small and fits else body)(
+            queries, key_rows, value_rows, grad_out, packing
+        )
+
+    placed_call = lambda one: jax.shard_map(
+        one,
         mesh=mesh,
         in_specs=placed,
         out_specs=(
@@ -216,3 +718,4 @@
         ),
         check_vma=False,
     )
+    return program

time: 222 us -> 66 us (0.30)
  matrix products: 55.7 us -> 0 us
  local copies, waits for them, and re-layouts: 60.3 us -> 5.6 us
  Pallas kernels: 0 us -> 30.4 us
  waiting for transfers between devices: 34.4 us -> 4.57 us
  loops' own time: 24.5 us -> 0 us
  starting transfers between devices: 0.3 us -> 24.4 us
  other arithmetic: 16.1 us -> 0 us
  between operations: 15.4 us -> 0.76 us
  blocking collectives: 13.8 us -> 0 us
    dot_general x22 -> x0, matrix products: 55.7 us -> none  [the longest x4 8.89 us: state_product(): jnp.einsum(form, token_rows, parts[1], preferred_element_type=jnp.float32)]
    psum x1 -> x0, waiting for transfers between devices: 31.4 us -> none  [body(): prompt_all = lax.psum(prompt_part, 'seq')]
    pallas_call x0 -> x9, Pallas kernels: none -> 30.4 us  [the longest x1 10.1 us: inside_products(): pl.pallas_call(functools.partial(inside_kernel, blocks), out_shape=[jax.S...]
    another operation x2 -> x0, loops' own time: 24.5 us -> none  [carried_in(): return lax.fori_loop(0, length, turn, start)]
    ppermute x0 -> x6, starting transfers between devices: none -> 24.4 us  [send(): return [lax.ppermute(value, 'seq', pairs) for value in values]]
    unnamed x83 -> x20, local copies, waits for them, and re-layouts: 23.4 us -> 5.6 us
    unnamed x1 -> x0, blocking collectives: 13.8 us -> none
    reshape x4 -> x0, local copies, waits for them, and re-layouts: 11.7 us -> none  [the longest x1 2.96 us: body(): grad_k = grad_k.reshape(block_count, BLK, local_heads, DH)]
  transfers between devices with their start and end apart: 3 -> 6, of which waited for: 2 -> 3; matrix products, arithmetic and copies ran while one was open for 33% -> 0% of each run, Pallas kernels for 0% -> 34%
where the time goes in v1:
time: 66 us; the launch traced here: 65.7 us
  Pallas kernels  30.4 us (46%)
  starting transfers between devices  24.4 us (37%)
  local copies, waits for them, and re-layouts  5.6 us (8%)
  waiting for transfers between devices  4.57 us (7%)
  between operations  0.76 us (1%)
    ppermute x6, starting transfers between devices, send(): return [lax.ppermute(value, 'seq', pairs) for value in values]  24.4 us
    pallas_call x1, Pallas kernels, inside_products(): pl.pallas_call(functools.partial(inside_kernel, blocks), out_shape=[jax.S...  10.1 us
    pallas_call x2, Pallas kernels, final_products(): pl.pallas_call(functools.partial(final_kernel, blocks, first), out_shape=...  9.08 us
    pallas_call x2, Pallas kernels, local_sums(): pl.pallas_call(functools.partial(sums_kernel, blocks, per_step, messages)...  8.81 us
    unnamed x20, local copies, waits for them, and re-layouts  5.6 us
    ppermute x6, waiting for transfers between devices, send(): return [lax.ppermute(value, 'seq', pairs) for value in values]  4.57 us
    pallas_call x4, Pallas kernels, join(): pl.pallas_call(functools.partial(join_kernel, blocks, message), out_shape...  2.43 us
  transfers between devices with their start and end apart: 6, of which 3 were waited for; matrix products, arithmetic and copies ran while one was open for 0% of the time, Pallas kernels for 34%

profile of v1, /device:TPU:0, one launch (start us, length us, event | category | flops | bytes accessed | tf_op | source)
XLA Modules:
  0.0 65.7 jit_solution(7752211336430447036)
XLA Ops:
  0.6 0.0 copy-start
  0.6 1.2 %copy-done = bf16[512,1024]{1,0:T(8,128)(2,1)S(1)} copy-done((bf16[512,1024]{1,0:T(8,128)(2,1)S(1)}, bf16[512,1024]{1,0:T(8,128)(2,1)}, u32[]{:S(2)}) %copy-start) | copy-done | bytes 1048600
  1.9 0.0 copy-start.2
  1.9 1.2 %copy-done.2 = bf16[512,1024]{1,0:T(8,128)(2,1)S(1)} copy-done((bf16[512,1024]{1,0:T(8,128)(2,1)S(1)}, bf16[512,1024]{1,0:T(8,128)(2,1)}, u32[]{:S(2)}) %copy-start.2) | copy-done | bytes 1048600
  3.1 0.0 copy-start.4
  3.1 1.2 %copy-done.4 = bf16[512,1024]{1,0:T(8,128)(2,1)S(1)} copy-done((bf16[512,1024]{1,0:T(8,128)(2,1)S(1)}, bf16[512,1024]{1,0:T(8,128)(2,1)}, u32[]{:S(2)}) %copy-start.4) | copy-done | bytes 1048600
  4.3 0.0 copy-start.6
  4.3 1.2 %copy-done.6 = bf16[512,1024]{1,0:T(8,128)(2,1)S(1)} copy-done((bf16[512,1024]{1,0:T(8,128)(2,1)S(1)}, bf16[512,1024]{1,0:T(8,128)(2,1)}, u32[]{:S(2)}) %copy-start.6) | copy-done | bytes 1048600
  5.5 0.0 copy-start.8
  5.5 0.7 %copy-done.8 = s32[3,4]{1,0:T(4,128)S(1)} copy-done((s32[3,4]{1,0:T(4,128)S(1)}, s32[3,4]{1,0:T(4,128)}, u32[]{:S(2)}) %copy-start.8) | copy-done | bytes 72
  6.2 3.5 %local_sums.2 = (f32[4,128,128]{2,1,0:T(8,128)S(1)}, f32[4,128,128]{2,1,0:T(8,128)S(1)}) custom-call(s32[3,4]{1,0:T(4,128)S(1)} %copy-done.8, s32[1]{0:T(128)} %bitcast.place, bf16[512,1024]{1,0:T(8,128)(2,1)S(1)} %copy-done, bf16[512,1024]{1,0:T(8,128)(2,1)S(1)} %copy-done.2, bf16[512,1024]{1,0:T(8,128)(2,1)S(1)} %copy-done.4, bf16[512,1024]{1,0:T(8,128)(2,1)S(1)} %copy-done.6), custom_call_target="tpu_custom_call" | custom-call | flops 134217728 | bytes 2097152 | tf_op jit(solution)/shard_map/local_sums/pallas_call | solution.py:276
  9.7 3.1 %collective-permute-start.3 = (f32[4,128,128]{2,1,0:T(8,128)S(1)}, f32[4,128,128]{2,1,0:T(8,128)S(1)}, u32[]{:S(2)}, u32[]{:S(2)}) collective-permute-start(f32[4,128,128]{2,1,0:T(8,128)S(1)} %get-tuple-element.25), channel_id=1, source_target_pairs={{0,4},{4,0},{8,12},{12,8},{1,5},{5,1},{9,13},{13,9},{2,6},{6,2},{1... | collective-permute-start | bytes 786440 | tf_op jit(solution)/shard_map/ppermute | solution.py:482
  12.8 0.1 collective-permute-start
  12.8 0.0 copy-start.7
  12.8 5.3 %local_sums.3 = (f32[4,128,128]{2,1,0:T(8,128)S(1)}, f32[4,128,128]{2,1,0:T(8,128)S(1)}, f32[4,128,128]{2,1,0:T(8,128)S(1)}, f32[4,128,128]{2,1,0:T(8,128)S(1)}) custom-call(s32[3,4]{1,0:T(4,128)S(1)} %copy-done.8, s32[1]{0:T(128)} %bitcast.place, bf16[512,1024]{1,0:T(8,128)(2,1)S(1)} %copy-done, bf16[512,1024]{1,0:T(8,128)(2,1)S(1)} %copy-done.2, ...), custom_call_target="tpu_custom_call" | custom-call | flops 268435456 | bytes 2097152 | tf_op jit(solution)/shard_map/local_sums/pallas_call | solution.py:276
  18.2 0.0 copy-start.1
  18.2 0.0 copy-start.3
  18.2 0.0 copy-start.5
  18.2 0.0 copy-start.9
  18.2 1.7 %collective-permute-done.3.got_ref.refs_8_ = f32[4,128,128]{2,1,0:T(8,128)S(1)} collective-permute-done((f32[4,128,128]{2,1,0:T(8,128)S(1)}, f32[4,128,128]{2,1,0:T(8,128)S(1)}, u32[]{:S(2)}, u32[]{:S(2)}) %collective-permute-start.3) | collective-permute-done | bytes 262176 | tf_op jit(solution)/shard_map/ppermute | solution.py:482
  19.9 0.6 join.6
  20.5 4.2 %collective-permute-start.4 = (f32[4,128,128]{2,1,0:T(8,128)S(1)}, f32[4,128,128]{2,1,0:T(8,128)S(1)}, u32[]{:S(2)}, u32[]{:S(2)}) collective-permute-start(f32[4,128,128]{2,1,0:T(8,128)S(1)} %join.6), channel_id=1, source_target_pairs={{0,12},{4,8},{8,4},{12,0},{1,13},{5,9},{9,5},{13,1},{2,14},{6,10},... | collective-permute-start | bytes 786440 | tf_op jit(solution)/shard_map/ppermute | solution.py:482
  24.7 0.4 collective-permute-done.got_ref.refs_8_
  25.1 0.6 join.4
  25.7 11.9 %collective-permute-start.1 = (f32[4,128,128]{2,1,0:T(8,128)S(1)}, f32[4,128,128]{2,1,0:T(8,128)S(1)}, u32[]{:S(2)}, u32[]{:S(2)}) collective-permute-start(f32[4,128,128]{2,1,0:T(8,128)S(1)} %join.4), channel_id=1, source_target_pairs={{0,12},{4,8},{8,4},{12,0},{1,13},{5,9},{9,5},{13,1},{2,14},{6,10},... | collective-permute-start | bytes 786440 | tf_op jit(solution)/shard_map/ppermute | solution.py:482
  37.6 0.0 collective-permute-done.4.got_ref.refs_9_
  37.6 0.6 join.7
  38.2 1.4 %collective-permute-start.5 = (f32[4,128,128]{2,1,0:T(8,128)S(1)}, f32[4,128,128]{2,1,0:T(8,128)S(1)}, u32[]{:S(2)}, u32[]{:S(2)}) collective-permute-start(f32[4,128,128]{2,1,0:T(8,128)S(1)} %join.7), channel_id=1, source_target_pairs={{0,4},{4,0},{8,12},{12,8},{1,5},{5,1},{9,13},{13,9},{2,6},{6,2},{1... | collective-permute-start | bytes 786440 | tf_op jit(solution)/shard_map/ppermute | solution.py:482
  39.6 2.5 %collective-permute-done.1.got_ref.refs_9_ = f32[4,128,128]{2,1,0:T(8,128)S(1)} collective-permute-done((f32[4,128,128]{2,1,0:T(8,128)S(1)}, f32[4,128,128]{2,1,0:T(8,128)S(1)}, u32[]{:S(2)}, u32[]{:S(2)}) %collective-permute-start.1) | collective-permute-done | bytes 262176 | tf_op jit(solution)/shard_map/ppermute | solution.py:482
  42.1 0.6 join.5
  42.7 3.9 %collective-permute-start.2 = (f32[4,128,128]{2,1,0:T(8,128)S(1)}, f32[4,128,128]{2,1,0:T(8,128)S(1)}, u32[]{:S(2)}, u32[]{:S(2)}) collective-permute-start(f32[4,128,128]{2,1,0:T(8,128)S(1)} %join.5), channel_id=1, source_target_pairs={{0,4},{4,0},{8,12},{12,8},{1,5},{5,1},{9,13},{13,9},{2,6},{6,2},{1... | collective-permute-start | bytes 786440 | tf_op jit(solution)/shard_map/ppermute | solution.py:482
  46.6 0.0 copy-done.7
  46.6 0.0 copy-done.1
  46.6 0.0 copy-done.3
  46.6 0.0 copy-done.5
  46.6 0.0 copy-done.9
  46.6 10.1 %inside_products.1 = (f32[512,1024]{1,0:T(8,128)S(1)}, f32[512,1024]{1,0:T(8,128)S(1)}, f32[512,1024]{1,0:T(8,128)S(1)}, f32[512,1024]{1,0:T(8,128)S(1)}) custom-call(s32[3,4]{1,0:T(4,128)S(1)} %copy-done.9, s32[1]{0:T(128)} %bitcast.place, bf16[512,1024]{1,0:T(8,128)(2,1)S(1)} %copy-done.1, bf16[512,1024]{1,0:T(8,128)(2,1)S(1)} %copy-done.3, ...), custom_call_target="tpu_custom_call" | custom-call | flops 2415919104 | bytes 12582912 | tf_op jit(solution)/shard_map/inside_products/pallas_call | solution.py:384
  56.6 0.0 collective-permute-done.5.refs_10_
  56.7 4.5 %final_products.2 = (bf16[512,1024]{1,0:T(8,128)(2,1)}, bf16[512,1024]{1,0:T(8,128)(2,1)}, bf16[512,1024]{1,0:T(8,128)(2,1)}, bf16[512,1024]{1,0:T(8,128)(2,1)}) custom-call(s32[3,4]{1,0:T(4,128)S(1)} %copy-done.9, s32[1]{0:T(128)} %bitcast.place, bf16[512,1024]{1,0:T(8,128)(2,1)S(1)} %copy-done.1, bf16[512,1024]{1,0:T(8,128)(2,1)S(1)} %copy-done.3, ...), custom_call_target="tpu_custom_call" | custom-call | flops 268435456 | bytes 8388608 | tf_op jit(solution)/shard_map/final_products/pallas_call | solution.py:448
  61.2 0.0 collective-permute-done.2.refs_10_
  61.2 4.5 %final_products.3 = (bf16[512,1024]{1,0:T(8,128)(2,1)}, bf16[512,1024]{1,0:T(8,128)(2,1)}, bf16[512,1024]{1,0:T(8,128)(2,1)}, bf16[512,1024]{1,0:T(8,128)(2,1)}) custom-call(s32[3,4]{1,0:T(4,128)S(1)} %copy-done.9, s32[1]{0:T(128)} %bitcast.place, ...), custom_call_target="tpu_custom_call", output_to_operand_aliasing={{0}: (13, {}), {1}: (14, {}), {2}: (15, {}), {3}: (16, {})} | custom-call | flops 268435456 | bytes 8388608 | tf_op jit(solution)/shard_map/final_products/pallas_call | solution.py:448
Async XLA Ops:
  0.6 1.2 %copy-start = (bf16[512,1024]{1,0:T(8,128)(2,1)S(1)}, bf16[512,1024]{1,0:T(8,128)(2,1)}, u32[]{:S(2)}) copy-start(bf16[512,1024]{1,0:T(8,128)(2,1)} %refs_0_.3) | copy-start | bytes 3145732
  1.9 1.2 %copy-start.2 = (bf16[512,1024]{1,0:T(8,128)(2,1)S(1)}, bf16[512,1024]{1,0:T(8,128)(2,1)}, u32[]{:S(2)}) copy-start(bf16[512,1024]{1,0:T(8,128)(2,1)} %refs_1_.3) | copy-start | bytes 3145732
  3.1 1.2 %copy-start.4 = (bf16[512,1024]{1,0:T(8,128)(2,1)S(1)}, bf16[512,1024]{1,0:T(8,128)(2,1)}, u32[]{:S(2)}) copy-start(bf16[512,1024]{1,0:T(8,128)(2,1)} %refs_2_.3) | copy-start | bytes 3145732
  4.3 1.2 %copy-start.6 = (bf16[512,1024]{1,0:T(8,128)(2,1)S(1)}, bf16[512,1024]{1,0:T(8,128)(2,1)}, u32[]{:S(2)}) copy-start(bf16[512,1024]{1,0:T(8,128)(2,1)} %refs_3_.3) | copy-start | bytes 3145732
  5.5 0.7 %copy-start.8 = (s32[3,4]{1,0:T(4,128)S(1)}, s32[3,4]{1,0:T(4,128)}, u32[]{:S(2)}) copy-start(s32[3,4]{1,0:T(4,128)} %pack.17) | copy-start | bytes 148
  9.7 10.2 %collective-permute-start.3 = (f32[4,128,128]{2,1,0:T(8,128)S(1)}, f32[4,128,128]{2,1,0:T(8,128)S(1)}, u32[]{:S(2)}, u32[]{:S(2)}) collective-permute-start(f32[4,128,128]{2,1,0:T(8,128)S(1)} %get-tuple-element.25), channel_id=1, source_target_pairs={{0,4},{4,0},{8,12},{12,8},{1,5},{5,1},{9,13},{13,9},{2,6},{6,2},{1... | collective-permute-start | bytes 786440 | tf_op jit(solution)/shard_map/ppermute | solution.py:482
  12.8 12.3 %collective-permute-start = (f32[4,128,128]{2,1,0:T(8,128)S(1)}, f32[4,128,128]{2,1,0:T(8,128)S(1)}, u32[]{:S(2)}, u32[]{:S(2)}) collective-permute-start(f32[4,128,128]{2,1,0:T(8,128)S(1)} %get-tuple-element.22), channel_id=1, source_target_pairs={{0,4},{4,0},{8,12},{12,8},{1,5},{5,1},{9,13},{13,9},{2,6},{6,2},{1... | collective-permute-start | bytes 786440 | tf_op jit(solution)/shard_map/ppermute | solution.py:482
  12.8 33.7 %copy-start.7 = (bf16[512,1024]{1,0:T(8,128)(2,1)S(1)}, bf16[512,1024]{1,0:T(8,128)(2,1)}, u32[]{:S(2)}) copy-start(bf16[512,1024]{1,0:T(8,128)(2,1)} %refs_3_.3) | copy-start | bytes 3145732
  18.2 28.4 %copy-start.1 = (bf16[512,1024]{1,0:T(8,128)(2,1)S(1)}, bf16[512,1024]{1,0:T(8,128)(2,1)}, u32[]{:S(2)}) copy-start(bf16[512,1024]{1,0:T(8,128)(2,1)} %refs_0_.3) | copy-start | bytes 3145732
  18.2 28.4 %copy-start.3 = (bf16[512,1024]{1,0:T(8,128)(2,1)S(1)}, bf16[512,1024]{1,0:T(8,128)(2,1)}, u32[]{:S(2)}) copy-start(bf16[512,1024]{1,0:T(8,128)(2,1)} %refs_1_.3) | copy-start | bytes 3145732
  18.2 28.4 %copy-start.5 = (bf16[512,1024]{1,0:T(8,128)(2,1)S(1)}, bf16[512,1024]{1,0:T(8,128)(2,1)}, u32[]{:S(2)}) copy-start(bf16[512,1024]{1,0:T(8,128)(2,1)} %refs_2_.3) | copy-start | bytes 3145732
  18.2 28.3 %copy-start.9 = (s32[3,4]{1,0:T(4,128)S(1)}, s32[3,4]{1,0:T(4,128)}, u32[]{:S(2)}) copy-start(s32[3,4]{1,0:T(4,128)} %pack.17) | copy-start | bytes 148
  20.5 17.1 %collective-permute-start.4 = (f32[4,128,128]{2,1,0:T(8,128)S(1)}, f32[4,128,128]{2,1,0:T(8,128)S(1)}, u32[]{:S(2)}, u32[]{:S(2)}) collective-permute-start(f32[4,128,128]{2,1,0:T(8,128)S(1)} %join.6), channel_id=1, source_target_pairs={{0,12},{4,8},{8,4},{12,0},{1,13},{5,9},{9,5},{13,1},{2,14},{6,10},... | collective-permute-start | bytes 786440 | tf_op jit(solution)/shard_map/ppermute | solution.py:482
  25.7 16.3 %collective-permute-start.1 = (f32[4,128,128]{2,1,0:T(8,128)S(1)}, f32[4,128,128]{2,1,0:T(8,128)S(1)}, u32[]{:S(2)}, u32[]{:S(2)}) collective-permute-start(f32[4,128,128]{2,1,0:T(8,128)S(1)} %join.4), channel_id=1, source_target_pairs={{0,12},{4,8},{8,4},{12,0},{1,13},{5,9},{9,5},{13,1},{2,14},{6,10},... | collective-permute-start | bytes 786440 | tf_op jit(solution)/shard_map/ppermute | solution.py:482
  38.2 18.4 %collective-permute-start.5 = (f32[4,128,128]{2,1,0:T(8,128)S(1)}, f32[4,128,128]{2,1,0:T(8,128)S(1)}, u32[]{:S(2)}, u32[]{:S(2)}) collective-permute-start(f32[4,128,128]{2,1,0:T(8,128)S(1)} %join.7), channel_id=1, source_target_pairs={{0,4},{4,0},{8,12},{12,8},{1,5},{5,1},{9,13},{13,9},{2,6},{6,2},{1... | collective-permute-start | bytes 786440 | tf_op jit(solution)/shard_map/ppermute | solution.py:482
  42.7 18.5 %collective-permute-start.2 = (f32[4,128,128]{2,1,0:T(8,128)S(1)}, f32[4,128,128]{2,1,0:T(8,128)S(1)}, u32[]{:S(2)}, u32[]{:S(2)}) collective-permute-start(f32[4,128,128]{2,1,0:T(8,128)S(1)} %join.5), channel_id=1, source_target_pairs={{0,4},{4,0},{8,12},{12,8},{1,5},{5,1},{9,13},{13,9},{2,6},{6,2},{1... | collective-permute-start | bytes 786440 | tf_op jit(solution)/shard_map/ppermute | solution.py:482

commit v2 on v1

--- a/solution.py
+++ b/solution.py
@@ -11,9 +11,16 @@
 BLK = 128
 GROUP = 512
 NB = GROUP // BLK
-CHUNKS = 2
+SIZES = (4, 4)
+ORDER = (("two", 0), ("two", 1), ("in", 0), ("three", 0), ("three", 1), ("end", 0), ("end", 1))
+HELD = jnp.bfloat16
 F32 = jnp.float32
 BF16 = jnp.bfloat16
+MIB = 2**20
+SUMS_LIMIT = 60 * MIB
+JOIN_LIMIT = 4 * MIB
+IN_LIMIT = 16 * MIB
+END_LIMIT = 16 * MIB
 
 
 def flag(condition):
@@ -175,15 +182,16 @@
     return forward, backward
 
 
-def block_rows(value_of, like):
-    return jnp.concatenate([jnp.full((BLK, like), value_of(b), F32) for b in range(NB)], axis=0)
-
-
-def fill_scale(pack, d, blocks, scale_ref, sign_ref):
-    seg, _, _ = edges(pack, blocks)
+SMEM = pl.BlockSpec(memory_space=pltpu.SMEM)
+ANY = pl.BlockSpec(memory_space=pl.ANY)
+VMEM = pl.BlockSpec(memory_space=pltpu.VMEM)
+
+
+def fill_scale(pack, d, scale_ref, sign_ref):
+    seg, _, _ = edges(pack, NB)
     prompt = pack[0, 1] - pack[0, 0]
     for b in range(NB):
-        block = d * blocks + b
+        block = d * NB + b
         s = seg(block)
         start = pick(s, [pack[0, 0], pack[1, 0], pack[2, 0]])
         role = pick(s, [pack[0, 3], pack[1, 3], pack[2, 3]])
@@ -193,12 +201,11 @@
         rows = pl.ds(b * BLK, BLK)
         if scale_ref is not None:
             scale_ref[rows, :] = scale
-        if sign_ref is not None:
-            sign_ref[rows, :] = jnp.where(role == 2, -1.0, 1.0) * scale
-
-
-def weighted(grad, sign_ref):
-    return (grad.astype(F32) * sign_ref[...]).astype(BF16)
+        sign_ref[rows, :] = jnp.where(role == 2, -1.0, 1.0) * scale
+
+
+def weighted(rows, weight):
+    return (rows.astype(F32) * weight).astype(BF16)
 
 
 def contract_rows(a, b):
@@ -213,95 +220,84 @@
     return lax.dot_general(a, b, (((1,), (0,)), ((), ())), preferred_element_type=F32)
 
 
-def row_mask(pack, d, blocks, coefs):
-    seg, _, _ = edges(pack, blocks)
-    return block_rows(lambda b: pick(seg(d * blocks + b), coefs).astype(F32), DH).astype(BF16)
-
-
-def sums_kernel(blocks, per_step, messages, pack, place, q_ref, k_ref, v_ref, g_ref, *refs):
-    outs, sign_ref = refs[:-1], refs[-1]
+def sums_kernel(messages, sizes, pack, place, q_hbm, k_hbm, v_hbm, g_hbm, after, *refs):
+    many, heads = len(messages), sum(sizes)
+    outs = refs[: many * len(sizes)]
+    left, right, weight_ref, sign_ref, sems = refs[many * len(sizes) :]
     d = place[0]
-    step = pl.program_id(0)
-
-    @pl.when(step == 0)
-    def _():
-        fill_scale(pack, d, blocks, None, sign_ref)
-
-    tables = [m(pack, d, blocks)[-4:] for m in messages]
-    masks = [row_mask(pack, d, blocks, t[1:]) for t in tables]
-    per_chunk = pl.num_programs(0) // CHUNKS
-
-    def emit(index, head, value):
-        for c in range(CHUNKS):
-
-            @pl.when(step // per_chunk == c)
+    seg, _, _ = edges(pack, NB)
+    tables = [m(pack, d, NB)[-4:] for m in messages]
+
+    def copies(m, source_left, source_right):
+        out = []
+        for h in range(heads):
+            cols = pl.ds(h * DH, DH)
+            out.append(
+                [
+                    pltpu.make_async_copy(src.at[:, cols], dst.at[m, :, cols], sems.at[m, n, h])
+                    for n, (src, dst) in enumerate(((source_left, left), (source_right, right)))
+                ]
+            )
+        return out
+
+    for m in range(many):
+        for kind, sources in ((1, (k_hbm, v_hbm)), (0, (q_hbm, g_hbm))):
+
+            @pl.when(tables[m][0] == kind)
             def _():
-                outs[index * CHUNKS + c][head] = value
-
-    for head in range(per_step):
-        cols = pl.ds(head * DH, DH)
-        for index, (table, mask) in enumerate(zip(tables, masks)):
-
-            @pl.when(table[0] == 1)
-            def _():
-                emit(index, head, contract_rows(k_ref[:, cols] * mask, v_ref[:, cols]))
-
-            @pl.when(table[0] == 0)
-            def _():
-                grads = weighted(g_ref[:, cols], sign_ref)
-                emit(index, head, contract_rows(q_ref[:, cols] * mask, grads))
-
-
-def local_sums(messages, blocks, pack, place, q, k, v, g):
-    heads = q.shape[1] // DH
-    per_step = 2 if heads % (2 * CHUNKS) == 0 else 1
-    steps = heads // per_step
-    per_chunk = steps // CHUNKS
-
-    def needed(kind):
-        def index(i, pack_ref, place_ref):
-            use = jnp.int32(0)
-            for m in messages:
-                use = either(use, flag(m(pack_ref, place_ref[0], blocks)[-4] == kind))
-            return (0, i * use)
-
-        return index
-
-    def chunk(c):
-        return lambda i, *_: (jnp.clip(i - c * per_chunk, 0, per_chunk - 1), 0, 0)
-
-    rows = q.shape[0]
-    tokens = (rows, per_step * DH)
-    out = jax.ShapeDtypeStruct((heads // CHUNKS, DH, DH), F32)
-    return pl.pallas_call(
-        functools.partial(sums_kernel, blocks, per_step, messages),
-        out_shape=[out] * (CHUNKS * len(messages)),
-        grid_spec=pltpu.PrefetchScalarGridSpec(
-            num_scalar_prefetch=2,
-            grid=(steps,),
-            in_specs=[
-                pl.BlockSpec(tokens, needed(0)),
-                pl.BlockSpec(tokens, needed(1)),
-                pl.BlockSpec(tokens, needed(1)),
-                pl.BlockSpec(tokens, needed(0)),
-            ],
-            out_specs=[
-                pl.BlockSpec((per_step, DH, DH), chunk(c)) for _ in messages for c in range(CHUNKS)
-            ],
-            scratch_shapes=[pltpu.VMEM((rows, DH), F32)],
-        ),
-        compiler_params=pltpu.CompilerParams(vmem_limit_bytes=16 * 2**20),
+                for both in copies(m, *sources):
+                    for copy in both:
+                        copy.start()
+
+    fill_scale(pack, d, None, sign_ref)
+    for m in range(many):
+        forward = tables[m][0] == 1
+        for b in range(NB):
+            rows = pl.ds(b * BLK, BLK)
+            takes = pick(seg(d * NB + b), tables[m][1:]).astype(F32)
+            weight_ref[m, rows, :] = jnp.where(forward, 1.0, sign_ref[rows, :]) * takes
+    waits = [copies(m, k_hbm, v_hbm) for m in range(many)]
+    for m in range(many):
+        h = 0
+        for c, size in enumerate(sizes):
+            for inner in range(size):
+                for copy in waits[m][h]:
+                    copy.wait()
+                cols = pl.ds(h * DH, DH)
+                rows = weighted(right[m, :, cols], weight_ref[m])
+                outs[m * len(sizes) + c][inner] = contract_rows(left[m, :, cols], rows)
+                h += 1
+
+
+def local_sums(messages, sizes, scalars, tokens, after):
+    rows, heads, many = tokens[0].shape[0], sum(sizes), len(messages)
+    out = pl.pallas_call(
+        functools.partial(sums_kernel, messages, sizes),
+        out_shape=[
+            jax.ShapeDtypeStruct((size, DH, DH), F32) for _ in messages for size in sizes
+        ],
+        in_specs=[SMEM, SMEM] + [ANY] * 5,
+        out_specs=[VMEM] * (many * len(sizes)),
+        scratch_shapes=[
+            pltpu.VMEM((many, rows, heads * DH), BF16),
+            pltpu.VMEM((many, rows, heads * DH), BF16),
+            pltpu.VMEM((many, rows, DH), F32),
+            pltpu.VMEM((rows, DH), F32),
+            pltpu.SemaphoreType.DMA((many, 2, heads)),
+        ],
+        compiler_params=pltpu.CompilerParams(vmem_limit_bytes=SUMS_LIMIT),
         cost_estimate=pl.CostEstimate(
-            flops=2 * rows * DH * DH * heads * len(messages),
-            bytes_accessed=4 * rows * heads * DH,
+            flops=2 * rows * DH * DH * heads * many,
+            bytes_accessed=8 * rows * heads * DH * many,
             transcendentals=0,
         ),
         name="local_sums",
-    )(pack, place, q, k, v, g)
-
-
-def join_kernel(blocks, message, pack, place, got_ref, own_ref, out_ref):
-    keep = message(pack, place[0], blocks)[0] == 1
+    )(*scalars, *tokens, after)
+    return [out[m * len(sizes) : (m + 1) * len(sizes)] for m in range(many)]
+
+
+def join_kernel(message, pack, place, got_ref, own_ref, after, out_ref):
+    keep = message(pack, place[0], NB)[0] == 1
 
     @pl.when(keep)
     def _():
@@ -312,191 +308,192 @@
         out_ref[...] = own_ref[...]
 
 
-def join(message, blocks, pack, place, got, own):
-    heads = got.shape[0]
+def join(message, scalars, got, own, after):
     return pl.pallas_call(
-        functools.partial(join_kernel, blocks, message),
+        functools.partial(join_kernel, message),
         out_shape=jax.ShapeDtypeStruct(got.shape, F32),
-        grid_spec=pltpu.PrefetchScalarGridSpec(
-            num_scalar_prefetch=2,
-            grid=(1,),
-            in_specs=[pl.BlockSpec((heads, DH, DH), lambda i, *_: (0, 0, 0))] * 2,
-            out_specs=pl.BlockSpec((heads, DH, DH), lambda i, *_: (0, 0, 0)),
-        ),
-        compiler_params=pltpu.CompilerParams(vmem_limit_bytes=8 * 2**20),
+        in_specs=[SMEM, SMEM, VMEM, VMEM, ANY],
+        out_specs=VMEM,
+        compiler_params=pltpu.CompilerParams(vmem_limit_bytes=JOIN_LIMIT),
         cost_estimate=pl.CostEstimate(
             flops=got.size, bytes_accessed=12 * got.size, transcendentals=0
         ),
         name="join",
-    )(pack, place, got, own)
-
-
-def inside_kernel(blocks, pack, place, q_ref, k_ref, v_ref, g_ref, o1, o2, o3, o4, mask_ref, sign_ref):
+    )(*scalars, got, own, after)
+
+
+def inside_kernel(per, pack, place, q_ref, k_ref, v_ref, g_ref, after, o1, o2, o3, o4, mask_ref, sign_ref):
     d = place[0]
     half = GROUP // 2
 
     @pl.when(pl.program_id(0) == 0)
     def _():
-        fill_scale(pack, d, blocks, None, sign_ref)
-        seg, _, _ = edges(pack, blocks)
+        fill_scale(pack, d, None, sign_ref)
+        seg, _, _ = edges(pack, NB)
+        segs = [seg(d * NB + b) for b in range(NB)]
         tri = lax.broadcasted_iota(jnp.int32, (BLK, BLK), 0) >= lax.broadcasted_iota(
             jnp.int32, (BLK, BLK), 1
         )
         for t in range(NB):
             for s in range(NB):
-                seg_t, seg_s = seg(d * blocks + t), seg(d * blocks + s)
-                ok = either(flag(seg_t == seg_s), flag(seg_s == 0)).astype(F32)
                 if s > t:
                     tile = jnp.zeros((BLK, BLK), F32)
                 elif s == t:
                     tile = jnp.where(tri, 1.0, 0.0)
                 else:
-                    tile = jnp.full((BLK, BLK), ok, F32)
+                    sees = either(flag(segs[t] == segs[s]), flag(segs[s] == 0))
+                    tile = jnp.full((BLK, BLK), sees.astype(F32))
                 mask_ref[pl.ds(t * BLK, BLK), pl.ds(s * BLK, BLK)] = tile.astype(BF16)
 
-    q, k, v = q_ref[...], k_ref[...], v_ref[...]
-    g = weighted(g_ref[...], sign_ref)
-    lo, hi = slice(0, half), slice(half, GROUP)
-
-    def masked(a, b, rows, cols):
-        return contract_cols(a[rows], b[cols]).astype(BF16) * mask_ref[rows, cols]
-
-    s_lo = masked(q, k, lo, lo)
-    s_hi = masked(q, k, hi, slice(0, GROUP))
-    o1[lo, :] = plain(s_lo, v[lo])
-    o1[hi, :] = plain(s_hi, v)
-    gv = contract_rows(s_hi, g[hi])
-    o4[lo, :] = gv[lo] + contract_rows(s_lo, g[lo])
-    o4[hi, :] = gv[hi]
-    b_lo = masked(g, v, lo, lo)
-    b_hi = masked(g, v, hi, slice(0, GROUP))
-    o2[lo, :] = plain(b_lo, k[lo])
-    o2[hi, :] = plain(b_hi, k)
-    gk = contract_rows(b_hi, q[hi])
-    o3[lo, :] = gk[lo] + contract_rows(b_lo, q[lo])
-    o3[hi, :] = gk[hi]
-
-
-def inside_products(blocks, pack, place, q, k, v, g):
-    rows, cols = q.shape
-    heads = cols // DH
-    spec = pl.BlockSpec((rows, DH), lambda i, *_: (0, i))
+    lo, hi, whole = slice(0, half), slice(half, GROUP), slice(0, GROUP)
+    for h in range(per):
+        cols = slice(h * DH, (h + 1) * DH)
+        q, k, v = q_ref[:, cols], k_ref[:, cols], v_ref[:, cols]
+        g = weighted(g_ref[:, cols], sign_ref[...])
+
+        def masked(a, b, rows, keys):
+            return contract_cols(a[rows], b[keys]).astype(BF16) * mask_ref[rows, keys]
+
+        def put(ref, rows, value):
+            ref[rows, cols] = value.astype(ref.dtype)
+
+        s_lo = masked(q, k, lo, lo)
+        s_hi = masked(q, k, hi, whole)
+        put(o1, lo, plain(s_lo, v[lo]))
+        put(o1, hi, plain(s_hi, v))
+        gv = contract_rows(s_hi, g[hi])
+        put(o4, lo, gv[lo] + contract_rows(s_lo, g[lo]))
+        put(o4, hi, gv[hi])
+        b_lo = masked(g, v, lo, lo)
+        b_hi = masked(g, v, hi, whole)
+        put(o2, lo, plain(b_lo, k[lo]))
+        put(o2, hi, plain(b_hi, k))
+        gk = contract_rows(b_hi, q[hi])
+        put(o3, lo, gk[lo] + contract_rows(b_lo, q[lo]))
+        put(o3, hi, gk[hi])
+
+
+def inside_products(scalars, tokens, after):
+    rows, heads = tokens[0].shape[0], tokens[0].shape[1] // DH
+    per = 2 if heads % 2 == 0 else 1
+    spec = pl.BlockSpec((rows, per * DH), lambda i: (0, i))
     return pl.pallas_call(
-        functools.partial(inside_kernel, blocks),
-        out_shape=[jax.ShapeDtypeStruct((rows, cols), F32)] * 4,
-        grid_spec=pltpu.PrefetchScalarGridSpec(
-            num_scalar_prefetch=2,
-            grid=(heads,),
-            in_specs=[spec] * 4,
-            out_specs=[spec] * 4,
-            scratch_shapes=[pltpu.VMEM((rows, rows), BF16), pltpu.VMEM((rows, DH), F32)],
-        ),
-        compiler_params=pltpu.CompilerParams(vmem_limit_bytes=24 * 2**20),
+        functools.partial(inside_kernel, per),
+        out_shape=[jax.ShapeDtypeStruct((rows, heads * DH), HELD)] * 4,
+        grid=(heads // per,),
+        in_specs=[SMEM, SMEM] + [spec] * 4 + [ANY],
+        out_specs=[spec] * 4,
+        scratch_shapes=[pltpu.VMEM((rows, rows), BF16), pltpu.VMEM((rows, DH), F32)],
+        compiler_params=pltpu.CompilerParams(vmem_limit_bytes=IN_LIMIT),
         cost_estimate=pl.CostEstimate(
             flops=9 * rows * rows * DH * heads,
-            bytes_accessed=24 * rows * cols,
+            bytes_accessed=16 * rows * heads * DH,
             transcendentals=0,
         ),
         name="inside_products",
-    )(pack, place, q, k, v, g)
-
-
-def final_kernel(blocks, first, pack, place, *refs):
+    )(*scalars, *tokens, after)
+
+
+def final_kernel(per, pack, place, *refs):
     q_ref, k_ref, v_ref, g_ref, i1, i2, i3, i4, r1, r2, r3 = refs[:11]
     o1, o2, o3, o4, scale_ref, sign_ref, st_ref, bk_ref = refs[-8:]
     d = place[0]
 
     @pl.when(pl.program_id(0) == 0)
     def _():
-        fill_scale(pack, d, blocks, scale_ref, sign_ref)
-
-    seg, _, _ = edges(pack, blocks)
-    forward, backward = state_table(pack, d, blocks)
-    got = [r1[0], r2[0], r3[0]]
-    for x in range(3):
-        for table, out in ((forward, st_ref), (backward, bk_ref)):
-            total = None
-            for weight, part in zip(table[x], got):
-                term = weight.astype(F32) * part
-                total = term if total is None else total + term
-            out[x] = total.astype(BF16)
-    for b in range(NB):
-        rows = pl.ds(b * BLK, BLK)
-        s = seg(d * blocks + b)
-        st, bk = st_ref[s], bk_ref[s]
-        q, k, v = q_ref[rows, :], k_ref[rows, :], v_ref[rows, :]
-        g = (g_ref[rows, :].astype(F32) * sign_ref[rows, :]).astype(BF16)
-        o1[rows, :] = (scale_ref[rows, :] * (i1[rows, :] + plain(q, st))).astype(BF16)
-        o2[rows, :] = (i2[rows, :] + contract_cols(g, st)).astype(BF16)
-        o3[rows, :] = (i3[rows, :] + contract_cols(v, bk)).astype(BF16)
-        o4[rows, :] = (i4[rows, :] + plain(k, bk)).astype(BF16)
-
-
-def final_products(blocks, chunk, pack, place, tokens, inside, got, before):
+        fill_scale(pack, d, scale_ref, sign_ref)
+
+    seg, _, _ = edges(pack, NB)
+    forward, backward = state_table(pack, d, NB)
+    for h in range(per):
+        cols = slice(h * DH, (h + 1) * DH)
+        got = [r1[h], r2[h], r3[h]]
+        for x in range(3):
+            for table, out in ((forward, st_ref), (backward, bk_ref)):
+                total = None
+                for weight, part in zip(table[x], got):
+                    term = weight.astype(F32) * part
+                    total = term if total is None else total + term
+                out[x] = total.astype(BF16)
+        for b in range(NB):
+            rows = pl.ds(b * BLK, BLK)
+            s = seg(d * NB + b)
+            st, bk = st_ref[s], bk_ref[s]
+            q, k, v = q_ref[rows, cols], k_ref[rows, cols], v_ref[rows, cols]
+            g = weighted(g_ref[rows, cols], sign_ref[rows, :])
+
+            def put(ref, held, value, scale=None):
+                total = held[rows, cols].astype(F32) + value
+                ref[rows, cols] = (total if scale is None else scale * total).astype(BF16)
+
+            put(o1, i1, plain(q, st), scale_ref[rows, :])
+            put(o2, i2, contract_cols(g, st))
+            put(o3, i3, contract_cols(v, bk))
+            put(o4, i4, plain(k, bk))
+
+
+def final_products(first, heads, scalars, tokens, inside, got, before):
     rows, cols = tokens[0].shape
-    heads = cols // DH // CHUNKS
-    first = chunk * heads
-    spec = pl.BlockSpec((rows, DH), lambda i, *_: (0, first + i))
-    state = pl.BlockSpec((1, DH, DH), lambda i, *_: (i, 0, 0))
-    operands = [*tokens, *inside, *got]
-    specs = [spec] * 8 + [state] * 3
+    per = 2 if first % 2 == 0 and heads % 2 == 0 else 1
+    spec = pl.BlockSpec((rows, per * DH), lambda i: (0, first // per + i))
+    state = pl.BlockSpec((per, DH, DH), lambda i: (i, 0, 0))
+    operands = [*scalars, *tokens, *inside, *got]
+    specs = [SMEM, SMEM] + [spec] * 8 + [state] * 3
     aliases = {}
     if before is not None:
-        aliases = {2 + len(operands) + n: n for n in range(4)}
+        aliases = {len(operands) + n: n for n in range(4)}
         operands += list(before)
-        specs += [pl.BlockSpec(memory_space=pl.ANY)] * 4
+        specs += [ANY] * 4
     return pl.pallas_call(
-        functools.partial(final_kernel, blocks, first),
+        functools.partial(final_kernel, per),
         out_shape=[jax.ShapeDtypeStruct((rows, cols), BF16)] * 4,
-        grid_spec=pltpu.PrefetchScalarGridSpec(
-            num_scalar_prefetch=2,
-            grid=(heads,),
-            in_specs=specs,
-            out_specs=[spec] * 4,
-            scratch_shapes=[
-                pltpu.VMEM((rows, DH), F32),
-                pltpu.VMEM((rows, DH), F32),
-                pltpu.VMEM((3, DH, DH), BF16),
-                pltpu.VMEM((3, DH, DH), BF16),
-            ],
-        ),
+        grid=(heads // per,),
+        in_specs=specs,
+        out_specs=[spec] * 4,
+        scratch_shapes=[
+            pltpu.VMEM((rows, DH), F32),
+            pltpu.VMEM((rows, DH), F32),
+            pltpu.VMEM((3, DH, DH), BF16),
+            pltpu.VMEM((3, DH, DH), BF16),
+        ],
         input_output_aliases=aliases,
-        compiler_params=pltpu.CompilerParams(vmem_limit_bytes=16 * 2**20),
+        compiler_params=pltpu.CompilerParams(vmem_limit_bytes=END_LIMIT),
         cost_estimate=pl.CostEstimate(
             flops=8 * rows * DH * DH * heads,
-            bytes_accessed=32 * rows * DH * heads,
+            bytes_accessed=28 * rows * DH * heads,
             transcendentals=0,
         ),
         name="final_products",
-    )(pack, place, *operands)
+    )(*operands)
 
 
 def exchange_body(queries, key_rows, value_rows, grad_out, packing):
-    blocks = queries.shape[0] // BLK
     place = lax.axis_index("seq").astype(jnp.int32).reshape(1)
+    scalars = (packing, place)
     tokens = (queries, key_rows, value_rows, grad_out)
+    starts = [sum(SIZES[:c]) for c in range(len(SIZES))]
     near = [(i, i ^ 1) for i in range(4)]
     across = [(i, 3 - i) for i in range(4)]
 
-    def send(values, pairs):
-        return [lax.ppermute(value, "seq", pairs) for value in values]
-
-    sent = local_sums((message_one,), blocks, packing, place, *tokens)
-    one = send(sent, near)
-    own = local_sums((message_two, message_three), blocks, packing, place, *tokens)
-    own_two, own_three = own[:CHUNKS], own[CHUNKS:]
-    inside = inside_products(blocks, packing, place, *tokens)
-    two = send(
-        [join(message_two, blocks, packing, place, a, b) for a, b in zip(one, own_two)], across
-    )
-    three = send(
-        [join(message_three, blocks, packing, place, a, b) for a, b in zip(two, own_three)], near
-    )
+    (early,) = local_sums((message_one,), SIZES, scalars, tokens, packing)
+    one = [lax.ppermute(value, "seq", near) for value in early]
+    own_two, own_three = local_sums((message_two, message_three), SIZES, scalars, tokens, early[0])
+    last = own_two[0]
+    two, three = [None] * len(SIZES), [None] * len(SIZES)
     out = None
-    for c in range(CHUNKS):
-        out = final_products(
-            blocks, c, packing, place, tokens, inside, (one[c], two[c], three[c]), out
-        )
+    for what, c in ORDER:
+        if what == "two":
+            last = join(message_two, scalars, one[c], own_two[c], last)
+            two[c] = lax.ppermute(last, "seq", across)
+        elif what == "three":
+            last = join(message_three, scalars, two[c], own_three[c], last)
+            three[c] = lax.ppermute(last, "seq", near)
+        elif what == "in":
+            inside = inside_products(scalars, tokens, last)
+            last = inside[0]
+        else:
+            got = (one[c], two[c], three[c])
+            out = final_products(starts[c], SIZES[c], scalars, tokens, inside, got, out)
     return tuple(out)
 
 
@@ -689,33 +686,20 @@
 
 
 def solution(mesh):
-    placed = (
-        P(("grp", "seq"), "head"),
-        P(("grp", "seq"), "head"),
-        P(("grp", "seq"), "head"),
-        P(("grp", "seq"), "head"),
-        P("grp", None),
-    )
-    pairs_of = lambda packing: packing.shape[0] // mesh.shape["grp"] // 3
+    tokens = P(("grp", "seq"), "head")
 
     def program(queries, key_rows, value_rows, grad_out, packing):
-        small = mesh.shape["seq"] == 4 and pairs_of(packing) == 1
         rows = queries.shape[0] // mesh.shape["grp"] // mesh.shape["seq"]
-        fits = rows == GROUP and queries.shape[1] // mesh.shape["head"] % (CHUNKS * DH) == 0
-        return placed_call(exchange_body if small and fits else body)(
-            queries, key_rows, value_rows, grad_out, packing
-        )
-
-    placed_call = lambda one: jax.shard_map(
-        one,
-        mesh=mesh,
-        in_specs=placed,
-        out_specs=(
-            P(("grp", "seq"), "head"),
-            P(("grp", "seq"), "head"),
-            P(("grp", "seq"), "head"),
-            P(("grp", "seq"), "head"),
-        ),
-        check_vma=False,
-    )
+        heads = queries.shape[1] // mesh.shape["head"] // DH
+        pairs = packing.shape[0] // mesh.shape["grp"] // 3
+        four = mesh.shape["seq"] == 4 and pairs == 1
+        fits = rows == GROUP and heads == sum(SIZES)
+        return jax.shard_map(
+            exchange_body if four and fits else body,
+            mesh=mesh,
+            in_specs=(tokens,) * 4 + (P("grp", None),),
+            out_specs=(tokens,) * 4,
+            check_vma=False,
+        )(queries, key_rows, value_rows, grad_out, packing)
+
     return program

time: 66 us -> 53.6 us (0.81)
  starting transfers between devices: 24.4 us -> 18.7 us
  local copies, waits for them, and re-layouts: 5.6 us -> 1.93 us
  Pallas kernels: 30.4 us -> 28.7 us
  waiting for transfers between devices: 4.57 us -> 3.36 us
    ppermute x6, starting transfers between devices: 24.4 us -> 18.7 us  [the longest x2 8.4 us: exchange_body(): three[c] = lax.ppermute(last, 'seq', near)]
    unnamed x20 -> x18, local copies, waits for them, and re-layouts: 5.6 us -> 1.93 us
    pallas_call x9, Pallas kernels: 30.4 us -> 28.7 us  [the longest x2 11.4 us: local_sums(): pl.pallas_call(functools.partial(sums_kernel, messages, sizes), out_shape...]
    ppermute x6, waiting for transfers between devices: 4.57 us -> 3.36 us  [the longest x2 2.91 us: exchange_body(): three[c] = lax.ppermute(last, 'seq', near)]
  transfers between devices with their start and end apart: 6 -> 6, of which waited for: 3 -> 3; matrix products, arithmetic and copies ran while one was open for 0% -> 0% of each run, Pallas kernels for 34% -> 39%
where the time goes in v2:
time: 53.6 us; the launch traced here: 53.4 us
  Pallas kernels  28.7 us (54%)
  starting transfers between devices  18.7 us (35%)
  waiting for transfers between devices  3.36 us (6%)
  local copies, waits for them, and re-layouts  1.93 us (4%)
  between operations  0.74 us (1%)
    pallas_call x2, Pallas kernels, local_sums(): pl.pallas_call(functools.partial(sums_kernel, messages, sizes), out_shape...  11.4 us
    ppermute x2, starting transfers between devices, exchange_body(): three[c] = lax.ppermute(last, 'seq', near)  8.4 us
    pallas_call x1, Pallas kernels, inside_products(): pl.pallas_call(functools.partial(inside_kernel, per), out_shape=[jax.Shap...  8.25 us
    ppermute x2, starting transfers between devices, exchange_body(): two[c] = lax.ppermute(last, 'seq', across)  7.09 us
    pallas_call x2, Pallas kernels, final_products(): pl.pallas_call(functools.partial(final_kernel, per), out_shape=[jax.Shape...  6.66 us
    ppermute x2, starting transfers between devices, exchange_body(): one = [lax.ppermute(value, 'seq', near) for value in early]  3.17 us
    ppermute x2, waiting for transfers between devices, exchange_body(): three[c] = lax.ppermute(last, 'seq', near)  2.91 us
    pallas_call x4, Pallas kernels, join(): pl.pallas_call(functools.partial(join_kernel, message), out_shape=jax.Sha...  2.45 us
  transfers between devices with their start and end apart: 6, of which 3 were waited for; matrix products, arithmetic and copies ran while one was open for 0% of the time, Pallas kernels for 39%

profile of v2, /device:TPU:0, one launch (start us, length us, event | category | flops | bytes accessed | tf_op | source)
XLA Modules:
  0.0 53.4 jit_solution(13213328499074954516)
XLA Ops:
  0.6 4.6 %local_sums.2 = (f32[4,128,128]{2,1,0:T(8,128)}, f32[4,128,128]{2,1,0:T(8,128)}) custom-call(s32[3,4]{1,0:T(4,128)} %pack.17, s32[1]{0:T(128)} %bitcast.place, bf16[512,1024]{1,0:T(8,128)(2,1)} %refs_0_.3, bf16[512,1024]{1,0:T(8,128)(2,1)} %refs_1_.3, bf16[512,1024]{1,0:T(8,128)(2,1)} %refs_2_.3, bf16[512,1024]{1,0:T(8,128)(2,1)} %refs_3_.3, s32[3,4]{1,0:T(4,128)} %pack.17), custom_call_target="tpu_custom_call" | custom-call | flops 134217728 | bytes 4194304 | tf_op jit(solution)/shard_map/local_sums/pallas_call | solution.py:274
  5.2 3.1 %collective-permute-start.1 = (f32[4,128,128]{2,1,0:T(8,128)}, f32[4,128,128]{2,1,0:T(8,128)S(1)}, u32[]{:S(2)}, u32[]{:S(2)}) collective-permute-start(f32[4,128,128]{2,1,0:T(8,128)} %get-tuple-element.19.after), channel_id=1, source_target_pairs={{0,4},{4,0},{8,12},{12,8},{1,5},{5,1},{9,13},{13,9},{2,6},{6,2},{1... | collective-permute-start | bytes 786440 | tf_op jit(solution)/shard_map/ppermute | solution.py:479
  8.3 0.1 collective-permute-start
  8.4 0.0 copy-start.8
  8.4 0.0 copy-start.2
  8.4 0.0 copy-start.3
  8.4 6.8 %local_sums.3 = (f32[4,128,128]{2,1,0:T(8,128)}, f32[4,128,128]{2,1,0:T(8,128)}, f32[4,128,128]{2,1,0:T(8,128)}, f32[4,128,128]{2,1,0:T(8,128)}) custom-call(s32[3,4]{1,0:T(4,128)} %pack.17, s32[1]{0:T(128)} %bitcast.place, bf16[512,1024]{1,0:T(8,128)(2,1)} %refs_0_.3, bf16[512,1024]{1,0:T(8,128)(2,1)} %refs_1_.3, bf16[512,1024]{1,0:T(8,128)(2,1)} %refs_2_.3, ...), custom_call_target="tpu_custom_call" | custom-call | flops 268435456 | bytes 8388608 | tf_op jit(solution)/shard_map/local_sums/pallas_call | solution.py:274
  15.2 0.4 collective-permute-done.1.got_ref.refs_8_
  15.6 0.0 copy-done.8
  15.6 0.0 copy-start.4
  15.6 0.9 %copy-done.4 = f32[4,128,128]{2,1,0:T(8,128)S(1)} copy-done((f32[4,128,128]{2,1,0:T(8,128)S(1)}, f32[4,128,128]{2,1,0:T(8,128)}, u32[]{:S(2)}) %copy-start.4) | copy-done | bytes 262168
  16.6 0.0 copy-start
  16.6 0.0 copy-start.1
  16.6 0.6 %join.4.after = f32[4,128,128]{2,1,0:T(8,128)S(1)} custom-call(s32[3,4]{1,0:T(4,128)S(1)} %copy-done.8, s32[1]{0:T(128)} %bitcast.place, f32[4,128,128]{2,1,0:T(8,128)S(1)} %collective-permute-done.1.got_ref.refs_8_, f32[4,128,128]{2,1,0:T(8,128)S(1)} %copy-done.4, f32[4,128,128]{2,1,0:T(8,128)S(1)} %copy-done.4), custom_call_target="tpu_custom_call" | custom-call | flops 65536 | bytes 786432 | tf_op jit(solution)/shard_map/join/pallas_call | solution.py:312
  17.2 4.2 %collective-permute-start.3 = (f32[4,128,128]{2,1,0:T(8,128)S(1)}, f32[4,128,128]{2,1,0:T(8,128)S(1)}, u32[]{:S(2)}, u32[]{:S(2)}) collective-permute-start(f32[4,128,128]{2,1,0:T(8,128)S(1)} %join.4.after), channel_id=1, source_target_pairs={{0,12},{4,8},{8,4},{12,0},{1,13},{5,9},{9,5},{13,1},{2,14},{6,10},... | collective-permute-start | bytes 786440 | tf_op jit(solution)/shard_map/ppermute | solution.py:487
  21.4 0.0 collective-permute-done.got_ref.refs_8_
  21.4 0.0 copy-start.7
  21.4 0.9 %copy-done.7 = f32[4,128,128]{2,1,0:T(8,128)S(1)} copy-done((f32[4,128,128]{2,1,0:T(8,128)S(1)}, f32[4,128,128]{2,1,0:T(8,128)}, u32[]{:S(2)}) %copy-start.7) | copy-done | bytes 262168
  22.4 0.6 %join.5.after = f32[4,128,128]{2,1,0:T(8,128)S(1)} custom-call(s32[3,4]{1,0:T(4,128)S(1)} %copy-done.8, s32[1]{0:T(128)} %bitcast.place, f32[4,128,128]{2,1,0:T(8,128)S(1)} %collective-permute-done.got_ref.refs_8_, f32[4,128,128]{2,1,0:T(8,128)S(1)} %copy-done.7, f32[4,128,128]{2,1,0:T(8,128)S(1)} %join.4.after), custom_call_target="tpu_custom_call" | custom-call | flops 65536 | bytes 786432 | tf_op jit(solution)/shard_map/join/pallas_call | solution.py:312
  23.0 0.0 copy-start.5
  23.0 2.9 %collective-permute-start.2 = (f32[4,128,128]{2,1,0:T(8,128)S(1)}, f32[4,128,128]{2,1,0:T(8,128)S(1)}, u32[]{:S(2)}, u32[]{:S(2)}) collective-permute-start(f32[4,128,128]{2,1,0:T(8,128)S(1)} %join.5.after), channel_id=1, source_target_pairs={{0,12},{4,8},{8,4},{12,0},{1,13},{5,9},{9,5},{13,1},{2,14},{6,10},... | collective-permute-start | bytes 786440 | tf_op jit(solution)/shard_map/ppermute | solution.py:487
  25.9 0.0 copy-done.2
  25.9 0.0 copy-done.3
  25.9 0.0 copy-done
  25.9 0.0 copy-done.1
  25.9 8.2 %inside_products.1 = (bf16[512,1024]{1,0:T(8,128)(2,1)S(1)}, bf16[512,1024]{1,0:T(8,128)(2,1)S(1)}, bf16[512,1024]{1,0:T(8,128)(2,1)S(1)}, bf16[512,1024]{1,0:T(8,128)(2,1)S(1)}) custom-call(s32[3,4]{1,0:T(4,128)S(1)} %copy-done.8, s32[1]{0:T(128)} %bitcast.place, bf16[512,1024]{1,0:T(8,128)(2,1)S(1)} %copy-done, bf16[512,1024]{1,0:T(8,128)(2,1)S(1)} %copy-done.1, ...), custom_call_target="tpu_custom_call" | custom-call | flops 2415919104 | bytes 8388608 | tf_op jit(solution)/shard_map/inside_products/pallas_call | solution.py:380
  34.2 0.0 collective-permute-done.3.got_ref.refs_9_
  34.2 0.0 copy-done.5
  34.2 0.0 copy-start.6
  34.2 0.6 %join.6.after = f32[4,128,128]{2,1,0:T(8,128)S(1)} custom-call(s32[3,4]{1,0:T(4,128)S(1)} %copy-done.8, s32[1]{0:T(128)} %bitcast.place, f32[4,128,128]{2,1,0:T(8,128)S(1)} %collective-permute-done.3.got_ref.refs_9_, f32[4,128,128]{2,1,0:T(8,128)S(1)} %copy-done.5, bf16[512,1024]{1,0:T(8,128)(2,1)S(1)} %get-tuple-element.22.after.refs_4_), custom_call_target="tpu_custom_call" | custom-call | flops 65536 | bytes 786432 | tf_op jit(solution)/shard_map/join/pallas_call | solution.py:312
  34.8 5.3 %collective-permute-start.5 = (f32[4,128,128]{2,1,0:T(8,128)S(1)}, f32[4,128,128]{2,1,0:T(8,128)S(1)}, u32[]{:S(2)}, u32[]{:S(2)}) collective-permute-start(f32[4,128,128]{2,1,0:T(8,128)S(1)} %join.6.after), channel_id=1, source_target_pairs={{0,4},{4,0},{8,12},{12,8},{1,5},{5,1},{9,13},{13,9},{2,6},{6,2},{1... | collective-permute-start | bytes 786440 | tf_op jit(solution)/shard_map/ppermute | solution.py:490
  40.1 0.0 collective-permute-done.2.got_ref.refs_9_
  40.1 0.0 copy-done.6
  40.1 0.6 %join.7 = f32[4,128,128]{2,1,0:T(8,128)S(1)} custom-call(s32[3,4]{1,0:T(4,128)S(1)} %copy-done.8, s32[1]{0:T(128)} %bitcast.place, f32[4,128,128]{2,1,0:T(8,128)S(1)} %collective-permute-done.2.got_ref.refs_9_, f32[4,128,128]{2,1,0:T(8,128)S(1)} %copy-done.6, f32[4,128,128]{2,1,0:T(8,128)S(1)} %join.6.after), custom_call_target="tpu_custom_call" | custom-call | flops 65536 | bytes 786432 | tf_op jit(solution)/shard_map/join/pallas_call | solution.py:312
  40.7 3.1 %collective-permute-start.4 = (f32[4,128,128]{2,1,0:T(8,128)S(1)}, f32[4,128,128]{2,1,0:T(8,128)S(1)}, u32[]{:S(2)}, u32[]{:S(2)}) collective-permute-start(f32[4,128,128]{2,1,0:T(8,128)S(1)} %join.7), channel_id=1, source_target_pairs={{0,4},{4,0},{8,12},{12,8},{1,5},{5,1},{9,13},{13,9},{2,6},{6,2},{1... | collective-permute-start | bytes 786440 | tf_op jit(solution)/shard_map/ppermute | solution.py:490
  43.8 2.1 %collective-permute-done.5.refs_10_ = f32[4,128,128]{2,1,0:T(8,128)S(1)} collective-permute-done((f32[4,128,128]{2,1,0:T(8,128)S(1)}, f32[4,128,128]{2,1,0:T(8,128)S(1)}, u32[]{:S(2)}, u32[]{:S(2)}) %collective-permute-start.5) | collective-permute-done | bytes 262176 | tf_op jit(solution)/shard_map/ppermute | solution.py:490
  46.0 3.3 %final_products.2 = (bf16[512,1024]{1,0:T(8,128)(2,1)}, bf16[512,1024]{1,0:T(8,128)(2,1)}, bf16[512,1024]{1,0:T(8,128)(2,1)}, bf16[512,1024]{1,0:T(8,128)(2,1)}) custom-call(s32[3,4]{1,0:T(4,128)S(1)} %copy-done.8, s32[1]{0:T(128)} %bitcast.place, bf16[512,1024]{1,0:T(8,128)(2,1)S(1)} %copy-done, bf16[512,1024]{1,0:T(8,128)(2,1)S(1)} %copy-done.1, ...), custom_call_target="tpu_custom_call" | custom-call | flops 268435456 | bytes 7340032 | tf_op jit(solution)/shard_map/final_products/pallas_call | solution.py:447
  49.3 0.8 %collective-permute-done.4.refs_10_ = f32[4,128,128]{2,1,0:T(8,128)S(1)} collective-permute-done((f32[4,128,128]{2,1,0:T(8,128)S(1)}, f32[4,128,128]{2,1,0:T(8,128)S(1)}, u32[]{:S(2)}, u32[]{:S(2)}) %collective-permute-start.4) | collective-permute-done | bytes 262176 | tf_op jit(solution)/shard_map/ppermute | solution.py:490
  50.1 3.3 %final_products.3 = (bf16[512,1024]{1,0:T(8,128)(2,1)}, bf16[512,1024]{1,0:T(8,128)(2,1)}, bf16[512,1024]{1,0:T(8,128)(2,1)}, bf16[512,1024]{1,0:T(8,128)(2,1)}) custom-call(s32[3,4]{1,0:T(4,128)S(1)} %copy-done.8, s32[1]{0:T(128)} %bitcast.place, ...), custom_call_target="tpu_custom_call", output_to_operand_aliasing={{0}: (13, {}), {1}: (14, {}), {2}: (15, {}), {3}: (16, {})} | custom-call | flops 268435456 | bytes 7340032 | tf_op jit(solution)/shard_map/final_products/pallas_call | solution.py:447
Async XLA Ops:
  5.2 10.4 %collective-permute-start.1 = (f32[4,128,128]{2,1,0:T(8,128)}, f32[4,128,128]{2,1,0:T(8,128)S(1)}, u32[]{:S(2)}, u32[]{:S(2)}) collective-permute-start(f32[4,128,128]{2,1,0:T(8,128)} %get-tuple-element.19.after), channel_id=1, source_target_pairs={{0,4},{4,0},{8,12},{12,8},{1,5},{5,1},{9,13},{13,9},{2,6},{6,2},{1... | collective-permute-start | bytes 786440 | tf_op jit(solution)/shard_map/ppermute | solution.py:479
  8.3 13.1 %collective-permute-start = (f32[4,128,128]{2,1,0:T(8,128)}, f32[4,128,128]{2,1,0:T(8,128)S(1)}, u32[]{:S(2)}, u32[]{:S(2)}) collective-permute-start(f32[4,128,128]{2,1,0:T(8,128)} %get-tuple-element.18), channel_id=1, source_target_pairs={{0,4},{4,0},{8,12},{12,8},{1,5},{5,1},{9,13},{13,9},{2,6},{6,2},{1... | collective-permute-start | bytes 786440 | tf_op jit(solution)/shard_map/ppermute | solution.py:479
  8.4 7.3 %copy-start.8 = (s32[3,4]{1,0:T(4,128)S(1)}, s32[3,4]{1,0:T(4,128)}, u32[]{:S(2)}) copy-start(s32[3,4]{1,0:T(4,128)} %pack.17) | copy-start | bytes 148
  8.4 17.5 %copy-start.2 = (bf16[512,1024]{1,0:T(8,128)(2,1)S(1)}, bf16[512,1024]{1,0:T(8,128)(2,1)}, u32[]{:S(2)}) copy-start(bf16[512,1024]{1,0:T(8,128)(2,1)} %refs_2_.3) | copy-start | bytes 3145732
  8.4 17.5 %copy-start.3 = (bf16[512,1024]{1,0:T(8,128)(2,1)S(1)}, bf16[512,1024]{1,0:T(8,128)(2,1)}, u32[]{:S(2)}) copy-start(bf16[512,1024]{1,0:T(8,128)(2,1)} %refs_3_.3) | copy-start | bytes 3145732
  15.6 1.0 %copy-start.4 = (f32[4,128,128]{2,1,0:T(8,128)S(1)}, f32[4,128,128]{2,1,0:T(8,128)}, u32[]{:S(2)}) copy-start(f32[4,128,128]{2,1,0:T(8,128)} %get-tuple-element.21.own_ref.after) | copy-start | bytes 786436
  16.6 9.3 %copy-start = (bf16[512,1024]{1,0:T(8,128)(2,1)S(1)}, bf16[512,1024]{1,0:T(8,128)(2,1)}, u32[]{:S(2)}) copy-start(bf16[512,1024]{1,0:T(8,128)(2,1)} %refs_0_.3) | copy-start | bytes 3145732
  16.6 9.3 %copy-start.1 = (bf16[512,1024]{1,0:T(8,128)(2,1)S(1)}, bf16[512,1024]{1,0:T(8,128)(2,1)}, u32[]{:S(2)}) copy-start(bf16[512,1024]{1,0:T(8,128)(2,1)} %refs_1_.3) | copy-start | bytes 3145732
  17.2 16.9 %collective-permute-start.3 = (f32[4,128,128]{2,1,0:T(8,128)S(1)}, f32[4,128,128]{2,1,0:T(8,128)S(1)}, u32[]{:S(2)}, u32[]{:S(2)}) collective-permute-start(f32[4,128,128]{2,1,0:T(8,128)S(1)} %join.4.after), channel_id=1, source_target_pairs={{0,12},{4,8},{8,4},{12,0},{1,13},{5,9},{9,5},{13,1},{2,14},{6,10},... | collective-permute-start | bytes 786440 | tf_op jit(solution)/shard_map/ppermute | solution.py:487
  21.4 1.0 %copy-start.7 = (f32[4,128,128]{2,1,0:T(8,128)S(1)}, f32[4,128,128]{2,1,0:T(8,128)}, u32[]{:S(2)}) copy-start(f32[4,128,128]{2,1,0:T(8,128)} %get-tuple-element.20.own_ref) | copy-start | bytes 786436
  23.0 11.2 %copy-start.5 = (f32[4,128,128]{2,1,0:T(8,128)S(1)}, f32[4,128,128]{2,1,0:T(8,128)}, u32[]{:S(2)}) copy-start(f32[4,128,128]{2,1,0:T(8,128)} %get-tuple-element.27.own_ref) | copy-start | bytes 786436
  23.0 17.1 %collective-permute-start.2 = (f32[4,128,128]{2,1,0:T(8,128)S(1)}, f32[4,128,128]{2,1,0:T(8,128)S(1)}, u32[]{:S(2)}, u32[]{:S(2)}) collective-permute-start(f32[4,128,128]{2,1,0:T(8,128)S(1)} %join.5.after), channel_id=1, source_target_pairs={{0,12},{4,8},{8,4},{12,0},{1,13},{5,9},{9,5},{13,1},{2,14},{6,10},... | collective-permute-start | bytes 786440 | tf_op jit(solution)/shard_map/ppermute | solution.py:487
  34.2 5.9 %copy-start.6 = (f32[4,128,128]{2,1,0:T(8,128)S(1)}, f32[4,128,128]{2,1,0:T(8,128)}, u32[]{:S(2)}) copy-start(f32[4,128,128]{2,1,0:T(8,128)} %get-tuple-element.26.own_ref) | copy-start | bytes 786436
  34.8 11.2 %collective-permute-start.5 = (f32[4,128,128]{2,1,0:T(8,128)S(1)}, f32[4,128,128]{2,1,0:T(8,128)S(1)}, u32[]{:S(2)}, u32[]{:S(2)}) collective-permute-start(f32[4,128,128]{2,1,0:T(8,128)S(1)} %join.6.after), channel_id=1, source_target_pairs={{0,4},{4,0},{8,12},{12,8},{1,5},{5,1},{9,13},{13,9},{2,6},{6,2},{1... | collective-permute-start | bytes 786440 | tf_op jit(solution)/shard_map/ppermute | solution.py:490
  40.7 9.3 %collective-permute-start.4 = (f32[4,128,128]{2,1,0:T(8,128)S(1)}, f32[4,128,128]{2,1,0:T(8,128)S(1)}, u32[]{:S(2)}, u32[]{:S(2)}) collective-permute-start(f32[4,128,128]{2,1,0:T(8,128)S(1)} %join.7), channel_id=1, source_target_pairs={{0,4},{4,0},{8,12},{12,8},{1,5},{5,1},{9,13},{13,9},{2,6},{6,2},{1... | collective-permute-start | bytes 786440 | tf_op jit(solution)/shard_map/ppermute | solution.py:490

commit v3 on v2

--- a/solution.py
+++ b/solution.py
@@ -12,15 +12,31 @@
 GROUP = 512
 NB = GROUP // BLK
 SIZES = (4, 4)
-ORDER = (("two", 0), ("two", 1), ("in", 0), ("three", 0), ("three", 1), ("end", 0), ("end", 1))
+IN_SIZES = (4, 4)
+ORDER = (
+    ("one", 0),
+    ("own_two", 0),
+    ("early", 0),
+    ("one", 1),
+    ("two", 0),
+    ("own_three", 0),
+    ("in", 0),
+    ("two", 1),
+    ("in", 1),
+    ("three", 0),
+    ("three", 1),
+    ("end", 0),
+    ("end", 1),
+)
+MIB = 2**20
+FIRST_LIMIT = 60 * MIB
+SUMS_LIMIT = 12 * MIB
+JOIN_LIMIT = 4 * MIB
+IN_LIMIT = 16 * MIB
+END_LIMIT = 16 * MIB
 HELD = jnp.bfloat16
 F32 = jnp.float32
 BF16 = jnp.bfloat16
-MIB = 2**20
-SUMS_LIMIT = 60 * MIB
-JOIN_LIMIT = 4 * MIB
-IN_LIMIT = 16 * MIB
-END_LIMIT = 16 * MIB
 
 
 def flag(condition):
@@ -182,8 +198,10 @@
     return forward, backward
 
 
+SHORT = pl.CostEstimate(flops=1, bytes_accessed=1, transcendentals=0)
 SMEM = pl.BlockSpec(memory_space=pltpu.SMEM)
 ANY = pl.BlockSpec(memory_space=pl.ANY)
+HBM = pl.BlockSpec(memory_space=pltpu.HBM)
 VMEM = pl.BlockSpec(memory_space=pltpu.VMEM)
 
 
@@ -220,33 +238,34 @@
     return lax.dot_general(a, b, (((1,), (0,)), ((), ())), preferred_element_type=F32)
 
 
-def sums_kernel(messages, sizes, pack, place, q_hbm, k_hbm, v_hbm, g_hbm, after, *refs):
-    many, heads = len(messages), sum(sizes)
-    outs = refs[: many * len(sizes)]
-    left, right, weight_ref, sign_ref, sems = refs[many * len(sizes) :]
+def sums_kernel(messages, first, sizes, pack, place, q_hbm, k_hbm, v_hbm, g_hbm, after, *refs):
+    many, chunks = len(messages), len(sizes)
+    outs = refs[: many * chunks]
+    left, right, total, weight_ref, sign_ref, in_sems, out_sems = refs[many * chunks :]
     d = place[0]
     seg, _, _ = edges(pack, NB)
     tables = [m(pack, d, NB)[-4:] for m in messages]
-
-    def copies(m, source_left, source_right):
-        out = []
-        for h in range(heads):
-            cols = pl.ds(h * DH, DH)
-            out.append(
-                [
-                    pltpu.make_async_copy(src.at[:, cols], dst.at[m, :, cols], sems.at[m, n, h])
-                    for n, (src, dst) in enumerate(((source_left, left), (source_right, right)))
-                ]
-            )
-        return out
+    starts = [sum(sizes[:c]) for c in range(chunks)]
+
+    def copies(m, c, sources):
+        there = pl.ds((first + starts[c]) * DH, sizes[c] * DH)
+        here = pl.ds(starts[c] * DH, sizes[c] * DH)
+        return [
+            pltpu.make_async_copy(src.at[:, there], dst.at[m, :, here], in_sems.at[m, n, c])
+            for n, (src, dst) in enumerate(zip(sources, (left, right)))
+        ]
+
+    def result(m, c):
+        heads = pl.ds(starts[c], sizes[c])
+        return pltpu.make_async_copy(total.at[m, heads], outs[m * chunks + c], out_sems.at[m, c])
 
     for m in range(many):
         for kind, sources in ((1, (k_hbm, v_hbm)), (0, (q_hbm, g_hbm))):
 
             @pl.when(tables[m][0] == kind)
             def _():
-                for both in copies(m, *sources):
-                    for copy in both:
+                for c in range(chunks):
+                    for copy in copies(m, c, sources):
                         copy.start()
 
     fill_scale(pack, d, None, sign_ref)
@@ -256,41 +275,40 @@
             rows = pl.ds(b * BLK, BLK)
             takes = pick(seg(d * NB + b), tables[m][1:]).astype(F32)
             weight_ref[m, rows, :] = jnp.where(forward, 1.0, sign_ref[rows, :]) * takes
-    waits = [copies(m, k_hbm, v_hbm) for m in range(many)]
     for m in range(many):
-        h = 0
-        for c, size in enumerate(sizes):
-            for inner in range(size):
-                for copy in waits[m][h]:
-                    copy.wait()
+        for c in range(chunks):
+            for copy in copies(m, c, (k_hbm, v_hbm)):
+                copy.wait()
+            for h in range(starts[c], starts[c] + sizes[c]):
                 cols = pl.ds(h * DH, DH)
                 rows = weighted(right[m, :, cols], weight_ref[m])
-                outs[m * len(sizes) + c][inner] = contract_rows(left[m, :, cols], rows)
-                h += 1
-
-
-def local_sums(messages, sizes, scalars, tokens, after):
+                total[m, h] = contract_rows(left[m, :, cols], rows)
+            result(m, c).start()
+    for m in range(many):
+        for c in range(chunks):
+            result(m, c).wait()
+
+
+def local_sums(messages, first, sizes, scalars, tokens, after, limit):
     rows, heads, many = tokens[0].shape[0], sum(sizes), len(messages)
     out = pl.pallas_call(
-        functools.partial(sums_kernel, messages, sizes),
+        functools.partial(sums_kernel, messages, first, sizes),
         out_shape=[
             jax.ShapeDtypeStruct((size, DH, DH), F32) for _ in messages for size in sizes
         ],
-        in_specs=[SMEM, SMEM] + [ANY] * 5,
-        out_specs=[VMEM] * (many * len(sizes)),
+        in_specs=[SMEM, SMEM] + [HBM] * 4 + [ANY],
+        out_specs=[ANY] * (many * len(sizes)),
         scratch_shapes=[
             pltpu.VMEM((many, rows, heads * DH), BF16),
             pltpu.VMEM((many, rows, heads * DH), BF16),
+            pltpu.VMEM((many, heads, DH, DH), F32),
             pltpu.VMEM((many, rows, DH), F32),
             pltpu.VMEM((rows, DH), F32),
-            pltpu.SemaphoreType.DMA((many, 2, heads)),
+            pltpu.SemaphoreType.DMA((many, 2, len(sizes))),
+            pltpu.SemaphoreType.DMA((many, len(sizes))),
         ],
-        compiler_params=pltpu.CompilerParams(vmem_limit_bytes=SUMS_LIMIT),
-        cost_estimate=pl.CostEstimate(
-            flops=2 * rows * DH * DH * heads * many,
-            bytes_accessed=8 * rows * heads * DH * many,
-            transcendentals=0,
-        ),
+        compiler_params=pltpu.CompilerParams(vmem_limit_bytes=limit),
+        cost_estimate=SHORT,
         name="local_sums",
     )(*scalars, *tokens, after)
     return [out[m * len(sizes) : (m + 1) * len(sizes)] for m in range(many)]
@@ -309,20 +327,21 @@
 
 
 def join(message, scalars, got, own, after):
+    block = pl.BlockSpec(got.shape, lambda i: (0, 0, 0))
     return pl.pallas_call(
         functools.partial(join_kernel, message),
         out_shape=jax.ShapeDtypeStruct(got.shape, F32),
-        in_specs=[SMEM, SMEM, VMEM, VMEM, ANY],
-        out_specs=VMEM,
+        grid=(1,),
+        in_specs=[SMEM, SMEM, block, block, ANY],
+        out_specs=block,
         compiler_params=pltpu.CompilerParams(vmem_limit_bytes=JOIN_LIMIT),
-        cost_estimate=pl.CostEstimate(
-            flops=got.size, bytes_accessed=12 * got.size, transcendentals=0
-        ),
+        cost_estimate=SHORT,
         name="join",
     )(*scalars, got, own, after)
 
 
-def inside_kernel(per, pack, place, q_ref, k_ref, v_ref, g_ref, after, o1, o2, o3, o4, mask_ref, sign_ref):
+def inside_kernel(per, pack, place, q_ref, k_ref, v_ref, g_ref, *refs):
+    o1, o2, o3, o4, mask_ref, sign_ref = refs[-6:]
     d = place[0]
     half = GROUP // 2
 
@@ -373,25 +392,29 @@
         put(o3, hi, gk[hi])
 
 
-def inside_products(scalars, tokens, after):
-    rows, heads = tokens[0].shape[0], tokens[0].shape[1] // DH
-    per = 2 if heads % 2 == 0 else 1
-    spec = pl.BlockSpec((rows, per * DH), lambda i: (0, i))
+def inside_products(first, heads, scalars, tokens, before, after):
+    rows, cols = tokens[0].shape
+    per = 2 if first % 2 == 0 and heads % 2 == 0 else 1
+    spec = pl.BlockSpec((rows, per * DH), lambda i: (0, first // per + i))
+    operands = [*scalars, *tokens, after]
+    specs = [SMEM, SMEM] + [spec] * 4 + [ANY]
+    aliases = {}
+    if before is not None:
+        aliases = {len(operands) + n: n for n in range(4)}
+        operands += list(before)
+        specs += [ANY] * 4
     return pl.pallas_call(
         functools.partial(inside_kernel, per),
-        out_shape=[jax.ShapeDtypeStruct((rows, heads * DH), HELD)] * 4,
+        out_shape=[jax.ShapeDtypeStruct((rows, cols), HELD)] * 4,
         grid=(heads // per,),
-        in_specs=[SMEM, SMEM] + [spec] * 4 + [ANY],
+        in_specs=specs,
         out_specs=[spec] * 4,
         scratch_shapes=[pltpu.VMEM((rows, rows), BF16), pltpu.VMEM((rows, DH), F32)],
+        input_output_aliases=aliases,
         compiler_params=pltpu.CompilerParams(vmem_limit_bytes=IN_LIMIT),
-        cost_estimate=pl.CostEstimate(
-            flops=9 * rows * rows * DH * heads,
-            bytes_accessed=16 * rows * heads * DH,
-            transcendentals=0,
-        ),
+        cost_estimate=SHORT,
         name="inside_products",
-    )(*scalars, *tokens, after)
+    )(*operands)
 
 
 def final_kernel(per, pack, place, *refs):
@@ -458,11 +481,7 @@
         ],
         input_output_aliases=aliases,
         compiler_params=pltpu.CompilerParams(vmem_limit_bytes=END_LIMIT),
-        cost_estimate=pl.CostEstimate(
-            flops=8 * rows * DH * DH * heads,
-            bytes_accessed=28 * rows * DH * heads,
-            transcendentals=0,
-        ),
+        cost_estimate=SHORT,
         name="final_products",
     )(*operands)
 
@@ -475,25 +494,46 @@
     near = [(i, i ^ 1) for i in range(4)]
     across = [(i, 3 - i) for i in range(4)]
 
-    (early,) = local_sums((message_one,), SIZES, scalars, tokens, packing)
-    one = [lax.ppermute(value, "seq", near) for value in early]
-    own_two, own_three = local_sums((message_two, message_three), SIZES, scalars, tokens, early[0])
-    last = own_two[0]
-    two, three = [None] * len(SIZES), [None] * len(SIZES)
-    out = None
+    count = len(SIZES)
+    one, two, three = [None] * count, [None] * count, [None] * count
+    early = local_sums((message_one,), 0, SIZES[:1], scalars, tokens, packing, FIRST_LIMIT)[0]
+    last = early[0]
+    inside, out = None, None
     for what, c in ORDER:
-        if what == "two":
+        if what == "one":
+            one[c] = lax.ppermute(early[c], "seq", near)
+        elif what == "early":
+            early += local_sums(
+                (message_one,), SIZES[0], SIZES[1:], scalars, tokens, last, SUMS_LIMIT
+            )[0]
+            last = early[-1]
+        elif what == "own":
+            own_two, own_three = local_sums(
+                (message_two, message_three), 0, SIZES, scalars, tokens, last, SUMS_LIMIT
+            )
+            last = own_two[0]
+        elif what == "own_two":
+            (own_two,) = local_sums((message_two,), 0, SIZES, scalars, tokens, last, SUMS_LIMIT)
+            last = own_two[0]
+        elif what == "own_three":
+            (own_three,) = local_sums(
+                (message_three,), 0, SIZES, scalars, tokens, last, SUMS_LIMIT
+            )
+            last = own_three[0]
+        elif what == "two":
             last = join(message_two, scalars, one[c], own_two[c], last)
             two[c] = lax.ppermute(last, "seq", across)
         elif what == "three":
             last = join(message_three, scalars, two[c], own_three[c], last)
             three[c] = lax.ppermute(last, "seq", near)
         elif what == "in":
-            inside = inside_products(scalars, tokens, last)
+            first = 0 if inside is None else sum(IN_SIZES[:c])
+            inside = inside_products(first, IN_SIZES[c], scalars, tokens, inside, last)
             last = inside[0]
         else:
             got = (one[c], two[c], three[c])
             out = final_products(starts[c], SIZES[c], scalars, tokens, inside, got, out)
+            last = out[0]
     return tuple(out)
 
 

time: 53.6 us -> 50.6 us (0.944)
  Pallas kernels: 28.7 us -> 26.2 us
  starting transfers between devices: 18.7 us -> 17.1 us
  waiting for transfers between devices: 3.36 us -> 4.12 us
    pallas_call x2 -> x4, Pallas kernels: 11.4 us -> 8.3 us  [local_sums(): pl.pallas_call(functools.partial(sums_kernel, messages, first, sizes), ou...]
    ppermute x2, starting transfers between devices: 8.4 us -> 5.63 us  [exchange_body(): three[c] = lax.ppermute(last, 'seq', near)]
    ppermute x2, starting transfers between devices: 7.09 us -> 8.25 us  [exchange_body(): two[c] = lax.ppermute(last, 'seq', across)]
    ppermute x2, waiting for transfers between devices: 0.45 us -> 1.05 us  [exchange_body(): one[c] = lax.ppermute(early[c], 'seq', near)]
    pallas_call x1 -> x2, Pallas kernels: 8.25 us -> 8.75 us  [inside_products(): pl.pallas_call(functools.partial(inside_kernel, per), out_shape=[jax.Shap...]
    unnamed x18 -> x14, local copies, waits for them, and re-layouts: 1.93 us -> 2.19 us
where the time goes in v3:
time: 50.6 us; the launch traced here: 50.4 us
  Pallas kernels  26.2 us (52%)
  starting transfers between devices  17.1 us (34%)
  waiting for transfers between devices  4.12 us (8%)
  local copies, waits for them, and re-layouts  2.19 us (4%)
  between operations  0.79 us (2%)
    pallas_call x2, Pallas kernels, inside_products(): pl.pallas_call(functools.partial(inside_kernel, per), out_shape=[jax.Shap...  8.75 us
    pallas_call x4, Pallas kernels, local_sums(): pl.pallas_call(functools.partial(sums_kernel, messages, first, sizes), ou...  8.3 us
    ppermute x2, starting transfers between devices, exchange_body(): two[c] = lax.ppermute(last, 'seq', across)  8.25 us
    pallas_call x2, Pallas kernels, final_products(): pl.pallas_call(functools.partial(final_kernel, per), out_shape=[jax.Shape...  6.66 us
    ppermute x2, starting transfers between devices, exchange_body(): three[c] = lax.ppermute(last, 'seq', near)  5.63 us
    ppermute x2, starting transfers between devices, exchange_body(): one[c] = lax.ppermute(early[c], 'seq', near)  3.19 us
    ppermute x2, waiting for transfers between devices, exchange_body(): three[c] = lax.ppermute(last, 'seq', near)  3.07 us
    pallas_call x4, Pallas kernels, join(): pl.pallas_call(functools.partial(join_kernel, message), out_shape=jax.Sha...  2.48 us
  transfers between devices with their start and end apart: 6, of which 3 were waited for; matrix products, arithmetic and copies ran while one was open for 0% of the time, Pallas kernels for 39%

profile of v3, /device:TPU:0, one launch (start us, length us, event | category | flops | bytes accessed | tf_op | source)
XLA Modules:
  0.0 50.4 jit_solution(2389909070964406090)
XLA Ops:
  0.6 0.0 copy-start
  0.6 0.0 copy-start.1
  0.7 0.0 copy-start.2
  0.7 0.0 copy-start.6
  0.7 3.2 %local_sums.4.after = f32[4,128,128]{2,1,0:T(8,128)} custom-call(s32[3,4]{1,0:T(4,128)} %pack.23, s32[1]{0:T(128)} %bitcast.place, bf16[512,1024]{1,0:T(8,128)(2,1)} %refs_0_.3, bf16[512,1024]{1,0:T(8,128)(2,1)} %refs_1_.3, bf16[512,1024]{1,0:T(8,128)(2,1)} %refs_2_.3, bf16[512,1024]{1,0:T(8,128)(2,1)} %refs_3_.3, s32[3,4]{1,0:T(4,128)} %pack.23), custom_call_target="tpu_custom_call" | custom-call | flops 1 | bytes 1 | tf_op jit(solution)/shard_map/local_sums/pallas_call | solution.py:294
  3.9 3.1 %collective-permute-start.1 = (f32[4,128,128]{2,1,0:T(8,128)}, f32[4,128,128]{2,1,0:T(8,128)S(1)}, u32[]{:S(2)}, u32[]{:S(2)}) collective-permute-start(f32[4,128,128]{2,1,0:T(8,128)} %local_sums.4.after), channel_id=1, source_target_pairs={{0,4},{4,0},{8,12},{12,8},{1,5},{5,1},{9,13},{13,9},{2,6},{6,2},{1... | collective-permute-start | bytes 786440 | tf_op jit(solution)/shard_map/ppermute | solution.py:504
  7.0 0.0 copy-done
  7.0 0.0 copy-done.1
  7.0 0.0 copy-done.2
  7.0 0.0 copy-done.6
  7.0 0.0 copy-start.3
  7.0 1.2 %copy-done.3 = bf16[512,1024]{1,0:T(8,128)(2,1)S(1)} copy-done((bf16[512,1024]{1,0:T(8,128)(2,1)S(1)}, bf16[512,1024]{1,0:T(8,128)(2,1)}, u32[]{:S(2)}) %copy-start.3) | copy-done | bytes 1048600
  8.2 0.0 copy-start.5
  8.2 0.9 %copy-done.5 = f32[4,128,128]{2,1,0:T(8,128)S(1)} copy-done((f32[4,128,128]{2,1,0:T(8,128)S(1)}, f32[4,128,128]{2,1,0:T(8,128)}, u32[]{:S(2)}) %copy-start.5) | copy-done | bytes 262168
  9.2 1.9 %local_sums.5 = (f32[4,128,128]{2,1,0:T(8,128)S(1)}, f32[4,128,128]{2,1,0:T(8,128)S(1)}) custom-call(s32[3,4]{1,0:T(4,128)S(1)} %copy-done.6, s32[1]{0:T(128)} %bitcast.place, bf16[512,1024]{1,0:T(8,128)(2,1)S(1)} %copy-done, bf16[512,1024]{1,0:T(8,128)(2,1)S(1)} %copy-done.1, bf16[512,1024]{1,0:T(8,128)(2,1)S(1)} %copy-done.2, ...), custom_call_target="tpu_custom_call" | custom-call | flops 1 | bytes 1 | tf_op jit(solution)/shard_map/local_sums/pallas_call | solution.py:294
  11.1 1.2 %local_sums.6.after = f32[4,128,128]{2,1,0:T(8,128)S(1)} custom-call(s32[3,4]{1,0:T(4,128)S(1)} %copy-done.6, s32[1]{0:T(128)} %bitcast.place, bf16[512,1024]{1,0:T(8,128)(2,1)S(1)} %copy-done, bf16[512,1024]{1,0:T(8,128)(2,1)S(1)} %copy-done.1, bf16[512,1024]{1,0:T(8,128)(2,1)S(1)} %copy-done.2, bf16[512,1024]{1,0:T(8,128)(2,1)S(1)} %copy-done.3, ...), custom_call_target="tpu_custom_call" | custom-call | flops 1 | bytes 1 | tf_op jit(solution)/shard_map/local_sums/pallas_call | solution.py:294
  12.3 0.1 collective-permute-start
  12.4 1.0 %collective-permute-done.1.got_ref.refs_8_ = f32[4,128,128]{2,1,0:T(8,128)S(1)} collective-permute-done((f32[4,128,128]{2,1,0:T(8,128)}, f32[4,128,128]{2,1,0:T(8,128)S(1)}, u32[]{:S(2)}, u32[]{:S(2)}) %collective-permute-start.1) | collective-permute-done | bytes 262176 | tf_op jit(solution)/shard_map/ppermute | solution.py:504
  13.5 0.6 %join.4.after = f32[4,128,128]{2,1,0:T(8,128)S(1)} custom-call(s32[3,4]{1,0:T(4,128)S(1)} %copy-done.6, s32[1]{0:T(128)} %bitcast.place, f32[4,128,128]{2,1,0:T(8,128)S(1)} %collective-permute-done.1.got_ref.refs_8_, f32[4,128,128]{2,1,0:T(8,128)S(1)} %get-tuple-element.20.after.own_ref, f32[4,128,128]{2,1,0:T(8,128)S(1)} %local_sums.6.after), custom_call_target="tpu_custom_call" | custom-call | flops 1 | bytes 1 | tf_op jit(solution)/shard_map/join/pallas_call | solution.py:331
  14.1 0.0 copy-start.4
  14.1 4.0 %collective-permute-start.3 = (f32[4,128,128]{2,1,0:T(8,128)S(1)}, f32[4,128,128]{2,1,0:T(8,128)S(1)}, u32[]{:S(2)}, u32[]{:S(2)}) collective-permute-start(f32[4,128,128]{2,1,0:T(8,128)S(1)} %join.4.after), channel_id=1, source_target_pairs={{0,12},{4,8},{8,4},{12,0},{1,13},{5,9},{9,5},{13,1},{2,14},{6,10},... | collective-permute-start | bytes 786440 | tf_op jit(solution)/shard_map/ppermute | solution.py:525
  18.1 1.9 %local_sums.7 = (f32[4,128,128]{2,1,0:T(8,128)S(1)}, f32[4,128,128]{2,1,0:T(8,128)S(1)}) custom-call(s32[3,4]{1,0:T(4,128)S(1)} %copy-done.6, s32[1]{0:T(128)} %bitcast.place, bf16[512,1024]{1,0:T(8,128)(2,1)S(1)} %copy-done, bf16[512,1024]{1,0:T(8,128)(2,1)S(1)} %copy-done.1, bf16[512,1024]{1,0:T(8,128)(2,1)S(1)} %copy-done.2, ...), custom_call_target="tpu_custom_call" | custom-call | flops 1 | bytes 1 | tf_op jit(solution)/shard_map/local_sums/pallas_call | solution.py:294
  20.1 0.0 copy-done.4
  20.1 4.4 %inside_products.2 = (bf16[512,1024]{1,0:T(8,128)(2,1)S(1)}, bf16[512,1024]{1,0:T(8,128)(2,1)S(1)}, bf16[512,1024]{1,0:T(8,128)(2,1)S(1)}, bf16[512,1024]{1,0:T(8,128)(2,1)S(1)}) custom-call(s32[3,4]{1,0:T(4,128)S(1)} %copy-done.6, s32[1]{0:T(128)} %bitcast.place, bf16[512,1024]{1,0:T(8,128)(2,1)S(1)} %copy-done, bf16[512,1024]{1,0:T(8,128)(2,1)S(1)} %copy-done.1, ...), custom_call_target="tpu_custom_call" | custom-call | flops 1 | bytes 1 | tf_op jit(solution)/shard_map/inside_products/pallas_call | solution.py:406
  24.5 0.0 collective-permute-done.got_ref.refs_8_
  24.5 0.6 %join.5.refs_0_ = f32[4,128,128]{2,1,0:T(8,128)S(1)} custom-call(s32[3,4]{1,0:T(4,128)S(1)} %copy-done.6, s32[1]{0:T(128)} %bitcast.place, f32[4,128,128]{2,1,0:T(8,128)S(1)} %collective-permute-done.got_ref.refs_8_, f32[4,128,128]{2,1,0:T(8,128)S(1)} %get-tuple-element.21.own_ref, bf16[512,1024]{1,0:T(8,128)(2,1)S(1)} %get-tuple-element.23.after.refs_1_), custom_call_target="tpu_custom_call" | custom-call | flops 1 | bytes 1 | tf_op jit(solution)/shard_map/join/pallas_call | solution.py:331
  25.1 4.3 %collective-permute-start.2 = (f32[4,128,128]{2,1,0:T(8,128)S(1)}, f32[4,128,128]{2,1,0:T(8,128)S(1)}, u32[]{:S(2)}, u32[]{:S(2)}) collective-permute-start(f32[4,128,128]{2,1,0:T(8,128)S(1)} %join.5.refs_0_), channel_id=1, source_target_pairs={{0,12},{4,8},{8,4},{12,0},{1,13},{5,9},{9,5},{13,1},{2,14},{6,10},... | collective-permute-start | bytes 786440 | tf_op jit(solution)/shard_map/ppermute | solution.py:525
  29.4 4.4 %inside_products.3 = (bf16[512,1024]{1,0:T(8,128)(2,1)S(1)}, bf16[512,1024]{1,0:T(8,128)(2,1)S(1)}, bf16[512,1024]{1,0:T(8,128)(2,1)S(1)}, bf16[512,1024]{1,0:T(8,128)(2,1)S(1)}) custom-call(s32[3,4]{1,0:T(4,128)S(1)} %copy-done.6, s32[1]{0:T(128)} %bitcast.place, ...), custom_call_target="tpu_custom_call", output_to_operand_aliasing={{0}: (7, {}), {1}: (8, {}), {2}: (9, {}), {3}: (10, {})} | custom-call | flops 1 | bytes 1 | tf_op jit(solution)/shard_map/inside_products/pallas_call | solution.py:406
  33.7 0.0 collective-permute-done.3.got_ref.refs_9_
  33.8 0.6 %join.6.after = f32[4,128,128]{2,1,0:T(8,128)S(1)} custom-call(s32[3,4]{1,0:T(4,128)S(1)} %copy-done.6, s32[1]{0:T(128)} %bitcast.place, f32[4,128,128]{2,1,0:T(8,128)S(1)} %collective-permute-done.3.got_ref.refs_9_, f32[4,128,128]{2,1,0:T(8,128)S(1)} %get-tuple-element.22.refs_0_.own_ref, bf16[512,1024]{1,0:T(8,128)(2,1)S(1)} %get-tuple-element.27.after.refs_4_), custom_call_target="tpu_custom_call" | custom-call | flops 1 | bytes 1 | tf_op jit(solution)/shard_map/join/pallas_call | solution.py:331
  34.4 0.7 %collective-permute-start.5 = (f32[4,128,128]{2,1,0:T(8,128)S(1)}, f32[4,128,128]{2,1,0:T(8,128)S(1)}, u32[]{:S(2)}, u32[]{:S(2)}) collective-permute-start(f32[4,128,128]{2,1,0:T(8,128)S(1)} %join.6.after), channel_id=1, source_target_pairs={{0,4},{4,0},{8,12},{12,8},{1,5},{5,1},{9,13},{13,9},{2,6},{6,2},{1... | collective-permute-start | bytes 786440 | tf_op jit(solution)/shard_map/ppermute | solution.py:528
  35.1 0.0 collective-permute-done.2.got_ref.refs_9_
  35.1 0.6 %join.7 = f32[4,128,128]{2,1,0:T(8,128)S(1)} custom-call(s32[3,4]{1,0:T(4,128)S(1)} %copy-done.6, s32[1]{0:T(128)} %bitcast.place, f32[4,128,128]{2,1,0:T(8,128)S(1)} %collective-permute-done.2.got_ref.refs_9_, f32[4,128,128]{2,1,0:T(8,128)S(1)} %get-tuple-element.31.own_ref, f32[4,128,128]{2,1,0:T(8,128)S(1)} %join.6.after), custom_call_target="tpu_custom_call" | custom-call | flops 1 | bytes 1 | tf_op jit(solution)/shard_map/join/pallas_call | solution.py:331
  35.7 5.0 %collective-permute-start.4 = (f32[4,128,128]{2,1,0:T(8,128)S(1)}, f32[4,128,128]{2,1,0:T(8,128)S(1)}, u32[]{:S(2)}, u32[]{:S(2)}) collective-permute-start(f32[4,128,128]{2,1,0:T(8,128)S(1)} %join.7), channel_id=1, source_target_pairs={{0,4},{4,0},{8,12},{12,8},{1,5},{5,1},{9,13},{13,9},{2,6},{6,2},{1... | collective-permute-start | bytes 786440 | tf_op jit(solution)/shard_map/ppermute | solution.py:528
  40.6 0.2 collective-permute-done.5.refs_10_
  40.8 3.3 %final_products.2 = (bf16[512,1024]{1,0:T(8,128)(2,1)}, bf16[512,1024]{1,0:T(8,128)(2,1)}, bf16[512,1024]{1,0:T(8,128)(2,1)}, bf16[512,1024]{1,0:T(8,128)(2,1)}) custom-call(s32[3,4]{1,0:T(4,128)S(1)} %copy-done.6, s32[1]{0:T(128)} %bitcast.place, bf16[512,1024]{1,0:T(8,128)(2,1)S(1)} %copy-done, bf16[512,1024]{1,0:T(8,128)(2,1)S(1)} %copy-done.1, ...), custom_call_target="tpu_custom_call" | custom-call | flops 1 | bytes 1 | tf_op jit(solution)/shard_map/final_products/pallas_call | solution.py:470
  44.2 2.9 %collective-permute-done.4.refs_10_ = f32[4,128,128]{2,1,0:T(8,128)S(1)} collective-permute-done((f32[4,128,128]{2,1,0:T(8,128)S(1)}, f32[4,128,128]{2,1,0:T(8,128)S(1)}, u32[]{:S(2)}, u32[]{:S(2)}) %collective-permute-start.4) | collective-permute-done | bytes 262176 | tf_op jit(solution)/shard_map/ppermute | solution.py:528
  47.1 3.3 %final_products.3 = (bf16[512,1024]{1,0:T(8,128)(2,1)}, bf16[512,1024]{1,0:T(8,128)(2,1)}, bf16[512,1024]{1,0:T(8,128)(2,1)}, bf16[512,1024]{1,0:T(8,128)(2,1)}) custom-call(s32[3,4]{1,0:T(4,128)S(1)} %copy-done.6, s32[1]{0:T(128)} %bitcast.place, ...), custom_call_target="tpu_custom_call", output_to_operand_aliasing={{0}: (13, {}), {1}: (14, {}), {2}: (15, {}), {3}: (16, {})} | custom-call | flops 1 | bytes 1 | tf_op jit(solution)/shard_map/final_products/pallas_call | solution.py:470
Async XLA Ops:
  0.6 6.3 %copy-start = (bf16[512,1024]{1,0:T(8,128)(2,1)S(1)}, bf16[512,1024]{1,0:T(8,128)(2,1)}, u32[]{:S(2)}) copy-start(bf16[512,1024]{1,0:T(8,128)(2,1)} %refs_0_.3) | copy-start | bytes 3145732
  0.6 6.3 %copy-start.1 = (bf16[512,1024]{1,0:T(8,128)(2,1)S(1)}, bf16[512,1024]{1,0:T(8,128)(2,1)}, u32[]{:S(2)}) copy-start(bf16[512,1024]{1,0:T(8,128)(2,1)} %refs_1_.3) | copy-start | bytes 3145732
  0.7 6.3 %copy-start.2 = (bf16[512,1024]{1,0:T(8,128)(2,1)S(1)}, bf16[512,1024]{1,0:T(8,128)(2,1)}, u32[]{:S(2)}) copy-start(bf16[512,1024]{1,0:T(8,128)(2,1)} %refs_2_.3) | copy-start | bytes 3145732
  0.7 6.3 %copy-start.6 = (s32[3,4]{1,0:T(4,128)S(1)}, s32[3,4]{1,0:T(4,128)}, u32[]{:S(2)}) copy-start(s32[3,4]{1,0:T(4,128)} %pack.23) | copy-start | bytes 148
  3.9 9.6 %collective-permute-start.1 = (f32[4,128,128]{2,1,0:T(8,128)}, f32[4,128,128]{2,1,0:T(8,128)S(1)}, u32[]{:S(2)}, u32[]{:S(2)}) collective-permute-start(f32[4,128,128]{2,1,0:T(8,128)} %local_sums.4.after), channel_id=1, source_target_pairs={{0,4},{4,0},{8,12},{12,8},{1,5},{5,1},{9,13},{13,9},{2,6},{6,2},{1... | collective-permute-start | bytes 786440 | tf_op jit(solution)/shard_map/ppermute | solution.py:504
  7.0 1.2 %copy-start.3 = (bf16[512,1024]{1,0:T(8,128)(2,1)S(1)}, bf16[512,1024]{1,0:T(8,128)(2,1)}, u32[]{:S(2)}) copy-start(bf16[512,1024]{1,0:T(8,128)(2,1)} %refs_3_.3) | copy-start | bytes 3145732
  8.2 0.9 %copy-start.5 = (f32[4,128,128]{2,1,0:T(8,128)S(1)}, f32[4,128,128]{2,1,0:T(8,128)}, u32[]{:S(2)}) copy-start(f32[4,128,128]{2,1,0:T(8,128)} %local_sums.4.after) | copy-start | bytes 786436
  12.3 12.1 %collective-permute-start = (f32[4,128,128]{2,1,0:T(8,128)S(1)}, f32[4,128,128]{2,1,0:T(8,128)S(1)}, u32[]{:S(2)}, u32[]{:S(2)}) collective-permute-start(f32[4,128,128]{2,1,0:T(8,128)S(1)} %local_sums.6.after), channel_id=1, source_target_pairs={{0,4},{4,0},{8,12},{12,8},{1,5},{5,1},{9,13},{13,9},{2,6},{6,2},{1... | collective-permute-start | bytes 786440 | tf_op jit(solution)/shard_map/ppermute | solution.py:504
  14.1 6.0 %copy-start.4 = (bf16[512,1024]{1,0:T(8,128)(2,1)S(1)}, bf16[512,1024]{1,0:T(8,128)(2,1)}, u32[]{:S(2)}) copy-start(bf16[512,1024]{1,0:T(8,128)(2,1)} %refs_3_.3) | copy-start | bytes 3145732
  14.1 19.6 %collective-permute-start.3 = (f32[4,128,128]{2,1,0:T(8,128)S(1)}, f32[4,128,128]{2,1,0:T(8,128)S(1)}, u32[]{:S(2)}, u32[]{:S(2)}) collective-permute-start(f32[4,128,128]{2,1,0:T(8,128)S(1)} %join.4.after), channel_id=1, source_target_pairs={{0,12},{4,8},{8,4},{12,0},{1,13},{5,9},{9,5},{13,1},{2,14},{6,10},... | collective-permute-start | bytes 786440 | tf_op jit(solution)/shard_map/ppermute | solution.py:525
  25.1 9.9 %collective-permute-start.2 = (f32[4,128,128]{2,1,0:T(8,128)S(1)}, f32[4,128,128]{2,1,0:T(8,128)S(1)}, u32[]{:S(2)}, u32[]{:S(2)}) collective-permute-start(f32[4,128,128]{2,1,0:T(8,128)S(1)} %join.5.refs_0_), channel_id=1, source_target_pairs={{0,12},{4,8},{8,4},{12,0},{1,13},{5,9},{9,5},{13,1},{2,14},{6,10},... | collective-permute-start | bytes 786440 | tf_op jit(solution)/shard_map/ppermute | solution.py:525
  34.4 6.4 %collective-permute-start.5 = (f32[4,128,128]{2,1,0:T(8,128)S(1)}, f32[4,128,128]{2,1,0:T(8,128)S(1)}, u32[]{:S(2)}, u32[]{:S(2)}) collective-permute-start(f32[4,128,128]{2,1,0:T(8,128)S(1)} %join.6.after), channel_id=1, source_target_pairs={{0,4},{4,0},{8,12},{12,8},{1,5},{5,1},{9,13},{13,9},{2,6},{6,2},{1... | collective-permute-start | bytes 786440 | tf_op jit(solution)/shard_map/ppermute | solution.py:528
  35.7 11.4 %collective-permute-start.4 = (f32[4,128,128]{2,1,0:T(8,128)S(1)}, f32[4,128,128]{2,1,0:T(8,128)S(1)}, u32[]{:S(2)}, u32[]{:S(2)}) collective-permute-start(f32[4,128,128]{2,1,0:T(8,128)S(1)} %join.7), channel_id=1, source_target_pairs={{0,4},{4,0},{8,12},{12,8},{1,5},{5,1},{9,13},{13,9},{2,6},{6,2},{1... | collective-permute-start | bytes 786440 | tf_op jit(solution)/shard_map/ppermute | solution.py:528

commit v4 on v3

--- a/solution.py
+++ b/solution.py
@@ -24,7 +24,9 @@
     ("two", 1),
     ("in", 1),
     ("three", 0),
+    ("base", 0),
     ("three", 1),
+    ("base", 1),
     ("end", 0),
     ("end", 1),
 )
@@ -205,6 +207,10 @@
 VMEM = pl.BlockSpec(memory_space=pltpu.VMEM)
 
 
+def order_spec(after):
+    return SMEM if after.dtype == jnp.int32 else ANY
+
+
 def fill_scale(pack, d, scale_ref, sign_ref):
     seg, _, _ = edges(pack, NB)
     prompt = pack[0, 1] - pack[0, 0]
@@ -332,7 +338,7 @@
         functools.partial(join_kernel, message),
         out_shape=jax.ShapeDtypeStruct(got.shape, F32),
         grid=(1,),
-        in_specs=[SMEM, SMEM, block, block, ANY],
+        in_specs=[SMEM, SMEM, block, block, order_spec(after)],
         out_specs=block,
         compiler_params=pltpu.CompilerParams(vmem_limit_bytes=JOIN_LIMIT),
         cost_estimate=SHORT,
@@ -397,7 +403,7 @@
     per = 2 if first % 2 == 0 and heads % 2 == 0 else 1
     spec = pl.BlockSpec((rows, per * DH), lambda i: (0, first // per + i))
     operands = [*scalars, *tokens, after]
-    specs = [SMEM, SMEM] + [spec] * 4 + [ANY]
+    specs = [SMEM, SMEM] + [spec] * 4 + [order_spec(after)]
     aliases = {}
     if before is not None:
         aliases = {len(operands) + n: n for n in range(4)}
@@ -417,67 +423,122 @@
     )(*operands)
 
 
-def final_kernel(per, pack, place, *refs):
-    q_ref, k_ref, v_ref, g_ref, i1, i2, i3, i4, r1, r2, r3 = refs[:11]
-    o1, o2, o3, o4, scale_ref, sign_ref, st_ref, bk_ref = refs[-8:]
+def base_kernel(first, heads, pack, place, *refs):
+    q_ref, k_ref, v_ref, g_ref, i1, i2, i3, i4, r1, r2, _ = refs[:11]
+    o1, o2, o3, o4, sign_ref, both_ref = refs[11:]
     d = place[0]
-
-    @pl.when(pl.program_id(0) == 0)
-    def _():
-        fill_scale(pack, d, scale_ref, sign_ref)
-
+    fill_scale(pack, d, None, sign_ref)
     seg, _, _ = edges(pack, NB)
-    forward, backward = state_table(pack, d, NB)
-    for h in range(per):
-        cols = slice(h * DH, (h + 1) * DH)
-        got = [r1[h], r2[h], r3[h]]
+    segs = [seg(d * NB + b) for b in range(NB)]
+    tables = state_table(pack, d, NB)
+    weights = [[[w.astype(F32) for w in row] for row in table] for table in tables]
+    both_ref[...] = jnp.zeros_like(both_ref)
+    for h in range(heads):
+        here = slice(h * DH, (h + 1) * DH)
+        cols = slice((first + h) * DH, (first + h + 1) * DH)
         for x in range(3):
-            for table, out in ((forward, st_ref), (backward, bk_ref)):
-                total = None
-                for weight, part in zip(table[x], got):
-                    term = weight.astype(F32) * part
-                    total = term if total is None else total + term
-                out[x] = total.astype(BF16)
+            for n, table in enumerate(weights):
+                total = table[x][0] * r1[h] + table[x][1] * r2[h]
+                part = slice(n * DH, (n + 1) * DH)
+                both_ref[h, x, part, part] = total.astype(BF16)
         for b in range(NB):
-            rows = pl.ds(b * BLK, BLK)
-            s = seg(d * NB + b)
-            st, bk = st_ref[s], bk_ref[s]
+            rows = slice(b * BLK, (b + 1) * BLK)
+            states = both_ref[h, segs[b]]
             q, k, v = q_ref[rows, cols], k_ref[rows, cols], v_ref[rows, cols]
             g = weighted(g_ref[rows, cols], sign_ref[rows, :])
-
-            def put(ref, held, value, scale=None):
-                total = held[rows, cols].astype(F32) + value
-                ref[rows, cols] = (total if scale is None else scale * total).astype(BF16)
-
-            put(o1, i1, plain(q, st), scale_ref[rows, :])
-            put(o2, i2, contract_cols(g, st))
-            put(o3, i3, contract_cols(v, bk))
-            put(o4, i4, plain(k, bk))
-
-
-def final_products(first, heads, scalars, tokens, inside, got, before):
+            one = plain(jnp.concatenate([q, k], axis=1), states)
+            two = contract_cols(jnp.concatenate([g, v], axis=1), states)
+            o1[rows, here] = i1[rows, cols].astype(F32) + one[:, :DH]
+            o4[rows, here] = i4[rows, cols].astype(F32) + one[:, DH:]
+            o2[rows, here] = i2[rows, cols].astype(F32) + two[:, :DH]
+            o3[rows, here] = i3[rows, cols].astype(F32) + two[:, DH:]
+
+
+def base_products(first, heads, scalars, tokens, inside, got, after):
+    rows = tokens[0].shape[0]
+    return pl.pallas_call(
+        functools.partial(base_kernel, first, heads),
+        out_shape=[jax.ShapeDtypeStruct((rows, heads * DH), F32)] * 4,
+        in_specs=[SMEM, SMEM] + [VMEM] * 10 + [order_spec(after)],
+        out_specs=[VMEM] * 4,
+        scratch_shapes=[
+            pltpu.VMEM((rows, DH), F32),
+            pltpu.VMEM((heads, 3, 2 * DH, 2 * DH), BF16),
+        ],
+        compiler_params=pltpu.CompilerParams(vmem_limit_bytes=END_LIMIT),
+        cost_estimate=SHORT,
+        name="base_products",
+    )(*scalars, *tokens, *inside, *got, after)
+
+
+def final_kernel(first, heads, pack, place, *refs):
+    q_ref, k_ref, v_ref, g_ref, i1, i2, i3, i4, r3 = refs[:9]
+    outs = refs[-12:-8]
+    b1, b2, b3, b4, scale_ref, sign_ref, both_ref, sems = refs[-8:]
+    d = place[0]
+    fill_scale(pack, d, scale_ref, sign_ref)
+    seg, _, _ = edges(pack, NB)
+    segs = [seg(d * NB + b) for b in range(NB)]
+    ahead, behind = [
+        [pick(s, [row[2] for row in table]).astype(F32) for s in segs]
+        for table in state_table(pack, d, NB)
+    ]
+    both_ref[...] = jnp.zeros_like(both_ref)
+    held = ((b1, outs[0]), (b2, outs[1]), (b3, outs[2]), (b4, outs[3]))
+
+    def copies(h):
+        return [
+            pltpu.make_async_copy(
+                buffer.at[:, pl.ds(h * DH, DH)], out.at[:, pl.ds((first + h) * DH, DH)], sems.at[n, h]
+            )
+            for n, (buffer, out) in enumerate(held)
+        ]
+
+    for h in range(heads):
+        here = slice(h * DH, (h + 1) * DH)
+        cols = slice((first + h) * DH, (first + h + 1) * DH)
+        state = r3[h].astype(BF16)
+        both_ref[h, :DH, :DH] = state
+        both_ref[h, DH:, DH:] = state
+        states = both_ref[h]
+        q, k, v = q_ref[:, cols], k_ref[:, cols], v_ref[:, cols]
+        g = weighted(g_ref[:, cols], sign_ref[...])
+        one = plain(jnp.concatenate([q, k], axis=1), states)
+        two = contract_cols(jnp.concatenate([g, v], axis=1), states)
+        for b in range(NB):
+            rows = slice(b * BLK, (b + 1) * BLK)
+            total = i1[rows, here] + ahead[b] * one[rows, :DH]
+            b1[rows, here] = (scale_ref[rows, :] * total).astype(BF16)
+            b4[rows, here] = (i4[rows, here] + behind[b] * one[rows, DH:]).astype(BF16)
+            b2[rows, here] = (i2[rows, here] + ahead[b] * two[rows, :DH]).astype(BF16)
+            b3[rows, here] = (i3[rows, here] + behind[b] * two[rows, DH:]).astype(BF16)
+        for copy in copies(h):
+            copy.start()
+    for h in range(heads):
+        for copy in copies(h):
+            copy.wait()
+
+
+def final_products(first, heads, scalars, tokens, base, got, before):
     rows, cols = tokens[0].shape
-    per = 2 if first % 2 == 0 and heads % 2 == 0 else 1
-    spec = pl.BlockSpec((rows, per * DH), lambda i: (0, first // per + i))
-    state = pl.BlockSpec((per, DH, DH), lambda i: (i, 0, 0))
-    operands = [*scalars, *tokens, *inside, *got]
-    specs = [SMEM, SMEM] + [spec] * 8 + [state] * 3
+    operands = [*scalars, *tokens, *base, got]
+    specs = [SMEM, SMEM] + [VMEM] * 9
     aliases = {}
     if before is not None:
         aliases = {len(operands) + n: n for n in range(4)}
         operands += list(before)
         specs += [ANY] * 4
     return pl.pallas_call(
-        functools.partial(final_kernel, per),
+        functools.partial(final_kernel, first, heads),
         out_shape=[jax.ShapeDtypeStruct((rows, cols), BF16)] * 4,
-        grid=(heads // per,),
         in_specs=specs,
-        out_specs=[spec] * 4,
-        scratch_shapes=[
+        out_specs=[ANY] * 4,
+        scratch_shapes=[pltpu.VMEM((rows, heads * DH), BF16)] * 4
+        + [
             pltpu.VMEM((rows, DH), F32),
             pltpu.VMEM((rows, DH), F32),
-            pltpu.VMEM((3, DH, DH), BF16),
-            pltpu.VMEM((3, DH, DH), BF16),
+            pltpu.VMEM((heads, 2 * DH, 2 * DH), BF16),
+            pltpu.SemaphoreType.DMA((4, heads)),
         ],
         input_output_aliases=aliases,
         compiler_params=pltpu.CompilerParams(vmem_limit_bytes=END_LIMIT),
@@ -498,7 +559,7 @@
     one, two, three = [None] * count, [None] * count, [None] * count
     early = local_sums((message_one,), 0, SIZES[:1], scalars, tokens, packing, FIRST_LIMIT)[0]
     last = early[0]
-    inside, out = None, None
+    inside, out, base = None, None, [None] * count
     for what, c in ORDER:
         if what == "one":
             one[c] = lax.ppermute(early[c], "seq", near)
@@ -507,11 +568,6 @@
                 (message_one,), SIZES[0], SIZES[1:], scalars, tokens, last, SUMS_LIMIT
             )[0]
             last = early[-1]
-        elif what == "own":
-            own_two, own_three = local_sums(
-                (message_two, message_three), 0, SIZES, scalars, tokens, last, SUMS_LIMIT
-            )
-            last = own_two[0]
         elif what == "own_two":
             (own_two,) = local_sums((message_two,), 0, SIZES, scalars, tokens, last, SUMS_LIMIT)
             last = own_two[0]
@@ -520,6 +576,10 @@
                 (message_three,), 0, SIZES, scalars, tokens, last, SUMS_LIMIT
             )
             last = own_three[0]
+        elif what == "base":
+            got = (one[c], two[c])
+            base[c] = base_products(starts[c], SIZES[c], scalars, tokens, inside, got, last)
+            last = base[c][0]
         elif what == "two":
             last = join(message_two, scalars, one[c], own_two[c], last)
             two[c] = lax.ppermute(last, "seq", across)
@@ -531,8 +591,7 @@
             inside = inside_products(first, IN_SIZES[c], scalars, tokens, inside, last)
             last = inside[0]
         else:
-            got = (one[c], two[c], three[c])
-            out = final_products(starts[c], SIZES[c], scalars, tokens, inside, got, out)
+            out = final_products(starts[c], SIZES[c], scalars, tokens, base[c], three[c], out)
             last = out[0]
     return tuple(out)
 

time: 50.6 us -> 50.3 us (level)
  Pallas kernels: 26.2 us -> 30 us
  starting transfers between devices: 17.1 us -> 14.7 us
  waiting for transfers between devices: 4.12 us -> 2.27 us
    pallas_call x2 -> x4, Pallas kernels: 6.66 us -> 10.3 us  [the longest x2 5.38 us: final_products(): pl.pallas_call(functools.partial(final_kernel, first, heads), out_shape=[...]
    ppermute x2, starting transfers between devices: 5.63 us -> 3.23 us  [exchange_body(): three[c] = lax.ppermute(last, 'seq', near)]
    ppermute x2, waiting for transfers between devices: 3.07 us -> 1.21 us  [exchange_body(): three[c] = lax.ppermute(last, 'seq', near)]
  transfers between devices with their start and end apart: 6 -> 6, of which waited for: 3 -> 2; matrix products, arithmetic and copies ran while one was open for 0% -> 0% of each run, Pallas kernels for 39% -> 48%
where the time goes in v4:
time: 50.3 us; the launch traced here: 50.1 us
  Pallas kernels  30 us (60%)
  starting transfers between devices  14.7 us (29%)
  waiting for transfers between devices  2.27 us (5%)
  local copies, waits for them, and re-layouts  2.19 us (4%)
  between operations  1 us (2%)
    pallas_call x2, Pallas kernels, inside_products(): pl.pallas_call(functools.partial(inside_kernel, per), out_shape=[jax.Shap...  8.74 us
    pallas_call x4, Pallas kernels, local_sums(): pl.pallas_call(functools.partial(sums_kernel, messages, first, sizes), ou...  8.3 us
    ppermute x2, starting transfers between devices, exchange_body(): two[c] = lax.ppermute(last, 'seq', across)  8.23 us
    pallas_call x2, Pallas kernels, final_products(): pl.pallas_call(functools.partial(final_kernel, first, heads), out_shape=[...  5.38 us
    pallas_call x2, Pallas kernels, base_products(): pl.pallas_call(functools.partial(base_kernel, first, heads), out_shape=[j...  4.92 us
    ppermute x2, starting transfers between devices, exchange_body(): three[c] = lax.ppermute(last, 'seq', near)  3.23 us
    ppermute x2, starting transfers between devices, exchange_body(): one[c] = lax.ppermute(early[c], 'seq', near)  3.19 us
    pallas_call x4, Pallas kernels, join(): pl.pallas_call(functools.partial(join_kernel, message), out_shape=jax.Sha...  2.61 us
  transfers between devices with their start and end apart: 6, of which 2 were waited for; matrix products, arithmetic and copies ran while one was open for 0% of the time, Pallas kernels for 48%

profile of v4, /device:TPU:0, one launch (start us, length us, event | category | flops | bytes accessed | tf_op | source)
XLA Modules:
  0.0 50.1 jit_solution(16037343763645838906)
XLA Ops:
  0.6 0.0 copy-start
  0.6 0.0 copy-start.1
  0.7 0.0 copy-start.2
  0.7 0.0 copy-start.6
  0.7 3.2 %local_sums.4.after = f32[4,128,128]{2,1,0:T(8,128)} custom-call(s32[3,4]{1,0:T(4,128)} %pack.27, s32[1]{0:T(128)} %bitcast.place, bf16[512,1024]{1,0:T(8,128)(2,1)} %refs_0_.7, bf16[512,1024]{1,0:T(8,128)(2,1)} %refs_1_.7, bf16[512,1024]{1,0:T(8,128)(2,1)} %refs_2_.7, bf16[512,1024]{1,0:T(8,128)(2,1)} %refs_3_.7, s32[3,4]{1,0:T(4,128)} %pack.27), custom_call_target="tpu_custom_call" | custom-call | flops 1 | bytes 1 | tf_op jit(solution)/shard_map/local_sums/pallas_call | solution.py:300
  3.9 3.1 %collective-permute-start.1 = (f32[4,128,128]{2,1,0:T(8,128)}, f32[4,128,128]{2,1,0:T(8,128)S(1)}, u32[]{:S(2)}, u32[]{:S(2)}) collective-permute-start(f32[4,128,128]{2,1,0:T(8,128)} %local_sums.4.after), channel_id=1, source_target_pairs={{0,4},{4,0},{8,12},{12,8},{1,5},{5,1},{9,13},{13,9},{2,6},{6,2},{1... | collective-permute-start | bytes 786440 | tf_op jit(solution)/shard_map/ppermute | solution.py:565
  7.0 0.0 copy-done
  7.0 0.0 copy-done.1
  7.0 0.0 copy-done.2
  7.0 0.0 copy-done.6
  7.0 0.0 copy-start.3
  7.0 1.2 %copy-done.3 = bf16[512,1024]{1,0:T(8,128)(2,1)S(1)} copy-done((bf16[512,1024]{1,0:T(8,128)(2,1)S(1)}, bf16[512,1024]{1,0:T(8,128)(2,1)}, u32[]{:S(2)}) %copy-start.3) | copy-done | bytes 1048600
  8.2 0.0 copy-start.5
  8.2 0.9 %copy-done.5 = f32[4,128,128]{2,1,0:T(8,128)S(1)} copy-done((f32[4,128,128]{2,1,0:T(8,128)S(1)}, f32[4,128,128]{2,1,0:T(8,128)}, u32[]{:S(2)}) %copy-start.5) | copy-done | bytes 262168
  9.2 1.9 %local_sums.5 = (f32[4,128,128]{2,1,0:T(8,128)S(1)}, f32[4,128,128]{2,1,0:T(8,128)S(1)}) custom-call(s32[3,4]{1,0:T(4,128)S(1)} %copy-done.6, s32[1]{0:T(128)} %bitcast.place, bf16[512,1024]{1,0:T(8,128)(2,1)S(1)} %copy-done, bf16[512,1024]{1,0:T(8,128)(2,1)S(1)} %copy-done.1, bf16[512,1024]{1,0:T(8,128)(2,1)S(1)} %copy-done.2, ...), custom_call_target="tpu_custom_call" | custom-call | flops 1 | bytes 1 | tf_op jit(solution)/shard_map/local_sums/pallas_call | solution.py:300
  11.1 1.2 %local_sums.6.after = f32[4,128,128]{2,1,0:T(8,128)S(1)} custom-call(s32[3,4]{1,0:T(4,128)S(1)} %copy-done.6, s32[1]{0:T(128)} %bitcast.place, bf16[512,1024]{1,0:T(8,128)(2,1)S(1)} %copy-done, bf16[512,1024]{1,0:T(8,128)(2,1)S(1)} %copy-done.1, bf16[512,1024]{1,0:T(8,128)(2,1)S(1)} %copy-done.2, bf16[512,1024]{1,0:T(8,128)(2,1)S(1)} %copy-done.3, ...), custom_call_target="tpu_custom_call" | custom-call | flops 1 | bytes 1 | tf_op jit(solution)/shard_map/local_sums/pallas_call | solution.py:300
  12.3 0.1 collective-permute-start
  12.4 1.1 %collective-permute-done.1.got_ref.refs_8_ = f32[4,128,128]{2,1,0:T(8,128)S(1)} collective-permute-done((f32[4,128,128]{2,1,0:T(8,128)}, f32[4,128,128]{2,1,0:T(8,128)S(1)}, u32[]{:S(2)}, u32[]{:S(2)}) %collective-permute-start.1) | collective-permute-done | bytes 262176 | tf_op jit(solution)/shard_map/ppermute | solution.py:565
  13.5 0.6 %join.4.after = f32[4,128,128]{2,1,0:T(8,128)S(1)} custom-call(s32[3,4]{1,0:T(4,128)S(1)} %copy-done.6, s32[1]{0:T(128)} %bitcast.place, f32[4,128,128]{2,1,0:T(8,128)S(1)} %collective-permute-done.1.got_ref.refs_8_, f32[4,128,128]{2,1,0:T(8,128)S(1)} %get-tuple-element.28.after.own_ref, f32[4,128,128]{2,1,0:T(8,128)S(1)} %local_sums.6.after), custom_call_target="tpu_custom_call" | custom-call | flops 1 | bytes 1 | tf_op jit(solution)/shard_map/join/pallas_call | solution.py:337
  14.1 0.0 copy-start.4
  14.1 4.0 %collective-permute-start.3 = (f32[4,128,128]{2,1,0:T(8,128)S(1)}, f32[4,128,128]{2,1,0:T(8,128)S(1)}, u32[]{:S(2)}, u32[]{:S(2)}) collective-permute-start(f32[4,128,128]{2,1,0:T(8,128)S(1)} %join.4.after), channel_id=1, source_target_pairs={{0,12},{4,8},{8,4},{12,0},{1,13},{5,9},{9,5},{13,1},{2,14},{6,10},... | collective-permute-start | bytes 786440 | tf_op jit(solution)/shard_map/ppermute | solution.py:585
  18.1 1.9 %local_sums.7 = (f32[4,128,128]{2,1,0:T(8,128)S(1)}, f32[4,128,128]{2,1,0:T(8,128)S(1)}) custom-call(s32[3,4]{1,0:T(4,128)S(1)} %copy-done.6, s32[1]{0:T(128)} %bitcast.place, bf16[512,1024]{1,0:T(8,128)(2,1)S(1)} %copy-done, bf16[512,1024]{1,0:T(8,128)(2,1)S(1)} %copy-done.1, bf16[512,1024]{1,0:T(8,128)(2,1)S(1)} %copy-done.2, ...), custom_call_target="tpu_custom_call" | custom-call | flops 1 | bytes 1 | tf_op jit(solution)/shard_map/local_sums/pallas_call | solution.py:300
  20.1 0.0 copy-done.4
  20.1 4.4 %inside_products.2 = (bf16[512,1024]{1,0:T(8,128)(2,1)S(1)}, bf16[512,1024]{1,0:T(8,128)(2,1)S(1)}, bf16[512,1024]{1,0:T(8,128)(2,1)S(1)}, bf16[512,1024]{1,0:T(8,128)(2,1)S(1)}) custom-call(s32[3,4]{1,0:T(4,128)S(1)} %copy-done.6, s32[1]{0:T(128)} %bitcast.place, bf16[512,1024]{1,0:T(8,128)(2,1)S(1)} %copy-done, bf16[512,1024]{1,0:T(8,128)(2,1)S(1)} %copy-done.1, ...), custom_call_target="tpu_custom_call" | custom-call | flops 1 | bytes 1 | tf_op jit(solution)/shard_map/inside_products/pallas_call | solution.py:412
  24.5 0.0 collective-permute-done.got_ref.refs_8_
  24.5 0.6 %join.5.refs_0_ = f32[4,128,128]{2,1,0:T(8,128)S(1)} custom-call(s32[3,4]{1,0:T(4,128)S(1)} %copy-done.6, s32[1]{0:T(128)} %bitcast.place, f32[4,128,128]{2,1,0:T(8,128)S(1)} %collective-permute-done.got_ref.refs_8_, f32[4,128,128]{2,1,0:T(8,128)S(1)} %get-tuple-element.29.own_ref, bf16[512,1024]{1,0:T(8,128)(2,1)S(1)} %get-tuple-element.31.after.refs_1_), custom_call_target="tpu_custom_call" | custom-call | flops 1 | bytes 1 | tf_op jit(solution)/shard_map/join/pallas_call | solution.py:337
  25.1 4.2 %collective-permute-start.2 = (f32[4,128,128]{2,1,0:T(8,128)S(1)}, f32[4,128,128]{2,1,0:T(8,128)S(1)}, u32[]{:S(2)}, u32[]{:S(2)}) collective-permute-start(f32[4,128,128]{2,1,0:T(8,128)S(1)} %join.5.refs_0_), channel_id=1, source_target_pairs={{0,12},{4,8},{8,4},{12,0},{1,13},{5,9},{9,5},{13,1},{2,14},{6,10},... | collective-permute-start | bytes 786440 | tf_op jit(solution)/shard_map/ppermute | solution.py:585
  29.3 4.4 %inside_products.3 = (bf16[512,1024]{1,0:T(8,128)(2,1)S(1)}, bf16[512,1024]{1,0:T(8,128)(2,1)S(1)}, bf16[512,1024]{1,0:T(8,128)(2,1)S(1)}, bf16[512,1024]{1,0:T(8,128)(2,1)S(1)}) custom-call(s32[3,4]{1,0:T(4,128)S(1)} %copy-done.6, s32[1]{0:T(128)} %bitcast.place, ...), custom_call_target="tpu_custom_call", output_to_operand_aliasing={{0}: (7, {}), {1}: (8, {}), {2}: (9, {}), {3}: (10, {})} | custom-call | flops 1 | bytes 1 | tf_op jit(solution)/shard_map/inside_products/pallas_call | solution.py:412
  33.7 0.0 collective-permute-done.3.got_ref.refs_9_
  33.7 0.6 %join.6.refs_10_ = f32[4,128,128]{2,1,0:T(8,128)S(1)} custom-call(s32[3,4]{1,0:T(4,128)S(1)} %copy-done.6, s32[1]{0:T(128)} %bitcast.place, f32[4,128,128]{2,1,0:T(8,128)S(1)} %collective-permute-done.3.got_ref.refs_9_, f32[4,128,128]{2,1,0:T(8,128)S(1)} %get-tuple-element.30.refs_0_.own_ref, bf16[512,1024]{1,0:T(8,128)(2,1)S(1)} %get-tuple-element.35.after.refs_4_), custom_call_target="tpu_custom_call" | custom-call | flops 1 | bytes 1 | tf_op jit(solution)/shard_map/join/pallas_call | solution.py:337
  34.3 0.8 %collective-permute-start.5 = (f32[4,128,128]{2,1,0:T(8,128)S(1)}, f32[4,128,128]{2,1,0:T(8,128)S(1)}, u32[]{:S(2)}, u32[]{:S(2)}) collective-permute-start(f32[4,128,128]{2,1,0:T(8,128)S(1)} %join.6.refs_10_), channel_id=1, source_target_pairs={{0,4},{4,0},{8,12},{12,8},{1,5},{5,1},{9,13},{13,9},{2,6},{6,2},{1... | collective-permute-start | bytes 786440 | tf_op jit(solution)/shard_map/ppermute | solution.py:588
  35.1 2.5 %base_products.2 = (f32[512,512]{1,0:T(8,128)S(1)}, f32[512,512]{1,0:T(8,128)S(1)}, f32[512,512]{1,0:T(8,128)S(1)}, f32[512,512]{1,0:T(8,128)S(1)}) custom-call(s32[3,4]{1,0:T(4,128)S(1)} %copy-done.6, s32[1]{0:T(128)} %bitcast.place, bf16[512,1024]{1,0:T(8,128)(2,1)S(1)} %copy-done, bf16[512,1024]{1,0:T(8,128)(2,1)S(1)} %copy-done.1, ...), custom_call_target="tpu_custom_call" | custom-call | flops 1 | bytes 1 | tf_op jit(solution)/shard_map/base_products/pallas_call | solution.py:459
  37.6 0.0 collective-permute-done.2.got_ref.refs_9_
  37.6 0.8 %join.7.refs_10_ = f32[4,128,128]{2,1,0:T(8,128)S(1)} custom-call(s32[3,4]{1,0:T(4,128)S(1)} %copy-done.6, s32[1]{0:T(128)} %bitcast.place, f32[4,128,128]{2,1,0:T(8,128)S(1)} %collective-permute-done.2.got_ref.refs_9_, f32[4,128,128]{2,1,0:T(8,128)S(1)} %get-tuple-element.39.own_ref, f32[512,512]{1,0:T(8,128)S(1)} %get-tuple-element.40.after.refs_4_), custom_call_target="tpu_custom_call" | custom-call | flops 1 | bytes 1 | tf_op jit(solution)/shard_map/join/pallas_call | solution.py:337
  38.4 2.4 %collective-permute-start.4 = (f32[4,128,128]{2,1,0:T(8,128)S(1)}, f32[4,128,128]{2,1,0:T(8,128)S(1)}, u32[]{:S(2)}, u32[]{:S(2)}) collective-permute-start(f32[4,128,128]{2,1,0:T(8,128)S(1)} %join.7.refs_10_), channel_id=1, source_target_pairs={{0,4},{4,0},{8,12},{12,8},{1,5},{5,1},{9,13},{13,9},{2,6},{6,2},{1... | collective-permute-start | bytes 786440 | tf_op jit(solution)/shard_map/ppermute | solution.py:588
  40.8 2.5 %base_products.3 = (f32[512,512]{1,0:T(8,128)S(1)}, f32[512,512]{1,0:T(8,128)S(1)}, f32[512,512]{1,0:T(8,128)S(1)}, f32[512,512]{1,0:T(8,128)S(1)}) custom-call(s32[3,4]{1,0:T(4,128)S(1)} %copy-done.6, s32[1]{0:T(128)} %bitcast.place, bf16[512,1024]{1,0:T(8,128)(2,1)S(1)} %copy-done, bf16[512,1024]{1,0:T(8,128)(2,1)S(1)} %copy-done.1, ...), custom_call_target="tpu_custom_call" | custom-call | flops 1 | bytes 1 | tf_op jit(solution)/shard_map/base_products/pallas_call | solution.py:459
  43.3 0.0 collective-permute-done.5.refs_8_
  43.3 2.7 %final_products.2 = (bf16[512,1024]{1,0:T(8,128)(2,1)}, bf16[512,1024]{1,0:T(8,128)(2,1)}, bf16[512,1024]{1,0:T(8,128)(2,1)}, bf16[512,1024]{1,0:T(8,128)(2,1)}) custom-call(s32[3,4]{1,0:T(4,128)S(1)} %copy-done.6, s32[1]{0:T(128)} %bitcast.place, bf16[512,1024]{1,0:T(8,128)(2,1)S(1)} %copy-done, bf16[512,1024]{1,0:T(8,128)(2,1)S(1)} %copy-done.1, ...), custom_call_target="tpu_custom_call" | custom-call | flops 1 | bytes 1 | tf_op jit(solution)/shard_map/final_products/pallas_call | solution.py:531
  46.0 1.2 %collective-permute-done.4.refs_8_ = f32[4,128,128]{2,1,0:T(8,128)S(1)} collective-permute-done((f32[4,128,128]{2,1,0:T(8,128)S(1)}, f32[4,128,128]{2,1,0:T(8,128)S(1)}, u32[]{:S(2)}, u32[]{:S(2)}) %collective-permute-start.4) | collective-permute-done | bytes 262176 | tf_op jit(solution)/shard_map/ppermute | solution.py:588
  47.2 2.7 %final_products.3 = (bf16[512,1024]{1,0:T(8,128)(2,1)}, bf16[512,1024]{1,0:T(8,128)(2,1)}, bf16[512,1024]{1,0:T(8,128)(2,1)}, bf16[512,1024]{1,0:T(8,128)(2,1)}) custom-call(s32[3,4]{1,0:T(4,128)S(1)} %copy-done.6, s32[1]{0:T(128)} %bitcast.place, ...), custom_call_target="tpu_custom_call", output_to_operand_aliasing={{0}: (11, {}), {1}: (12, {}), {2}: (13, {}), {3}: (14, {})} | custom-call | flops 1 | bytes 1 | tf_op jit(solution)/shard_map/final_products/pallas_call | solution.py:531
Async XLA Ops:
  0.6 6.3 %copy-start = (bf16[512,1024]{1,0:T(8,128)(2,1)S(1)}, bf16[512,1024]{1,0:T(8,128)(2,1)}, u32[]{:S(2)}) copy-start(bf16[512,1024]{1,0:T(8,128)(2,1)} %refs_0_.7) | copy-start | bytes 3145732
  0.6 6.3 %copy-start.1 = (bf16[512,1024]{1,0:T(8,128)(2,1)S(1)}, bf16[512,1024]{1,0:T(8,128)(2,1)}, u32[]{:S(2)}) copy-start(bf16[512,1024]{1,0:T(8,128)(2,1)} %refs_1_.7) | copy-start | bytes 3145732
  0.7 6.3 %copy-start.2 = (bf16[512,1024]{1,0:T(8,128)(2,1)S(1)}, bf16[512,1024]{1,0:T(8,128)(2,1)}, u32[]{:S(2)}) copy-start(bf16[512,1024]{1,0:T(8,128)(2,1)} %refs_2_.7) | copy-start | bytes 3145732
  0.7 6.3 %copy-start.6 = (s32[3,4]{1,0:T(4,128)S(1)}, s32[3,4]{1,0:T(4,128)}, u32[]{:S(2)}) copy-start(s32[3,4]{1,0:T(4,128)} %pack.27) | copy-start | bytes 148
  3.9 9.6 %collective-permute-start.1 = (f32[4,128,128]{2,1,0:T(8,128)}, f32[4,128,128]{2,1,0:T(8,128)S(1)}, u32[]{:S(2)}, u32[]{:S(2)}) collective-permute-start(f32[4,128,128]{2,1,0:T(8,128)} %local_sums.4.after), channel_id=1, source_target_pairs={{0,4},{4,0},{8,12},{12,8},{1,5},{5,1},{9,13},{13,9},{2,6},{6,2},{1... | collective-permute-start | bytes 786440 | tf_op jit(solution)/shard_map/ppermute | solution.py:565
  7.0 1.2 %copy-start.3 = (bf16[512,1024]{1,0:T(8,128)(2,1)S(1)}, bf16[512,1024]{1,0:T(8,128)(2,1)}, u32[]{:S(2)}) copy-start(bf16[512,1024]{1,0:T(8,128)(2,1)} %refs_3_.7) | copy-start | bytes 3145732
  8.2 0.9 %copy-start.5 = (f32[4,128,128]{2,1,0:T(8,128)S(1)}, f32[4,128,128]{2,1,0:T(8,128)}, u32[]{:S(2)}) copy-start(f32[4,128,128]{2,1,0:T(8,128)} %local_sums.4.after) | copy-start | bytes 786436
  12.3 12.1 %collective-permute-start = (f32[4,128,128]{2,1,0:T(8,128)S(1)}, f32[4,128,128]{2,1,0:T(8,128)S(1)}, u32[]{:S(2)}, u32[]{:S(2)}) collective-permute-start(f32[4,128,128]{2,1,0:T(8,128)S(1)} %local_sums.6.after), channel_id=1, source_target_pairs={{0,4},{4,0},{8,12},{12,8},{1,5},{5,1},{9,13},{13,9},{2,6},{6,2},{1... | collective-permute-start | bytes 786440 | tf_op jit(solution)/shard_map/ppermute | solution.py:565
  14.1 6.0 %copy-start.4 = (bf16[512,1024]{1,0:T(8,128)(2,1)S(1)}, bf16[512,1024]{1,0:T(8,128)(2,1)}, u32[]{:S(2)}) copy-start(bf16[512,1024]{1,0:T(8,128)(2,1)} %refs_3_.7) | copy-start | bytes 3145732
  14.1 19.6 %collective-permute-start.3 = (f32[4,128,128]{2,1,0:T(8,128)S(1)}, f32[4,128,128]{2,1,0:T(8,128)S(1)}, u32[]{:S(2)}, u32[]{:S(2)}) collective-permute-start(f32[4,128,128]{2,1,0:T(8,128)S(1)} %join.4.after), channel_id=1, source_target_pairs={{0,12},{4,8},{8,4},{12,0},{1,13},{5,9},{9,5},{13,1},{2,14},{6,10},... | collective-permute-start | bytes 786440 | tf_op jit(solution)/shard_map/ppermute | solution.py:585
  25.1 12.5 %collective-permute-start.2 = (f32[4,128,128]{2,1,0:T(8,128)S(1)}, f32[4,128,128]{2,1,0:T(8,128)S(1)}, u32[]{:S(2)}, u32[]{:S(2)}) collective-permute-start(f32[4,128,128]{2,1,0:T(8,128)S(1)} %join.5.refs_0_), channel_id=1, source_target_pairs={{0,12},{4,8},{8,4},{12,0},{1,13},{5,9},{9,5},{13,1},{2,14},{6,10},... | collective-permute-start | bytes 786440 | tf_op jit(solution)/shard_map/ppermute | solution.py:585
  34.3 9.0 %collective-permute-start.5 = (f32[4,128,128]{2,1,0:T(8,128)S(1)}, f32[4,128,128]{2,1,0:T(8,128)S(1)}, u32[]{:S(2)}, u32[]{:S(2)}) collective-permute-start(f32[4,128,128]{2,1,0:T(8,128)S(1)} %join.6.refs_10_), channel_id=1, source_target_pairs={{0,4},{4,0},{8,12},{12,8},{1,5},{5,1},{9,13},{13,9},{2,6},{6,2},{1... | collective-permute-start | bytes 786440 | tf_op jit(solution)/shard_map/ppermute | solution.py:588
  38.4 8.8 %collective-permute-start.4 = (f32[4,128,128]{2,1,0:T(8,128)S(1)}, f32[4,128,128]{2,1,0:T(8,128)S(1)}, u32[]{:S(2)}, u32[]{:S(2)}) collective-permute-start(f32[4,128,128]{2,1,0:T(8,128)S(1)} %join.7.refs_10_), channel_id=1, source_target_pairs={{0,4},{4,0},{8,12},{12,8},{1,5},{5,1},{9,13},{13,9},{2,6},{6,2},{1... | collective-permute-start | bytes 786440 | tf_op jit(solution)/shard_map/ppermute | solution.py:588

commit v5 on v4

--- a/solution.py
+++ b/solution.py
@@ -15,9 +15,9 @@
 IN_SIZES = (4, 4)
 ORDER = (
     ("one", 0),
-    ("own_two", 0),
     ("early", 0),
     ("one", 1),
+    ("own_two", 0),
     ("two", 0),
     ("own_three", 0),
     ("in", 0),

time: 50.3 us -> 49.6 us (0.986)
    ppermute x2, waiting for transfers between devices: 1.05 us -> 1.88 us  [exchange_body(): one[c] = lax.ppermute(early[c], 'seq', near)]
    ppermute x2, starting transfers between devices: 8.23 us -> 7.5 us  [exchange_body(): two[c] = lax.ppermute(last, 'seq', across)]
    ppermute x2, waiting for transfers between devices: 1.21 us -> 0.53 us  [exchange_body(): three[c] = lax.ppermute(last, 'seq', near)]
where the time goes in v5:
time: 49.6 us; the launch traced here: 49.4 us
  Pallas kernels  29.5 us (59%)
  starting transfers between devices  14.2 us (29%)
  waiting for transfers between devices  2.42 us (5%)
  local copies, waits for them, and re-layouts  2.19 us (4%)
  between operations  0.99 us (2%)
    pallas_call x2, Pallas kernels, inside_products(): pl.pallas_call(functools.partial(inside_kernel, per), out_shape=[jax.Shap...  8.75 us
    pallas_call x4, Pallas kernels, local_sums(): pl.pallas_call(functools.partial(sums_kernel, messages, first, sizes), ou...  8.29 us
    ppermute x2, starting transfers between devices, exchange_body(): two[c] = lax.ppermute(last, 'seq', across)  7.5 us
    pallas_call x2, Pallas kernels, final_products(): pl.pallas_call(functools.partial(final_kernel, first, heads), out_shape=[...  5.09 us
    pallas_call x2, Pallas kernels, base_products(): pl.pallas_call(functools.partial(base_kernel, first, heads), out_shape=[j...  4.8 us
    ppermute x2, starting transfers between devices, exchange_body(): three[c] = lax.ppermute(last, 'seq', near)  3.54 us
    ppermute x2, starting transfers between devices, exchange_body(): one[c] = lax.ppermute(early[c], 'seq', near)  3.19 us
    pallas_call x4, Pallas kernels, join(): pl.pallas_call(functools.partial(join_kernel, message), out_shape=jax.Sha...  2.61 us
  transfers between devices with their start and end apart: 6, of which 2 were waited for; matrix products, arithmetic and copies ran while one was open for 0% of the time, Pallas kernels for 48%

profile of v5, /device:TPU:0, one launch (start us, length us, event | category | flops | bytes accessed | tf_op | source)
XLA Modules:
  0.0 49.4 jit_solution(995008964629401256)
XLA Ops:
  0.6 0.0 copy-start
  0.6 0.0 copy-start.1
  0.7 0.0 copy-start.2
  0.7 0.0 copy-start.6
  0.7 3.2 %local_sums.4.after = f32[4,128,128]{2,1,0:T(8,128)} custom-call(s32[3,4]{1,0:T(4,128)} %pack.27, s32[1]{0:T(128)} %bitcast.place, bf16[512,1024]{1,0:T(8,128)(2,1)} %refs_0_.7, bf16[512,1024]{1,0:T(8,128)(2,1)} %refs_1_.7, bf16[512,1024]{1,0:T(8,128)(2,1)} %refs_2_.7, bf16[512,1024]{1,0:T(8,128)(2,1)} %refs_3_.7, s32[3,4]{1,0:T(4,128)} %pack.27), custom_call_target="tpu_custom_call" | custom-call | flops 1 | bytes 1 | tf_op jit(solution)/shard_map/local_sums/pallas_call | solution.py:300
  3.9 3.1 %collective-permute-start.1 = (f32[4,128,128]{2,1,0:T(8,128)}, f32[4,128,128]{2,1,0:T(8,128)S(1)}, u32[]{:S(2)}, u32[]{:S(2)}) collective-permute-start(f32[4,128,128]{2,1,0:T(8,128)} %local_sums.4.after), channel_id=1, source_target_pairs={{0,4},{4,0},{8,12},{12,8},{1,5},{5,1},{9,13},{13,9},{2,6},{6,2},{1... | collective-permute-start | bytes 786440 | tf_op jit(solution)/shard_map/ppermute | solution.py:565
  7.0 0.0 copy-done
  7.0 0.0 copy-done.1
  7.0 0.0 copy-done.2
  7.0 0.0 copy-done.6
  7.0 0.0 copy-start.3
  7.0 1.2 %copy-done.3 = bf16[512,1024]{1,0:T(8,128)(2,1)S(1)} copy-done((bf16[512,1024]{1,0:T(8,128)(2,1)S(1)}, bf16[512,1024]{1,0:T(8,128)(2,1)}, u32[]{:S(2)}) %copy-start.3) | copy-done | bytes 1048600
  8.2 0.0 copy-start.5
  8.2 0.9 %copy-done.5 = f32[4,128,128]{2,1,0:T(8,128)S(1)} copy-done((f32[4,128,128]{2,1,0:T(8,128)S(1)}, f32[4,128,128]{2,1,0:T(8,128)}, u32[]{:S(2)}) %copy-start.5) | copy-done | bytes 262168
  9.2 1.2 %local_sums.5.after = f32[4,128,128]{2,1,0:T(8,128)S(1)} custom-call(s32[3,4]{1,0:T(4,128)S(1)} %copy-done.6, s32[1]{0:T(128)} %bitcast.place, bf16[512,1024]{1,0:T(8,128)(2,1)S(1)} %copy-done, bf16[512,1024]{1,0:T(8,128)(2,1)S(1)} %copy-done.1, bf16[512,1024]{1,0:T(8,128)(2,1)S(1)} %copy-done.2, bf16[512,1024]{1,0:T(8,128)(2,1)S(1)} %copy-done.3, ...), custom_call_target="tpu_custom_call" | custom-call | flops 1 | bytes 1 | tf_op jit(solution)/shard_map/local_sums/pallas_call | solution.py:300
  10.4 0.1 collective-permute-start
  10.5 1.9 %local_sums.6 = (f32[4,128,128]{2,1,0:T(8,128)S(1)}, f32[4,128,128]{2,1,0:T(8,128)S(1)}) custom-call(s32[3,4]{1,0:T(4,128)S(1)} %copy-done.6, s32[1]{0:T(128)} %bitcast.place, bf16[512,1024]{1,0:T(8,128)(2,1)S(1)} %copy-done, bf16[512,1024]{1,0:T(8,128)(2,1)S(1)} %copy-done.1, bf16[512,1024]{1,0:T(8,128)(2,1)S(1)} %copy-done.2, ...), custom_call_target="tpu_custom_call" | custom-call | flops 1 | bytes 1 | tf_op jit(solution)/shard_map/local_sums/pallas_call | solution.py:300
  12.4 1.9 %collective-permute-done.1.got_ref.refs_8_ = f32[4,128,128]{2,1,0:T(8,128)S(1)} collective-permute-done((f32[4,128,128]{2,1,0:T(8,128)}, f32[4,128,128]{2,1,0:T(8,128)S(1)}, u32[]{:S(2)}, u32[]{:S(2)}) %collective-permute-start.1) | collective-permute-done | bytes 262176 | tf_op jit(solution)/shard_map/ppermute | solution.py:565
  14.3 0.6 %join.4.after = f32[4,128,128]{2,1,0:T(8,128)S(1)} custom-call(s32[3,4]{1,0:T(4,128)S(1)} %copy-done.6, s32[1]{0:T(128)} %bitcast.place, f32[4,128,128]{2,1,0:T(8,128)S(1)} %collective-permute-done.1.got_ref.refs_8_, f32[4,128,128]{2,1,0:T(8,128)S(1)} %get-tuple-element.29.own_ref.after, f32[4,128,128]{2,1,0:T(8,128)S(1)} %get-tuple-element.29.own_ref.after), custom_call_target="tpu_custom_call" | custom-call | flops 1 | bytes 1 | tf_op jit(solution)/shard_map/join/pallas_call | solution.py:337
  14.9 0.0 copy-start.4
  14.9 4.2 %collective-permute-start.3 = (f32[4,128,128]{2,1,0:T(8,128)S(1)}, f32[4,128,128]{2,1,0:T(8,128)S(1)}, u32[]{:S(2)}, u32[]{:S(2)}) collective-permute-start(f32[4,128,128]{2,1,0:T(8,128)S(1)} %join.4.after), channel_id=1, source_target_pairs={{0,12},{4,8},{8,4},{12,0},{1,13},{5,9},{9,5},{13,1},{2,14},{6,10},... | collective-permute-start | bytes 786440 | tf_op jit(solution)/shard_map/ppermute | solution.py:585
  19.1 1.9 %local_sums.7 = (f32[4,128,128]{2,1,0:T(8,128)S(1)}, f32[4,128,128]{2,1,0:T(8,128)S(1)}) custom-call(s32[3,4]{1,0:T(4,128)S(1)} %copy-done.6, s32[1]{0:T(128)} %bitcast.place, bf16[512,1024]{1,0:T(8,128)(2,1)S(1)} %copy-done, bf16[512,1024]{1,0:T(8,128)(2,1)S(1)} %copy-done.1, bf16[512,1024]{1,0:T(8,128)(2,1)S(1)} %copy-done.2, ...), custom_call_target="tpu_custom_call" | custom-call | flops 1 | bytes 1 | tf_op jit(solution)/shard_map/local_sums/pallas_call | solution.py:300
  21.1 0.0 copy-done.4
  21.1 4.4 %inside_products.2 = (bf16[512,1024]{1,0:T(8,128)(2,1)S(1)}, bf16[512,1024]{1,0:T(8,128)(2,1)S(1)}, bf16[512,1024]{1,0:T(8,128)(2,1)S(1)}, bf16[512,1024]{1,0:T(8,128)(2,1)S(1)}) custom-call(s32[3,4]{1,0:T(4,128)S(1)} %copy-done.6, s32[1]{0:T(128)} %bitcast.place, bf16[512,1024]{1,0:T(8,128)(2,1)S(1)} %copy-done, bf16[512,1024]{1,0:T(8,128)(2,1)S(1)} %copy-done.1, ...), custom_call_target="tpu_custom_call" | custom-call | flops 1 | bytes 1 | tf_op jit(solution)/shard_map/inside_products/pallas_call | solution.py:412
  25.5 0.0 collective-permute-done.got_ref.refs_8_
  25.5 0.6 %join.5.refs_0_ = f32[4,128,128]{2,1,0:T(8,128)S(1)} custom-call(s32[3,4]{1,0:T(4,128)S(1)} %copy-done.6, s32[1]{0:T(128)} %bitcast.place, f32[4,128,128]{2,1,0:T(8,128)S(1)} %collective-permute-done.got_ref.refs_8_, f32[4,128,128]{2,1,0:T(8,128)S(1)} %get-tuple-element.28.own_ref, bf16[512,1024]{1,0:T(8,128)(2,1)S(1)} %get-tuple-element.31.after.refs_1_), custom_call_target="tpu_custom_call" | custom-call | flops 1 | bytes 1 | tf_op jit(solution)/shard_map/join/pallas_call | solution.py:337
  26.1 3.3 %collective-permute-start.2 = (f32[4,128,128]{2,1,0:T(8,128)S(1)}, f32[4,128,128]{2,1,0:T(8,128)S(1)}, u32[]{:S(2)}, u32[]{:S(2)}) collective-permute-start(f32[4,128,128]{2,1,0:T(8,128)S(1)} %join.5.refs_0_), channel_id=1, source_target_pairs={{0,12},{4,8},{8,4},{12,0},{1,13},{5,9},{9,5},{13,1},{2,14},{6,10},... | collective-permute-start | bytes 786440 | tf_op jit(solution)/shard_map/ppermute | solution.py:585
  29.4 4.4 %inside_products.3 = (bf16[512,1024]{1,0:T(8,128)(2,1)S(1)}, bf16[512,1024]{1,0:T(8,128)(2,1)S(1)}, bf16[512,1024]{1,0:T(8,128)(2,1)S(1)}, bf16[512,1024]{1,0:T(8,128)(2,1)S(1)}) custom-call(s32[3,4]{1,0:T(4,128)S(1)} %copy-done.6, s32[1]{0:T(128)} %bitcast.place, ...), custom_call_target="tpu_custom_call", output_to_operand_aliasing={{0}: (7, {}), {1}: (8, {}), {2}: (9, {}), {3}: (10, {})} | custom-call | flops 1 | bytes 1 | tf_op jit(solution)/shard_map/inside_products/pallas_call | solution.py:412
  33.8 0.0 collective-permute-done.3.got_ref.refs_9_
  33.8 0.6 %join.6.refs_10_ = f32[4,128,128]{2,1,0:T(8,128)S(1)} custom-call(s32[3,4]{1,0:T(4,128)S(1)} %copy-done.6, s32[1]{0:T(128)} %bitcast.place, f32[4,128,128]{2,1,0:T(8,128)S(1)} %collective-permute-done.3.got_ref.refs_9_, f32[4,128,128]{2,1,0:T(8,128)S(1)} %get-tuple-element.30.refs_0_.own_ref, bf16[512,1024]{1,0:T(8,128)(2,1)S(1)} %get-tuple-element.35.after.refs_4_), custom_call_target="tpu_custom_call" | custom-call | flops 1 | bytes 1 | tf_op jit(solution)/shard_map/join/pallas_call | solution.py:337
  34.4 2.4 %collective-permute-start.5 = (f32[4,128,128]{2,1,0:T(8,128)S(1)}, f32[4,128,128]{2,1,0:T(8,128)S(1)}, u32[]{:S(2)}, u32[]{:S(2)}) collective-permute-start(f32[4,128,128]{2,1,0:T(8,128)S(1)} %join.6.refs_10_), channel_id=1, source_target_pairs={{0,4},{4,0},{8,12},{12,8},{1,5},{5,1},{9,13},{13,9},{2,6},{6,2},{1... | collective-permute-start | bytes 786440 | tf_op jit(solution)/shard_map/ppermute | solution.py:588
  36.8 2.4 %base_products.2 = (f32[512,512]{1,0:T(8,128)S(1)}, f32[512,512]{1,0:T(8,128)S(1)}, f32[512,512]{1,0:T(8,128)S(1)}, f32[512,512]{1,0:T(8,128)S(1)}) custom-call(s32[3,4]{1,0:T(4,128)S(1)} %copy-done.6, s32[1]{0:T(128)} %bitcast.place, bf16[512,1024]{1,0:T(8,128)(2,1)S(1)} %copy-done, bf16[512,1024]{1,0:T(8,128)(2,1)S(1)} %copy-done.1, ...), custom_call_target="tpu_custom_call" | custom-call | flops 1 | bytes 1 | tf_op jit(solution)/shard_map/base_products/pallas_call | solution.py:459
  39.2 0.0 collective-permute-done.2.got_ref.refs_9_
  39.2 0.8 %join.7.refs_10_ = f32[4,128,128]{2,1,0:T(8,128)S(1)} custom-call(s32[3,4]{1,0:T(4,128)S(1)} %copy-done.6, s32[1]{0:T(128)} %bitcast.place, f32[4,128,128]{2,1,0:T(8,128)S(1)} %collective-permute-done.2.got_ref.refs_9_, f32[4,128,128]{2,1,0:T(8,128)S(1)} %get-tuple-element.39.own_ref, f32[512,512]{1,0:T(8,128)S(1)} %get-tuple-element.40.after.refs_4_), custom_call_target="tpu_custom_call" | custom-call | flops 1 | bytes 1 | tf_op jit(solution)/shard_map/join/pallas_call | solution.py:337
  40.0 1.2 %collective-permute-start.4 = (f32[4,128,128]{2,1,0:T(8,128)S(1)}, f32[4,128,128]{2,1,0:T(8,128)S(1)}, u32[]{:S(2)}, u32[]{:S(2)}) collective-permute-start(f32[4,128,128]{2,1,0:T(8,128)S(1)} %join.7.refs_10_), channel_id=1, source_target_pairs={{0,4},{4,0},{8,12},{12,8},{1,5},{5,1},{9,13},{13,9},{2,6},{6,2},{1... | collective-permute-start | bytes 786440 | tf_op jit(solution)/shard_map/ppermute | solution.py:588
  41.2 2.4 %base_products.3 = (f32[512,512]{1,0:T(8,128)S(1)}, f32[512,512]{1,0:T(8,128)S(1)}, f32[512,512]{1,0:T(8,128)S(1)}, f32[512,512]{1,0:T(8,128)S(1)}) custom-call(s32[3,4]{1,0:T(4,128)S(1)} %copy-done.6, s32[1]{0:T(128)} %bitcast.place, bf16[512,1024]{1,0:T(8,128)(2,1)S(1)} %copy-done, bf16[512,1024]{1,0:T(8,128)(2,1)S(1)} %copy-done.1, ...), custom_call_target="tpu_custom_call" | custom-call | flops 1 | bytes 1 | tf_op jit(solution)/shard_map/base_products/pallas_call | solution.py:459
  43.6 0.0 collective-permute-done.5.refs_8_
  43.6 2.6 %final_products.2 = (bf16[512,1024]{1,0:T(8,128)(2,1)}, bf16[512,1024]{1,0:T(8,128)(2,1)}, bf16[512,1024]{1,0:T(8,128)(2,1)}, bf16[512,1024]{1,0:T(8,128)(2,1)}) custom-call(s32[3,4]{1,0:T(4,128)S(1)} %copy-done.6, s32[1]{0:T(128)} %bitcast.place, bf16[512,1024]{1,0:T(8,128)(2,1)S(1)} %copy-done, bf16[512,1024]{1,0:T(8,128)(2,1)S(1)} %copy-done.1, ...), custom_call_target="tpu_custom_call" | custom-call | flops 1 | bytes 1 | tf_op jit(solution)/shard_map/final_products/pallas_call | solution.py:531
  46.2 0.5 %collective-permute-done.4.refs_8_ = f32[4,128,128]{2,1,0:T(8,128)S(1)} collective-permute-done((f32[4,128,128]{2,1,0:T(8,128)S(1)}, f32[4,128,128]{2,1,0:T(8,128)S(1)}, u32[]{:S(2)}, u32[]{:S(2)}) %collective-permute-start.4) | collective-permute-done | bytes 262176 | tf_op jit(solution)/shard_map/ppermute | solution.py:588
  46.8 2.5 %final_products.3 = (bf16[512,1024]{1,0:T(8,128)(2,1)}, bf16[512,1024]{1,0:T(8,128)(2,1)}, bf16[512,1024]{1,0:T(8,128)(2,1)}, bf16[512,1024]{1,0:T(8,128)(2,1)}) custom-call(s32[3,4]{1,0:T(4,128)S(1)} %copy-done.6, s32[1]{0:T(128)} %bitcast.place, ...), custom_call_target="tpu_custom_call", output_to_operand_aliasing={{0}: (11, {}), {1}: (12, {}), {2}: (13, {}), {3}: (14, {})} | custom-call | flops 1 | bytes 1 | tf_op jit(solution)/shard_map/final_products/pallas_call | solution.py:531
Async XLA Ops:
  0.6 6.3 %copy-start = (bf16[512,1024]{1,0:T(8,128)(2,1)S(1)}, bf16[512,1024]{1,0:T(8,128)(2,1)}, u32[]{:S(2)}) copy-start(bf16[512,1024]{1,0:T(8,128)(2,1)} %refs_0_.7) | copy-start | bytes 3145732
  0.6 6.3 %copy-start.1 = (bf16[512,1024]{1,0:T(8,128)(2,1)S(1)}, bf16[512,1024]{1,0:T(8,128)(2,1)}, u32[]{:S(2)}) copy-start(bf16[512,1024]{1,0:T(8,128)(2,1)} %refs_1_.7) | copy-start | bytes 3145732
  0.7 6.3 %copy-start.2 = (bf16[512,1024]{1,0:T(8,128)(2,1)S(1)}, bf16[512,1024]{1,0:T(8,128)(2,1)}, u32[]{:S(2)}) copy-start(bf16[512,1024]{1,0:T(8,128)(2,1)} %refs_2_.7) | copy-start | bytes 3145732
  0.7 6.3 %copy-start.6 = (s32[3,4]{1,0:T(4,128)S(1)}, s32[3,4]{1,0:T(4,128)}, u32[]{:S(2)}) copy-start(s32[3,4]{1,0:T(4,128)} %pack.27) | copy-start | bytes 148
  3.9 10.4 %collective-permute-start.1 = (f32[4,128,128]{2,1,0:T(8,128)}, f32[4,128,128]{2,1,0:T(8,128)S(1)}, u32[]{:S(2)}, u32[]{:S(2)}) collective-permute-start(f32[4,128,128]{2,1,0:T(8,128)} %local_sums.4.after), channel_id=1, source_target_pairs={{0,4},{4,0},{8,12},{12,8},{1,5},{5,1},{9,13},{13,9},{2,6},{6,2},{1... | collective-permute-start | bytes 786440 | tf_op jit(solution)/shard_map/ppermute | solution.py:565
  7.0 1.2 %copy-start.3 = (bf16[512,1024]{1,0:T(8,128)(2,1)S(1)}, bf16[512,1024]{1,0:T(8,128)(2,1)}, u32[]{:S(2)}) copy-start(bf16[512,1024]{1,0:T(8,128)(2,1)} %refs_3_.7) | copy-start | bytes 3145732
  8.2 0.9 %copy-start.5 = (f32[4,128,128]{2,1,0:T(8,128)S(1)}, f32[4,128,128]{2,1,0:T(8,128)}, u32[]{:S(2)}) copy-start(f32[4,128,128]{2,1,0:T(8,128)} %local_sums.4.after) | copy-start | bytes 786436
  10.4 15.1 %collective-permute-start = (f32[4,128,128]{2,1,0:T(8,128)S(1)}, f32[4,128,128]{2,1,0:T(8,128)S(1)}, u32[]{:S(2)}, u32[]{:S(2)}) collective-permute-start(f32[4,128,128]{2,1,0:T(8,128)S(1)} %local_sums.5.after), channel_id=1, source_target_pairs={{0,4},{4,0},{8,12},{12,8},{1,5},{5,1},{9,13},{13,9},{2,6},{6,2},{1... | collective-permute-start | bytes 786440 | tf_op jit(solution)/shard_map/ppermute | solution.py:565
  14.9 6.1 %copy-start.4 = (bf16[512,1024]{1,0:T(8,128)(2,1)S(1)}, bf16[512,1024]{1,0:T(8,128)(2,1)}, u32[]{:S(2)}) copy-start(bf16[512,1024]{1,0:T(8,128)(2,1)} %refs_3_.7) | copy-start | bytes 3145732
  14.9 18.9 %collective-permute-start.3 = (f32[4,128,128]{2,1,0:T(8,128)S(1)}, f32[4,128,128]{2,1,0:T(8,128)S(1)}, u32[]{:S(2)}, u32[]{:S(2)}) collective-permute-start(f32[4,128,128]{2,1,0:T(8,128)S(1)} %join.4.after), channel_id=1, source_target_pairs={{0,12},{4,8},{8,4},{12,0},{1,13},{5,9},{9,5},{13,1},{2,14},{6,10},... | collective-permute-start | bytes 786440 | tf_op jit(solution)/shard_map/ppermute | solution.py:585
  26.1 13.1 %collective-permute-start.2 = (f32[4,128,128]{2,1,0:T(8,128)S(1)}, f32[4,128,128]{2,1,0:T(8,128)S(1)}, u32[]{:S(2)}, u32[]{:S(2)}) collective-permute-start(f32[4,128,128]{2,1,0:T(8,128)S(1)} %join.5.refs_0_), channel_id=1, source_target_pairs={{0,12},{4,8},{8,4},{12,0},{1,13},{5,9},{9,5},{13,1},{2,14},{6,10},... | collective-permute-start | bytes 786440 | tf_op jit(solution)/shard_map/ppermute | solution.py:585
  34.4 9.2 %collective-permute-start.5 = (f32[4,128,128]{2,1,0:T(8,128)S(1)}, f32[4,128,128]{2,1,0:T(8,128)S(1)}, u32[]{:S(2)}, u32[]{:S(2)}) collective-permute-start(f32[4,128,128]{2,1,0:T(8,128)S(1)} %join.6.refs_10_), channel_id=1, source_target_pairs={{0,4},{4,0},{8,12},{12,8},{1,5},{5,1},{9,13},{13,9},{2,6},{6,2},{1... | collective-permute-start | bytes 786440 | tf_op jit(solution)/shard_map/ppermute | solution.py:588
  40.0 6.8 %collective-permute-start.4 = (f32[4,128,128]{2,1,0:T(8,128)S(1)}, f32[4,128,128]{2,1,0:T(8,128)S(1)}, u32[]{:S(2)}, u32[]{:S(2)}) collective-permute-start(f32[4,128,128]{2,1,0:T(8,128)S(1)} %join.7.refs_10_), channel_id=1, source_target_pairs={{0,4},{4,0},{8,12},{12,8},{1,5},{5,1},{9,13},{13,9},{2,6},{6,2},{1... | collective-permute-start | bytes 786440 | tf_op jit(solution)/shard_map/ppermute | solution.py:588

commit v6 on v5

--- a/solution.py
+++ b/solution.py
@@ -19,9 +19,9 @@
     ("one", 1),
     ("own_two", 0),
     ("two", 0),
-    ("own_three", 0),
     ("in", 0),
     ("two", 1),
+    ("own_three", 0),
     ("in", 1),
     ("three", 0),
     ("base", 0),

time: 49.6 us -> 52.3 us (1.054)
  starting transfers between devices: 14.2 us -> 17.4 us
  waiting for transfers between devices: 2.42 us -> 1.88 us
    ppermute x2, starting transfers between devices: 7.5 us -> 12 us  [exchange_body(): two[c] = lax.ppermute(last, 'seq', across)]
    ppermute x2, starting transfers between devices: 3.54 us -> 2.14 us  [exchange_body(): three[c] = lax.ppermute(last, 'seq', near)]
    ppermute x2, waiting for transfers between devices: 0.53 us -> 0.01 us  [exchange_body(): three[c] = lax.ppermute(last, 'seq', near)]
  transfers between devices with their start and end apart: 6 -> 6, of which waited for: 2 -> 1; matrix products, arithmetic and copies ran while one was open for 0% -> 0% of each run, Pallas kernels for 48% -> 46%
where the time goes in v6:
time: 52.3 us; the launch traced here: 52.1 us
  Pallas kernels  29.6 us (57%)
  starting transfers between devices  17.4 us (33%)
  local copies, waits for them, and re-layouts  2.19 us (4%)
  waiting for transfers between devices  1.88 us (4%)
  between operations  1 us (2%)
    ppermute x2, starting transfers between devices, exchange_body(): two[c] = lax.ppermute(last, 'seq', across)  12 us
    pallas_call x2, Pallas kernels, inside_products(): pl.pallas_call(functools.partial(inside_kernel, per), out_shape=[jax.Shap...  8.75 us
    pallas_call x4, Pallas kernels, local_sums(): pl.pallas_call(functools.partial(sums_kernel, messages, first, sizes), ou...  8.29 us
    pallas_call x2, Pallas kernels, final_products(): pl.pallas_call(functools.partial(final_kernel, first, heads), out_shape=[...  5.11 us
    pallas_call x2, Pallas kernels, base_products(): pl.pallas_call(functools.partial(base_kernel, first, heads), out_shape=[j...  4.81 us
    ppermute x2, starting transfers between devices, exchange_body(): one[c] = lax.ppermute(early[c], 'seq', near)  3.19 us
    pallas_call x4, Pallas kernels, join(): pl.pallas_call(functools.partial(join_kernel, message), out_shape=jax.Sha...  2.66 us
    unnamed x14, local copies, waits for them, and re-layouts  2.19 us
  transfers between devices with their start and end apart: 6, of which 1 were waited for; matrix products, arithmetic and copies ran while one was open for 0% of the time, Pallas kernels for 46%

profile of v6, /device:TPU:0, one launch (start us, length us, event | category | flops | bytes accessed | tf_op | source)
XLA Modules:
  0.0 52.1 jit_solution(650999526364125659)
XLA Ops:
  0.6 0.0 copy-start
  0.6 0.0 copy-start.1
  0.7 0.0 copy-start.2
  0.7 0.0 copy-start.6
  0.7 3.2 %local_sums.4.after = f32[4,128,128]{2,1,0:T(8,128)} custom-call(s32[3,4]{1,0:T(4,128)} %pack.27, s32[1]{0:T(128)} %bitcast.place, bf16[512,1024]{1,0:T(8,128)(2,1)} %refs_0_.7, bf16[512,1024]{1,0:T(8,128)(2,1)} %refs_1_.7, bf16[512,1024]{1,0:T(8,128)(2,1)} %refs_2_.7, bf16[512,1024]{1,0:T(8,128)(2,1)} %refs_3_.7, s32[3,4]{1,0:T(4,128)} %pack.27), custom_call_target="tpu_custom_call" | custom-call | flops 1 | bytes 1 | tf_op jit(solution)/shard_map/local_sums/pallas_call | solution.py:300
  3.9 3.1 %collective-permute-start.1 = (f32[4,128,128]{2,1,0:T(8,128)}, f32[4,128,128]{2,1,0:T(8,128)S(1)}, u32[]{:S(2)}, u32[]{:S(2)}) collective-permute-start(f32[4,128,128]{2,1,0:T(8,128)} %local_sums.4.after), channel_id=1, source_target_pairs={{0,4},{4,0},{8,12},{12,8},{1,5},{5,1},{9,13},{13,9},{2,6},{6,2},{1... | collective-permute-start | bytes 786440 | tf_op jit(solution)/shard_map/ppermute | solution.py:565
  7.0 0.0 copy-done
  7.0 0.0 copy-done.1
  7.0 0.0 copy-done.2
  7.0 0.0 copy-done.6
  7.0 0.0 copy-start.3
  7.0 1.2 %copy-done.3 = bf16[512,1024]{1,0:T(8,128)(2,1)S(1)} copy-done((bf16[512,1024]{1,0:T(8,128)(2,1)S(1)}, bf16[512,1024]{1,0:T(8,128)(2,1)}, u32[]{:S(2)}) %copy-start.3) | copy-done | bytes 1048600
  8.2 0.0 copy-start.5
  8.2 0.9 %copy-done.5 = f32[4,128,128]{2,1,0:T(8,128)S(1)} copy-done((f32[4,128,128]{2,1,0:T(8,128)S(1)}, f32[4,128,128]{2,1,0:T(8,128)}, u32[]{:S(2)}) %copy-start.5) | copy-done | bytes 262168
  9.2 1.2 %local_sums.5.after = f32[4,128,128]{2,1,0:T(8,128)S(1)} custom-call(s32[3,4]{1,0:T(4,128)S(1)} %copy-done.6, s32[1]{0:T(128)} %bitcast.place, bf16[512,1024]{1,0:T(8,128)(2,1)S(1)} %copy-done, bf16[512,1024]{1,0:T(8,128)(2,1)S(1)} %copy-done.1, bf16[512,1024]{1,0:T(8,128)(2,1)S(1)} %copy-done.2, bf16[512,1024]{1,0:T(8,128)(2,1)S(1)} %copy-done.3, ...), custom_call_target="tpu_custom_call" | custom-call | flops 1 | bytes 1 | tf_op jit(solution)/shard_map/local_sums/pallas_call | solution.py:300
  10.4 0.1 collective-permute-start
  10.5 1.9 %local_sums.6 = (f32[4,128,128]{2,1,0:T(8,128)S(1)}, f32[4,128,128]{2,1,0:T(8,128)S(1)}) custom-call(s32[3,4]{1,0:T(4,128)S(1)} %copy-done.6, s32[1]{0:T(128)} %bitcast.place, bf16[512,1024]{1,0:T(8,128)(2,1)S(1)} %copy-done, bf16[512,1024]{1,0:T(8,128)(2,1)S(1)} %copy-done.1, bf16[512,1024]{1,0:T(8,128)(2,1)S(1)} %copy-done.2, ...), custom_call_target="tpu_custom_call" | custom-call | flops 1 | bytes 1 | tf_op jit(solution)/shard_map/local_sums/pallas_call | solution.py:300
  12.4 0.0 copy-start.4
  12.4 1.9 %collective-permute-done.1.got_ref.refs_8_ = f32[4,128,128]{2,1,0:T(8,128)S(1)} collective-permute-done((f32[4,128,128]{2,1,0:T(8,128)}, f32[4,128,128]{2,1,0:T(8,128)S(1)}, u32[]{:S(2)}, u32[]{:S(2)}) %collective-permute-start.1) | collective-permute-done | bytes 262176 | tf_op jit(solution)/shard_map/ppermute | solution.py:565
  14.3 0.6 %join.4.refs_0_ = f32[4,128,128]{2,1,0:T(8,128)S(1)} custom-call(s32[3,4]{1,0:T(4,128)S(1)} %copy-done.6, s32[1]{0:T(128)} %bitcast.place, f32[4,128,128]{2,1,0:T(8,128)S(1)} %collective-permute-done.1.got_ref.refs_8_, f32[4,128,128]{2,1,0:T(8,128)S(1)} %get-tuple-element.29.own_ref.after, f32[4,128,128]{2,1,0:T(8,128)S(1)} %get-tuple-element.29.own_ref.after), custom_call_target="tpu_custom_call" | custom-call | flops 1 | bytes 1 | tf_op jit(solution)/shard_map/join/pallas_call | solution.py:337
  14.9 4.2 %collective-permute-start.3 = (f32[4,128,128]{2,1,0:T(8,128)S(1)}, f32[4,128,128]{2,1,0:T(8,128)S(1)}, u32[]{:S(2)}, u32[]{:S(2)}) collective-permute-start(f32[4,128,128]{2,1,0:T(8,128)S(1)} %join.4.refs_0_), channel_id=1, source_target_pairs={{0,12},{4,8},{8,4},{12,0},{1,13},{5,9},{9,5},{13,1},{2,14},{6,10},... | collective-permute-start | bytes 786440 | tf_op jit(solution)/shard_map/ppermute | solution.py:585
  19.1 0.0 copy-done.4
  19.1 4.4 %inside_products.2 = (bf16[512,1024]{1,0:T(8,128)(2,1)S(1)}, bf16[512,1024]{1,0:T(8,128)(2,1)S(1)}, bf16[512,1024]{1,0:T(8,128)(2,1)S(1)}, bf16[512,1024]{1,0:T(8,128)(2,1)S(1)}) custom-call(s32[3,4]{1,0:T(4,128)S(1)} %copy-done.6, s32[1]{0:T(128)} %bitcast.place, bf16[512,1024]{1,0:T(8,128)(2,1)S(1)} %copy-done, bf16[512,1024]{1,0:T(8,128)(2,1)S(1)} %copy-done.1, ...), custom_call_target="tpu_custom_call" | custom-call | flops 1 | bytes 1 | tf_op jit(solution)/shard_map/inside_products/pallas_call | solution.py:412
  23.5 0.0 collective-permute-done.got_ref.refs_8_
  23.5 0.6 %join.5.after = f32[4,128,128]{2,1,0:T(8,128)S(1)} custom-call(s32[3,4]{1,0:T(4,128)S(1)} %copy-done.6, s32[1]{0:T(128)} %bitcast.place, f32[4,128,128]{2,1,0:T(8,128)S(1)} %collective-permute-done.got_ref.refs_8_, f32[4,128,128]{2,1,0:T(8,128)S(1)} %get-tuple-element.28.own_ref, bf16[512,1024]{1,0:T(8,128)(2,1)S(1)} %get-tuple-element.30.after.refs_1_), custom_call_target="tpu_custom_call" | custom-call | flops 1 | bytes 1 | tf_op jit(solution)/shard_map/join/pallas_call | solution.py:337
  24.1 7.9 %collective-permute-start.2 = (f32[4,128,128]{2,1,0:T(8,128)S(1)}, f32[4,128,128]{2,1,0:T(8,128)S(1)}, u32[]{:S(2)}, u32[]{:S(2)}) collective-permute-start(f32[4,128,128]{2,1,0:T(8,128)S(1)} %join.5.after), channel_id=1, source_target_pairs={{0,12},{4,8},{8,4},{12,0},{1,13},{5,9},{9,5},{13,1},{2,14},{6,10},... | collective-permute-start | bytes 786440 | tf_op jit(solution)/shard_map/ppermute | solution.py:585
  32.0 1.9 %local_sums.7 = (f32[4,128,128]{2,1,0:T(8,128)S(1)}, f32[4,128,128]{2,1,0:T(8,128)S(1)}) custom-call(s32[3,4]{1,0:T(4,128)S(1)} %copy-done.6, s32[1]{0:T(128)} %bitcast.place, bf16[512,1024]{1,0:T(8,128)(2,1)S(1)} %copy-done, bf16[512,1024]{1,0:T(8,128)(2,1)S(1)} %copy-done.1, bf16[512,1024]{1,0:T(8,128)(2,1)S(1)} %copy-done.2, ...), custom_call_target="tpu_custom_call" | custom-call | flops 1 | bytes 1 | tf_op jit(solution)/shard_map/local_sums/pallas_call | solution.py:300
  33.9 4.4 %inside_products.3 = (bf16[512,1024]{1,0:T(8,128)(2,1)S(1)}, bf16[512,1024]{1,0:T(8,128)(2,1)S(1)}, bf16[512,1024]{1,0:T(8,128)(2,1)S(1)}, bf16[512,1024]{1,0:T(8,128)(2,1)S(1)}) custom-call(s32[3,4]{1,0:T(4,128)S(1)} %copy-done.6, s32[1]{0:T(128)} %bitcast.place, ...), custom_call_target="tpu_custom_call", output_to_operand_aliasing={{0}: (7, {}), {1}: (8, {}), {2}: (9, {}), {3}: (10, {})} | custom-call | flops 1 | bytes 1 | tf_op jit(solution)/shard_map/inside_products/pallas_call | solution.py:412
  38.3 0.0 collective-permute-done.3.got_ref.refs_9_
  38.4 0.6 %join.6.refs_10_ = f32[4,128,128]{2,1,0:T(8,128)S(1)} custom-call(s32[3,4]{1,0:T(4,128)S(1)} %copy-done.6, s32[1]{0:T(128)} %bitcast.place, f32[4,128,128]{2,1,0:T(8,128)S(1)} %collective-permute-done.3.got_ref.refs_9_, f32[4,128,128]{2,1,0:T(8,128)S(1)} %get-tuple-element.31.refs_0_.own_ref, bf16[512,1024]{1,0:T(8,128)(2,1)S(1)} %get-tuple-element.35.after.refs_4_), custom_call_target="tpu_custom_call" | custom-call | flops 1 | bytes 1 | tf_op jit(solution)/shard_map/join/pallas_call | solution.py:337
  39.0 0.1 collective-permute-start.5
  39.1 2.4 %base_products.2 = (f32[512,512]{1,0:T(8,128)S(1)}, f32[512,512]{1,0:T(8,128)S(1)}, f32[512,512]{1,0:T(8,128)S(1)}, f32[512,512]{1,0:T(8,128)S(1)}) custom-call(s32[3,4]{1,0:T(4,128)S(1)} %copy-done.6, s32[1]{0:T(128)} %bitcast.place, bf16[512,1024]{1,0:T(8,128)(2,1)S(1)} %copy-done, bf16[512,1024]{1,0:T(8,128)(2,1)S(1)} %copy-done.1, ...), custom_call_target="tpu_custom_call" | custom-call | flops 1 | bytes 1 | tf_op jit(solution)/shard_map/base_products/pallas_call | solution.py:459
  41.5 0.0 collective-permute-done.2.got_ref.refs_9_
  41.5 0.8 %join.7.refs_10_ = f32[4,128,128]{2,1,0:T(8,128)S(1)} custom-call(s32[3,4]{1,0:T(4,128)S(1)} %copy-done.6, s32[1]{0:T(128)} %bitcast.place, f32[4,128,128]{2,1,0:T(8,128)S(1)} %collective-permute-done.2.got_ref.refs_9_, f32[4,128,128]{2,1,0:T(8,128)S(1)} %get-tuple-element.39.own_ref, f32[512,512]{1,0:T(8,128)S(1)} %get-tuple-element.40.after.refs_4_), custom_call_target="tpu_custom_call" | custom-call | flops 1 | bytes 1 | tf_op jit(solution)/shard_map/join/pallas_call | solution.py:337
  42.3 2.1 %collective-permute-start.4 = (f32[4,128,128]{2,1,0:T(8,128)S(1)}, f32[4,128,128]{2,1,0:T(8,128)S(1)}, u32[]{:S(2)}, u32[]{:S(2)}) collective-permute-start(f32[4,128,128]{2,1,0:T(8,128)S(1)} %join.7.refs_10_), channel_id=1, source_target_pairs={{0,4},{4,0},{8,12},{12,8},{1,5},{5,1},{9,13},{13,9},{2,6},{6,2},{1... | collective-permute-start | bytes 786440 | tf_op jit(solution)/shard_map/ppermute | solution.py:588
  44.4 2.4 %base_products.3 = (f32[512,512]{1,0:T(8,128)S(1)}, f32[512,512]{1,0:T(8,128)S(1)}, f32[512,512]{1,0:T(8,128)S(1)}, f32[512,512]{1,0:T(8,128)S(1)}) custom-call(s32[3,4]{1,0:T(4,128)S(1)} %copy-done.6, s32[1]{0:T(128)} %bitcast.place, bf16[512,1024]{1,0:T(8,128)(2,1)S(1)} %copy-done, bf16[512,1024]{1,0:T(8,128)(2,1)S(1)} %copy-done.1, ...), custom_call_target="tpu_custom_call" | custom-call | flops 1 | bytes 1 | tf_op jit(solution)/shard_map/base_products/pallas_call | solution.py:459
  46.8 0.0 collective-permute-done.5.refs_8_
  46.8 2.6 %final_products.2 = (bf16[512,1024]{1,0:T(8,128)(2,1)}, bf16[512,1024]{1,0:T(8,128)(2,1)}, bf16[512,1024]{1,0:T(8,128)(2,1)}, bf16[512,1024]{1,0:T(8,128)(2,1)}) custom-call(s32[3,4]{1,0:T(4,128)S(1)} %copy-done.6, s32[1]{0:T(128)} %bitcast.place, bf16[512,1024]{1,0:T(8,128)(2,1)S(1)} %copy-done, bf16[512,1024]{1,0:T(8,128)(2,1)S(1)} %copy-done.1, ...), custom_call_target="tpu_custom_call" | custom-call | flops 1 | bytes 1 | tf_op jit(solution)/shard_map/final_products/pallas_call | solution.py:531
  49.4 0.0 collective-permute-done.4.refs_8_
  49.4 2.5 %final_products.3 = (bf16[512,1024]{1,0:T(8,128)(2,1)}, bf16[512,1024]{1,0:T(8,128)(2,1)}, bf16[512,1024]{1,0:T(8,128)(2,1)}, bf16[512,1024]{1,0:T(8,128)(2,1)}) custom-call(s32[3,4]{1,0:T(4,128)S(1)} %copy-done.6, s32[1]{0:T(128)} %bitcast.place, ...), custom_call_target="tpu_custom_call", output_to_operand_aliasing={{0}: (11, {}), {1}: (12, {}), {2}: (13, {}), {3}: (14, {})} | custom-call | flops 1 | bytes 1 | tf_op jit(solution)/shard_map/final_products/pallas_call | solution.py:531
Async XLA Ops:
  0.6 6.3 %copy-start = (bf16[512,1024]{1,0:T(8,128)(2,1)S(1)}, bf16[512,1024]{1,0:T(8,128)(2,1)}, u32[]{:S(2)}) copy-start(bf16[512,1024]{1,0:T(8,128)(2,1)} %refs_0_.7) | copy-start | bytes 3145732
  0.6 6.3 %copy-start.1 = (bf16[512,1024]{1,0:T(8,128)(2,1)S(1)}, bf16[512,1024]{1,0:T(8,128)(2,1)}, u32[]{:S(2)}) copy-start(bf16[512,1024]{1,0:T(8,128)(2,1)} %refs_1_.7) | copy-start | bytes 3145732
  0.7 6.3 %copy-start.2 = (bf16[512,1024]{1,0:T(8,128)(2,1)S(1)}, bf16[512,1024]{1,0:T(8,128)(2,1)}, u32[]{:S(2)}) copy-start(bf16[512,1024]{1,0:T(8,128)(2,1)} %refs_2_.7) | copy-start | bytes 3145732
  0.7 6.3 %copy-start.6 = (s32[3,4]{1,0:T(4,128)S(1)}, s32[3,4]{1,0:T(4,128)}, u32[]{:S(2)}) copy-start(s32[3,4]{1,0:T(4,128)} %pack.27) | copy-start | bytes 148
  3.9 10.4 %collective-permute-start.1 = (f32[4,128,128]{2,1,0:T(8,128)}, f32[4,128,128]{2,1,0:T(8,128)S(1)}, u32[]{:S(2)}, u32[]{:S(2)}) collective-permute-start(f32[4,128,128]{2,1,0:T(8,128)} %local_sums.4.after), channel_id=1, source_target_pairs={{0,4},{4,0},{8,12},{12,8},{1,5},{5,1},{9,13},{13,9},{2,6},{6,2},{1... | collective-permute-start | bytes 786440 | tf_op jit(solution)/shard_map/ppermute | solution.py:565
  7.0 1.2 %copy-start.3 = (bf16[512,1024]{1,0:T(8,128)(2,1)S(1)}, bf16[512,1024]{1,0:T(8,128)(2,1)}, u32[]{:S(2)}) copy-start(bf16[512,1024]{1,0:T(8,128)(2,1)} %refs_3_.7) | copy-start | bytes 3145732
  8.2 0.9 %copy-start.5 = (f32[4,128,128]{2,1,0:T(8,128)S(1)}, f32[4,128,128]{2,1,0:T(8,128)}, u32[]{:S(2)}) copy-start(f32[4,128,128]{2,1,0:T(8,128)} %local_sums.4.after) | copy-start | bytes 786436
  10.4 13.1 %collective-permute-start = (f32[4,128,128]{2,1,0:T(8,128)S(1)}, f32[4,128,128]{2,1,0:T(8,128)S(1)}, u32[]{:S(2)}, u32[]{:S(2)}) collective-permute-start(f32[4,128,128]{2,1,0:T(8,128)S(1)} %local_sums.5.after), channel_id=1, source_target_pairs={{0,4},{4,0},{8,12},{12,8},{1,5},{5,1},{9,13},{13,9},{2,6},{6,2},{1... | collective-permute-start | bytes 786440 | tf_op jit(solution)/shard_map/ppermute | solution.py:565
  12.4 6.7 %copy-start.4 = (bf16[512,1024]{1,0:T(8,128)(2,1)S(1)}, bf16[512,1024]{1,0:T(8,128)(2,1)}, u32[]{:S(2)}) copy-start(bf16[512,1024]{1,0:T(8,128)(2,1)} %refs_3_.7) | copy-start | bytes 3145732
  14.9 23.4 %collective-permute-start.3 = (f32[4,128,128]{2,1,0:T(8,128)S(1)}, f32[4,128,128]{2,1,0:T(8,128)S(1)}, u32[]{:S(2)}, u32[]{:S(2)}) collective-permute-start(f32[4,128,128]{2,1,0:T(8,128)S(1)} %join.4.refs_0_), channel_id=1, source_target_pairs={{0,12},{4,8},{8,4},{12,0},{1,13},{5,9},{9,5},{13,1},{2,14},{6,10},... | collective-permute-start | bytes 786440 | tf_op jit(solution)/shard_map/ppermute | solution.py:585
  24.1 17.4 %collective-permute-start.2 = (f32[4,128,128]{2,1,0:T(8,128)S(1)}, f32[4,128,128]{2,1,0:T(8,128)S(1)}, u32[]{:S(2)}, u32[]{:S(2)}) collective-permute-start(f32[4,128,128]{2,1,0:T(8,128)S(1)} %join.5.after), channel_id=1, source_target_pairs={{0,12},{4,8},{8,4},{12,0},{1,13},{5,9},{9,5},{13,1},{2,14},{6,10},... | collective-permute-start | bytes 786440 | tf_op jit(solution)/shard_map/ppermute | solution.py:585
  39.0 7.8 %collective-permute-start.5 = (f32[4,128,128]{2,1,0:T(8,128)S(1)}, f32[4,128,128]{2,1,0:T(8,128)S(1)}, u32[]{:S(2)}, u32[]{:S(2)}) collective-permute-start(f32[4,128,128]{2,1,0:T(8,128)S(1)} %join.6.refs_10_), channel_id=1, source_target_pairs={{0,4},{4,0},{8,12},{12,8},{1,5},{5,1},{9,13},{13,9},{2,6},{6,2},{1... | collective-permute-start | bytes 786440 | tf_op jit(solution)/shard_map/ppermute | solution.py:588
  42.3 7.1 %collective-permute-start.4 = (f32[4,128,128]{2,1,0:T(8,128)S(1)}, f32[4,128,128]{2,1,0:T(8,128)S(1)}, u32[]{:S(2)}, u32[]{:S(2)}) collective-permute-start(f32[4,128,128]{2,1,0:T(8,128)S(1)} %join.7.refs_10_), channel_id=1, source_target_pairs={{0,4},{4,0},{8,12},{12,8},{1,5},{5,1},{9,13},{13,9},{2,6},{6,2},{1... | collective-permute-start | bytes 786440 | tf_op jit(solution)/shard_map/ppermute | solution.py:588
